TPU v7x, 256 devices: a whole 4x4x8 slice. The times are simulated.
256 devices in a mesh: row: 8 (over x_hi, y), col: 32 (over x_lo, z, core).
Axes of the slice: x: 4 (x_hi: 2, x_lo: 2; x = x_hi * 2 + x_lo), y: 4, z: 8, core: 2. Of those that a mesh axis runs over, the one named last changes fastest.
Arguments:
- pair: bfloat16 [768, 768, 128], P('row', 'col'), may hold values from -1.5 to 1.5
- norm_gain: float32 [2, 128], replicated, may hold values from 0.1 to 1.9
- w_proj: bfloat16 [2, 128, 512], replicated, may hold values from -5 to 5
- w_bias: bfloat16 [2, 128, 4], replicated, may hold values from -1 to 1
- gate_bias: float32 [2, 128], replicated, may hold values from -4 to 4
- w_out: bfloat16 [2, 128, 128], replicated, may hold values from -1 to 1
- out_bias: float32 [2, 128], replicated, may hold values from -3 to 3
Outputs:
- updated_pair: bfloat16 [768, 768, 128], P('row', 'col')
All inputs are finite; a program needn't handle non-finite values.
Results may differ from a plain program's by a relative error of at most 0.03.
Values may be sent and summed in bfloat16 or wider, within the bound.
No kernel may reach another device: no remote copies, remote signals or barrier semaphores. Data moves between devices by JAX's collectives and lax.ppermute only.
A program may use at most 64 MiB of HBM per device.

v0:
```python
import jax
import jax.numpy as jnp
from jax import lax
from jax.sharding import PartitionSpec as P

HEAD_COUNT = 4
HEAD_WIDTH = 32


def normalize(pair_map, gain):
    values = pair_map.astype(jnp.float32)
    center = jnp.mean(values, axis=-1, keepdims=True)
    spread = jnp.mean((values - center) ** 2, axis=-1, keepdims=True)
    return ((values - center) * lax.rsqrt(spread + 1e-05) * gain).astype(jnp.bfloat16)


def attend(row_block, pair_bias, proj_weight, gate_shift):
    inner = HEAD_COUNT * HEAD_WIDTH
    length = row_block.shape[1]
    scale = HEAD_WIDTH ** (-0.5)

    def one_row(row_entries):
        projected = jnp.dot(row_entries, proj_weight, preferred_element_type=jnp.float32)
        queries = projected[:, :inner].astype(jnp.bfloat16).reshape(length, HEAD_COUNT, HEAD_WIDTH)
        key_rows = (
            projected[:, inner : 2 * inner]
            .astype(jnp.bfloat16)
            .reshape(length, HEAD_COUNT, HEAD_WIDTH)
        )
        value_rows = (
            projected[:, 2 * inner : 3 * inner]
            .astype(jnp.bfloat16)
            .reshape(length, HEAD_COUNT, HEAD_WIDTH)
        )
        scores = (
            jnp.einsum("jhd,khd->hjk", queries, key_rows, preferred_element_type=jnp.float32)
            * scale
            + pair_bias
        )
        weights = jax.nn.softmax(scores, axis=-1).astype(jnp.bfloat16)
        mixed = jnp.einsum(
            "hjk,khd->jhd", weights, value_rows, preferred_element_type=jnp.float32
        ).reshape(length, inner)
        return (mixed * jax.nn.sigmoid(projected[:, 3 * inner :] + gate_shift)).astype(jnp.bfloat16)

    return lax.map(one_row, row_block)


def project_out(gated, out_weight, out_shift):
    return jnp.dot(gated, out_weight, preferred_element_type=jnp.float32) + out_shift


def per_device(pair, norm_gain, w_proj, w_bias, gate_bias, w_out, out_bias):
    normed = normalize(pair, norm_gain[0])
    local_bias = jnp.einsum(
        "rcd,dh->hrc", normed, w_bias[0], preferred_element_type=jnp.float32
    ).astype(jnp.bfloat16)
    partial_bias = lax.all_gather(local_bias, "row", axis=1, tiled=True)
    start_bias = lax.all_gather(partial_bias, "col", axis=2, tiled=True)
    full_rows = lax.all_to_all(normed, "col", split_axis=0, concat_axis=1, tiled=True)
    gated = attend(full_rows, start_bias, w_proj[0], gate_bias[0])
    row_delta = project_out(gated, w_out[0], out_bias[0])
    start_delta = lax.all_to_all(row_delta, "col", split_axis=1, concat_axis=0, tiled=True)
    first = (pair.astype(jnp.float32) + start_delta).astype(jnp.bfloat16)
    normed_home = normalize(first, norm_gain[1])
    normed_cols = lax.all_to_all(normed_home, "row", split_axis=1, concat_axis=0, tiled=True)
    end_local = jnp.einsum(
        "rcd,dh->hcr", normed_cols, w_bias[1], preferred_element_type=jnp.float32
    ).astype(jnp.bfloat16)
    end_partial = lax.all_gather(end_local, "row", axis=1, tiled=True)
    end_bias = lax.all_gather(end_partial, "col", axis=1, tiled=True)
    column_block = jnp.swapaxes(normed_cols, 0, 1)
    end_gated = attend(column_block, end_bias, w_proj[1], gate_bias[1])
    column_delta = jnp.swapaxes(project_out(end_gated, w_out[1], out_bias[1]), 0, 1)
    end_delta = lax.all_to_all(column_delta, "row", split_axis=0, concat_axis=1, tiled=True)
    return (first.astype(jnp.float32) + end_delta).astype(jnp.bfloat16)


def solution(mesh):
    return jax.shard_map(
        per_device,
        mesh=mesh,
        in_specs=(P("row", "col", None), P(), P(), P(), P(), P(), P()),
        out_specs=P("row", "col", None),
        check_vma=False,
    )
```

profile of v0, /device:TPU:1, one launch (start us, length us, event | category | flops | bytes accessed | tf_op | source)
XLA Modules:
  0.0 429.0 jit_solution(953989093200435543)
XLA Ops:
  15.2 31.8 %all_gather.12 = bf16[4,768,24]{2,0,1:T(4,128)(2,1)S(1)} all-gather(bf16[4,96,24]{2,0,1:T(4,128)(2,1)S(1)} %fusion.51), channel_id=1, replica_groups=mesh['row'=8,'col'=32] {'row'}, dimensions={1}, use_global_device_ids=true | all-gather | bytes 165888 | tf_op jit(solution)/shard_map/all_gather | solution.py:58
  48.1 15.0 %all-to-all-start = ((bf16[96,24,128]{2,1,0:T(8,128)(2,1)}), bf16[96,24,128]{2,1,0:T(8,128)(2,1)S(1)}, u32[]{:S(2)}, u32[]{:S(2)}) async-start(bf16[96,24,128]{2,1,0:T(8,128)(2,1)} %fusion.48), calls=%async_computation | async-start | bytes 1179648 | tf_op jit(solution)/shard_map/all_to_all | solution.py:60
  64.5 20.4 %all-to-all-done = bf16[96,24,128]{2,1,0:T(8,128)(2,1)S(1)} async-done(((bf16[96,24,128]{2,1,0:T(8,128)(2,1)}), bf16[96,24,128]{2,1,0:T(8,128)(2,1)S(1)}, u32[]{:S(2)}, u32[]{:S(2)}) %all-to-all-start) | async-done | bytes 589856 | tf_op jit(solution)/shard_map/all_to_all | solution.py:60
  84.9 43.0 %all-gather.3.cloned.1.call-done = bf16[4,768,768]{1,0,2:T(4,128)(2,1)} async-done(((bf16[4,768,24]{1,0,2:T(4,128)(2,1)}), bf16[4,768,768]{1,0,2:T(4,128)(2,1)}) %all-gather.3.cloned.1.call-update) | async-done | bytes 4718608 | tf_op jit(solution)/shard_map/all_gather | solution.py:59
  127.9 5.1 %copy.66 = bf16[4,768,768]{1,2,0:T(8,128)(2,1)} copy(bf16[4,768,768]{1,0,2:T(4,128)(2,1)} %all-gather.3.cloned.1.call-done) | data formatting | bytes 9437184 | tf_op jit(solution)/shard_map/while | solution.py:46
  133.8 37.1 %while.20 = (s32[]{:T(128)}, bf16[3,768,128]{1,2,0:T(8,128)(2,1)}, bf16[3,768,128]{2,1,0:T(8,128)(2,1)S(1)}, bf16[128,512]{1,0:T(8,128)(2,1)S(1)}, bf16[4,768,76...) while((s32[]{:T(128)}, bf16[3,768,128]{1,2,0:T(8,128)(2,1)}, bf16[3,768,128]{2,1,0:T(8,128)(2,1)S(1)}, ...), condition=%wide.region_5.6_spmd, body=%wide.region_2.5_spmd.sunk | while | flops 580588032 | bytes 15688785 | solution.py:46
  134.3 4.9 %fusion.113 = f32[4,768]{1,0:T(4,128)S(1)} fusion(bf16[4,768,768]{1,2,0:T(8,128)(2,1)} %get-tuple-element.275, bf16[768,4,32]{0,2,1:T(8,128)(2,1)S(1)} %bitcast.154, bf16[768,4,32]{0,2,1:T(8,128)(2,1)S(1)} %bitcast.152), kind=kOutput, calls=%fused_computation.89.clone.1 | convolution fusion | flops 162792192 | bytes 5124096 | tf_op jit(solution)/shard_map/while/body/eval_jaxpr/sub | solution.py:40
  139.2 6.2 %fusion.114 = f32[4,32,768]{2,1,0:T(8,128)S(1)} fusion(bf16[768,4,32]{0,2,1:T(8,128)(2,1)S(1)} %bitcast.156, f32[4,768]{1,0:T(4,128)S(1)} %fusion.113, bf16[4,768,768]{1,2,0:T(8,128)(2,1)} %get-tuple-element.275, bf16[768,4,32]{0,2,1:T(8,128)(2,1)S(1)} %bitcast.155, bf16[768,4,32]{0,2,1:T(8,128)(2,1)S(1)} %bitcast.153), kind=kOutput, calls=%fused_computation.4.clone.1 | convolution fusion | flops 316149504 | bytes 5713920 | tf_op jit(solution)/shard_map/while/body/eval_jaxpr/hjk,khd->jhd/dot_general | solution.py:41
  151.5 6.2 %fusion.114 = f32[4,32,768]{2,1,0:T(8,128)S(1)} fusion(bf16[768,4,32]{0,2,1:T(8,128)(2,1)S(1)} %bitcast.156, f32[4,768]{1,0:T(4,128)S(1)} %fusion.113, bf16[4,768,768]{1,2,0:T(8,128)(2,1)} %get-tuple-element.275, bf16[768,4,32]{0,2,1:T(8,128)(2,1)S(1)} %bitcast.155, bf16[768,4,32]{0,2,1:T(8,128)(2,1)S(1)} %bitcast.153), kind=kOutput, calls=%fused_computation.4.clone.1 | convolution fusion | flops 316149504 | bytes 5713920 | tf_op jit(solution)/shard_map/while/body/eval_jaxpr/hjk,khd->jhd/dot_general | solution.py:41
  159.0 4.9 %fusion.113 = f32[4,768]{1,0:T(4,128)S(1)} fusion(bf16[4,768,768]{1,2,0:T(8,128)(2,1)} %get-tuple-element.275, bf16[768,4,32]{0,2,1:T(8,128)(2,1)S(1)} %bitcast.154, bf16[768,4,32]{0,2,1:T(8,128)(2,1)S(1)} %bitcast.152), kind=kOutput, calls=%fused_computation.89.clone.1 | convolution fusion | flops 162792192 | bytes 5124096 | tf_op jit(solution)/shard_map/while/body/eval_jaxpr/sub | solution.py:40
  163.9 6.2 %fusion.114 = f32[4,32,768]{2,1,0:T(8,128)S(1)} fusion(bf16[768,4,32]{0,2,1:T(8,128)(2,1)S(1)} %bitcast.156, f32[4,768]{1,0:T(4,128)S(1)} %fusion.113, bf16[4,768,768]{1,2,0:T(8,128)(2,1)} %get-tuple-element.275, bf16[768,4,32]{0,2,1:T(8,128)(2,1)S(1)} %bitcast.155, bf16[768,4,32]{0,2,1:T(8,128)(2,1)S(1)} %bitcast.153), kind=kOutput, calls=%fused_computation.4.clone.1 | convolution fusion | flops 316149504 | bytes 5713920 | tf_op jit(solution)/shard_map/while/body/eval_jaxpr/hjk,khd->jhd/dot_general | solution.py:41
  173.1 45.4 %all_to_all.72 = f32[3,768,128]{2,0,1:T(4,128)S(1)} all-to-all(f32[3,768,128]{2,0,1:T(4,128)S(1)} %copy.68), channel_id=1, replica_groups=mesh['row'=8,'col'=32] {'col'}, dimensions={1} | all-to-all | bytes 2359296 | tf_op jit(solution)/shard_map/all_to_all | solution.py:63
  220.8 14.9 %all_to_all.73 = bf16[96,24,128]{2,0,1:T(8,128)(2,1)S(1)} all-to-all(bf16[96,24,128]{2,0,1:T(8,128)(2,1)S(1)} %copy.71), channel_id=1, replica_groups=mesh['row'=8,'col'=32] {'row'}, dimensions={1} | all-to-all | bytes 1179648 | tf_op jit(solution)/shard_map/all_to_all | solution.py:66
  236.0 30.3 %all_gather.14 = bf16[4,24,768]{2,0,1:T(4,128)(2,1)} all-gather(bf16[4,3,768]{2,0,1:T(4,128)(2,1)S(1)} %fusion.52), channel_id=1, replica_groups=mesh['row'=8,'col'=32] {'row'}, dimensions={1}, use_global_device_ids=true | all-gather | bytes 165888 | tf_op jit(solution)/shard_map/all_gather | solution.py:70
  266.3 71.3 %all-gather.5.cloned.1.call-done = bf16[4,768,768]{2,0,1:T(4,128)(2,1)} async-done(((bf16[4,24,768]{2,0,1:T(4,128)(2,1)}), bf16[4,768,768]{2,0,1:T(4,128)(2,1)}) %all-gather.5.cloned.1.call-update) | async-done | bytes 4718608 | tf_op jit(solution)/shard_map/all_gather | solution.py:71
  337.6 8.4 %copy.73 = bf16[4,768,768]{1,2,0:T(8,128)(2,1)} copy(bf16[4,768,768]{2,0,1:T(4,128)(2,1)} %all-gather.5.cloned.1.call-done) | data formatting | bytes 9437184 | tf_op jit(solution)/shard_map/while | solution.py:46
  346.9 43.6 %while.21 = (s32[]{:T(128)}, bf16[3,768,128]{1,2,0:T(8,128)(2,1)}, bf16[3,768,128]{2,1,0:T(8,128)(2,1)S(1)}, bf16[128,512]{1,0:T(8,128)(2,1)}, bf16[4,768,768]{1...) while((s32[]{:T(128)}, bf16[3,768,128]{1,2,0:T(8,128)(2,1)}, bf16[3,768,128]{2,1,0:T(8,128)(2,1)S(1)}, ...), condition=%wide.region_11.12_spmd, body=%wide.region_8.11_spmd.sunk | while | flops 580588032 | bytes 15688785 | solution.py:46
  348.9 5.5 %fusion.123 = f32[4,768]{1,0:T(4,128)} fusion(bf16[4,768,768]{1,2,0:T(8,128)(2,1)} %get-tuple-element.296, bf16[768,4,32]{0,2,1:T(8,128)(2,1)S(1)} %bitcast.159, bf16[768,4,32]{0,2,1:T(8,128)(2,1)S(1)} %bitcast.157), kind=kOutput, calls=%fused_computation.92.clone.1 | convolution fusion | flops 162792192 | bytes 5124096 | tf_op jit(solution)/shard_map/while/body/eval_jaxpr/sub | solution.py:40
  354.4 6.2 %fusion.124 = f32[4,32,768]{2,1,0:T(8,128)S(1)} fusion(bf16[768,4,32]{0,2,1:T(8,128)(2,1)} %bitcast.161, f32[4,768]{1,0:T(4,128)} %fusion.123, bf16[4,768,768]{1,2,0:T(8,128)(2,1)} %get-tuple-element.296, bf16[768,4,32]{0,2,1:T(8,128)(2,1)S(1)} %bitcast.160, bf16[768,4,32]{0,2,1:T(8,128)(2,1)S(1)} %bitcast.158), kind=kOutput, calls=%fused_computation.26.clone.1 | convolution fusion | flops 316149504 | bytes 5713920 | tf_op jit(solution)/shard_map/while/body/eval_jaxpr/hjk,khd->jhd/dot_general | solution.py:41
  363.4 5.5 %fusion.123 = f32[4,768]{1,0:T(4,128)} fusion(bf16[4,768,768]{1,2,0:T(8,128)(2,1)} %get-tuple-element.296, bf16[768,4,32]{0,2,1:T(8,128)(2,1)S(1)} %bitcast.159, bf16[768,4,32]{0,2,1:T(8,128)(2,1)S(1)} %bitcast.157), kind=kOutput, calls=%fused_computation.92.clone.1 | convolution fusion | flops 162792192 | bytes 5124096 | tf_op jit(solution)/shard_map/while/body/eval_jaxpr/sub | solution.py:40
  368.9 6.2 %fusion.124 = f32[4,32,768]{2,1,0:T(8,128)S(1)} fusion(bf16[768,4,32]{0,2,1:T(8,128)(2,1)} %bitcast.161, f32[4,768]{1,0:T(4,128)} %fusion.123, bf16[4,768,768]{1,2,0:T(8,128)(2,1)} %get-tuple-element.296, bf16[768,4,32]{0,2,1:T(8,128)(2,1)S(1)} %bitcast.160, bf16[768,4,32]{0,2,1:T(8,128)(2,1)S(1)} %bitcast.158), kind=kOutput, calls=%fused_computation.26.clone.1 | convolution fusion | flops 316149504 | bytes 5713920 | tf_op jit(solution)/shard_map/while/body/eval_jaxpr/hjk,khd->jhd/dot_general | solution.py:41
  378.0 5.5 %fusion.123 = f32[4,768]{1,0:T(4,128)} fusion(bf16[4,768,768]{1,2,0:T(8,128)(2,1)} %get-tuple-element.296, bf16[768,4,32]{0,2,1:T(8,128)(2,1)S(1)} %bitcast.159, bf16[768,4,32]{0,2,1:T(8,128)(2,1)S(1)} %bitcast.157), kind=kOutput, calls=%fused_computation.92.clone.1 | convolution fusion | flops 162792192 | bytes 5124096 | tf_op jit(solution)/shard_map/while/body/eval_jaxpr/sub | solution.py:40
  383.4 6.2 %fusion.124 = f32[4,32,768]{2,1,0:T(8,128)S(1)} fusion(bf16[768,4,32]{0,2,1:T(8,128)(2,1)} %bitcast.161, f32[4,768]{1,0:T(4,128)} %fusion.123, bf16[4,768,768]{1,2,0:T(8,128)(2,1)} %get-tuple-element.296, bf16[768,4,32]{0,2,1:T(8,128)(2,1)S(1)} %bitcast.160, bf16[768,4,32]{0,2,1:T(8,128)(2,1)S(1)} %bitcast.158), kind=kOutput, calls=%fused_computation.26.clone.1 | convolution fusion | flops 316149504 | bytes 5713920 | tf_op jit(solution)/shard_map/while/body/eval_jaxpr/hjk,khd->jhd/dot_general | solution.py:41
  392.7 27.7 %all_to_all.74 = f32[768,3,128]{2,1,0:T(4,128)S(1)} all-to-all(f32[768,3,128]{2,1,0:T(4,128)S(1)} %copy.75), channel_id=1, replica_groups=mesh['row'=8,'col'=32] {'row'}, dimensions={0} | all-to-all | bytes 2359296 | tf_op jit(solution)/shard_map/all_to_all | solution.py:75
  (68 shorter events, 38.9 us)
Async XLA Ops:
  6.5 56.6 %copy-start.5 = (f32[2,128]{1,0:T(2,128)S(1)}, f32[2,128]{1,0:T(2,128)}, u32[]{:S(2)}) copy-start(f32[2,128]{1,0:T(2,128)} %param.15) | copy-start | bytes 3076
  6.5 56.7 %copy-start.6 = (f32[2,128]{1,0:T(2,128)S(1)}, f32[2,128]{1,0:T(2,128)}, u32[]{:S(2)}) copy-start(f32[2,128]{1,0:T(2,128)} %param.17) | copy-start | bytes 3076
  6.5 57.3 %copy-start.1 = (bf16[2,128,512]{2,1,0:T(8,128)(2,1)S(1)}, bf16[2,128,512]{2,1,0:T(8,128)(2,1)}, u32[]{:S(2)}) copy-start(bf16[2,128,512]{2,1,0:T(8,128)(2,1)} %param.13) | copy-start | bytes 786436
  6.5 121.3 %all-gather.3.cloned.1.call-start = ((), (), s32[]{:S(2)}) async-start(), calls=%async_computation.4 | async-start | bytes 4866048 | tf_op jit(solution)/shard_map/all_gather | solution.py:59
  48.1 36.7 %all-to-all-start = ((bf16[96,24,128]{2,1,0:T(8,128)(2,1)}), bf16[96,24,128]{2,1,0:T(8,128)(2,1)S(1)}, u32[]{:S(2)}, u32[]{:S(2)}) async-start(bf16[96,24,128]{2,1,0:T(8,128)(2,1)} %fusion.48), calls=%async_computation | async-start | bytes 1179648 | tf_op jit(solution)/shard_map/all_to_all | solution.py:60
  63.1 274.5 %all-gather.5.cloned.1.call-start = ((), (), s32[]{:S(2)}) async-start(), calls=%async_computation.5 | async-start | bytes 4866048 | tf_op jit(solution)/shard_map/all_gather | solution.py:71
  133.8 37.1 %copy-start.2 = (bf16[2,128,128]{2,1,0:T(8,128)(2,1)S(1)}, bf16[2,128,128]{2,1,0:T(8,128)(2,1)}, u32[]{:S(2)}) copy-start(bf16[2,128,128]{2,1,0:T(8,128)(2,1)} %param.16) | copy-start | bytes 196612
  173.1 45.6 %copy-start = (bf16[96,24,128]{2,1,0:T(8,128)(2,1)S(1)}, bf16[96,24,128]{2,1,0:T(8,128)(2,1)}, u32[]{:S(2)}) copy-start(bf16[96,24,128]{2,1,0:T(8,128)(2,1)} %param.11) | copy-start | bytes 1769476
  218.6 17.1 %copy-start.3 = (bf16[2,128,4]{1,2,0:T(4,128)(2,1)S(1)}, bf16[2,128,4]{1,2,0:T(4,128)(2,1)}, u32[]{:S(2)}) copy-start(bf16[2,128,4]{1,2,0:T(4,128)(2,1)} %param.14) | copy-start | bytes 6148
  346.9 43.6 %copy-start.4 = (f32[128]{0:T(128)S(1)}, f32[128]{0:T(128)}, u32[]{:S(2)}) copy-start(f32[128]{0:T(128)} %get-tuple-element.157) | copy-start | bytes 1540
Sparse Core Ops, SparseCore 0:
  48.2 79.6 all-gather.2
  266.4 71.1 all-gather.4
where the time goes:
time: 430 us; the launch traced here: 429 us
  blocking collectives  150 us (35%)
  waiting for transfers between devices  135 us (31%)
  matrix products  78.4 us (18%)
  local copies, waits for them, and re-layouts  22.7 us (5%)
  starting transfers between devices  15 us (3%)
  other arithmetic  14.3 us (3%)
  between operations  13.6 us (3%)
    all_gather x1, waiting for transfers between devices, per_device(): end_bias = lax.all_gather(end_partial, 'col', axis=1, tiled=True)  71.3 us
    all_to_all x1, blocking collectives, per_device(): lax.all_to_all(row_delta, 'col', split_axis=1, concat_axis=0, tiled=True)  45.4 us
    all_gather x1, waiting for transfers between devices, per_device(): start_bias = lax.all_gather(partial_bias, 'col', axis=2, tiled=True)  43 us
    dot_general x6, matrix products, one_row(): jnp.einsum('hjk,khd->jhd', weights, value_rows, preferred_element_type=jn...  36.9 us
    all_gather x1, blocking collectives, per_device(): partial_bias = lax.all_gather(local_bias, 'row', axis=1, tiled=True)  31.8 us
    sub x6, matrix products, one_row(): weights = jax.nn.softmax(scores, axis=-1).astype(jnp.bfloat16)  31.1 us
    all_gather x1, blocking collectives, per_device(): end_partial = lax.all_gather(end_local, 'row', axis=1, tiled=True)  30.3 us
    all_to_all x1, blocking collectives, per_device(): lax.all_to_all(column_delta, 'row', split_axis=0, concat_axis=1, tiled=True)  27.7 us
  transfers between devices with their start and end apart: 3, of which 3 were waited for; matrix products, arithmetic and copies ran while one was open for 0% of the time, Pallas kernels for 0%

commit v1 on v0

v1 whole, which is shorter than its diff:
```python
import functools

import jax
import jax.numpy as jnp
from jax import lax
from jax.experimental import pallas as pl
from jax.experimental.pallas import tpu as pltpu
from jax.sharding import PartitionSpec as P

HEADS = 4
WIDTH = 32
CH = 128
LOG2E = 1.4426950408889634
NT = (((1,), (1,)), ((), ()))


def normalize(values, gain):
    values = values.astype(jnp.float32)
    center = jnp.mean(values, axis=-1, keepdims=True)
    spread = jnp.mean((values - center) ** 2, axis=-1, keepdims=True)
    return ((values - center) * lax.rsqrt(spread + 1e-05) * gain).astype(jnp.bfloat16)


def attention_kernel(
    nblk, blk_ref, x_ref, xq_ref, *refs
):
    bias_refs = refs[:nblk]
    gain_ref, wp_ref, gb_ref, wo_ref, ob_ref, out_ref, biasf = refs[nblk:]
    keys = x_ref.shape[1]
    half = bias_refs[0].shape[0]
    rows = bias_refs[0].shape[1] // 2
    block = rows // HEADS

    @pl.when(pl.program_id(0) == 0)
    def _():
        at = lax.broadcasted_iota(jnp.int32, (rows, 2 * rows), 0)
        to = lax.broadcasted_iota(jnp.int32, (rows, 2 * rows), 1)
        for s in range(2):
            pick = (to == at + s * rows).astype(jnp.bfloat16)
            for b in range(nblk):
                biasf[b, :, s * half : (s + 1) * half] = (
                    lax.dot_general(pick, bias_refs[b][...], NT, preferred_element_type=jnp.float32)
                    * LOG2E
                )

    gain = gain_ref[...]
    xn = normalize(x_ref[0], gain)
    kv = jnp.dot(xn, wp_ref[:, CH : 3 * CH], preferred_element_type=jnp.float32).astype(jnp.bfloat16)
    k2 = jnp.concatenate([kv[:, :CH], kv[:, :CH]], axis=1)
    v1 = jnp.concatenate([kv[:, CH:], jnp.ones((keys, CH), jnp.bfloat16)], axis=1)
    head_of = lax.broadcasted_iota(jnp.int32, (block, CH), 1) // WIDTH

    for b in range(nblk):
        q0 = pl.multiple_of(blk_ref[b] * block, 16)
        xq = xq_ref[0, pl.ds(q0, block), :]
        xqn = normalize(xq, gain)
        q = jnp.dot(xqn, wp_ref[:, :CH], preferred_element_type=jnp.float32)
        gate = jnp.dot(xqn, wp_ref[:, 3 * CH :], preferred_element_type=jnp.float32)
        qs = q.astype(jnp.bfloat16).astype(jnp.float32) * (WIDTH**-0.5 * LOG2E)
        qh = qs.astype(jnp.bfloat16).astype(jnp.float32)
        ql = qs - qh
        qm = jnp.concatenate(
            [
                jnp.concatenate([jnp.where(head_of == h, t, 0.0) for t in (qh, ql)], axis=1)
                for h in range(HEADS)
            ],
            axis=0,
        ).astype(jnp.bfloat16)
        s = lax.dot_general(qm, k2, NT, preferred_element_type=jnp.float32) + biasf[b]
        top = jnp.max(s, axis=-1, keepdims=True)
        p = jnp.exp2(s - top).astype(jnp.bfloat16)
        o = jnp.dot(p, v1, preferred_element_type=jnp.float32)
        o = o[:, :CH] / o[:, CH:]
        mixed = jnp.zeros((block, CH), jnp.float32)
        for h in range(HEADS):
            mixed = jnp.where(head_of == h, o[h * block : (h + 1) * block], mixed)
        gated = (mixed * jax.nn.sigmoid(gate + gb_ref[...])).astype(jnp.bfloat16)
        y = jnp.dot(gated, wo_ref[...], preferred_element_type=jnp.float32) + ob_ref[...]
        out_ref[0, pl.ds(q0, block), :] = (xq.astype(jnp.float32) + y).astype(jnp.bfloat16)


def attention(blocks, x, xq, biases, gain, wp, gb, wo, ob):
    nrow, keys, _ = x.shape
    nq = xq.shape[1]
    nblk = len(biases)
    rows = biases[0].shape[1] // 2
    whole = lambda a: pl.BlockSpec(a.shape, lambda i, *_: (0,) * a.ndim)
    small = [gain[None], wp, gb[None], wo, ob[None]]
    flops = 2 * nrow * HEADS * nq * keys * 512
    return pl.pallas_call(
        functools.partial(attention_kernel, nblk),
        grid_spec=pltpu.PrefetchScalarGridSpec(
            num_scalar_prefetch=1,
            grid=(nrow,),
            in_specs=[
                pl.BlockSpec((1, keys, CH), lambda i, *_: (i, 0, 0)),
                pl.BlockSpec((1, nq, CH), lambda i, *_: (i, 0, 0)),
            ]
            + [whole(a) for a in list(biases) + small],
            out_specs=pl.BlockSpec((1, nq, CH), lambda i, *_: (i, 0, 0)),
            scratch_shapes=[pltpu.VMEM((nblk, rows, keys), jnp.float32)],
        ),
        out_shape=jax.ShapeDtypeStruct((nrow, nq, CH), jnp.bfloat16),
        compiler_params=pltpu.CompilerParams(vmem_limit_bytes=40 << 20),
        cost_estimate=pl.CostEstimate(
            flops=flops, bytes_accessed=6 << 20, transcendentals=nrow * HEADS * nq * keys
        ),
    )(blocks, x, xq, *biases, *small)


def solution(mesh):
    nr, nc = mesh.shape["row"], mesh.shape["col"]
    ng = nc // 2
    same_core_col = [[2 * g + c for g in range(ng)] for c in range(2)]
    same_core_all = [[r * nc + 2 * g + c for r in range(nr) for g in range(ng)] for c in range(2)]
    swap_core = [(i, i ^ 1) for i in range(nc)]
    turns = ((0, 1), (0, 3), (1, 0), (0, 2), (1, 1), (1, 3), (1, 2))

    def turned(i, dx, dy):
        return ((i // 4) ^ dx) * 4 + (i % 4 + dy) % 4

    def spread(bias):
        me = lax.axis_index("row")
        got, ids = [bias], [me]
        for dx, dy in turns:
            got.append(lax.ppermute(bias, "row", [(i, turned(i, dx, dy)) for i in range(nr)]))
            ids.append(((me // 4) ^ dx) * 4 + (me % 4 - dy + 4) % 4)
        return got, jnp.stack(ids).astype(jnp.int32)

    def per_device(pair, norm_gain, w_proj, w_bias, gate_bias, w_out, out_bias):
        core = lax.axis_index("col") % 2
        nrow = pair.shape[0] // ng
        ncol = pair.shape[1]
        keys = nc * ncol
        half = keys // 2
        normed = normalize(pair, norm_gain[0])
        local = jnp.einsum("qmc,ch->mhq", normed, w_bias[0], preferred_element_type=jnp.float32)
        local = local.astype(jnp.bfloat16).reshape(ncol, HEADS, 2, 2, ncol).transpose(0, 3, 1, 2, 4)
        local = jnp.where(core == 0, local, local[:, ::-1]).reshape(-1, CH)
        brow = local.shape[0]
        message = jnp.concatenate(
            [
                pair.reshape(ng, nrow * ncol, CH),
                jnp.broadcast_to(local[None], (ng, brow, CH)),
                jnp.zeros((ng, -brow % 16, CH), jnp.bfloat16),
            ],
            axis=1,
        )
        got = lax.all_to_all(message, "col", 0, 0, tiled=True, axis_index_groups=same_core_col)
        x_own = got[:, : nrow * ncol]
        x_other = lax.ppermute(x_own, "col", swap_core)
        bias = got[:, nrow * ncol : nrow * ncol + brow].reshape(half, 2, half // 2)
        bias_other = lax.ppermute(bias[:, 1], "col", swap_core)
        bias = jnp.concatenate([bias[:, 0], bias_other], axis=1)
        biases, ids = spread(bias)
        x = jnp.stack([x_own, x_other]).reshape(2, ng, nrow, ncol, CH)
        x = x.transpose(2, 0, 1, 3, 4).reshape(nrow, keys, CH)
        first = attention(
            ids, x, x[:, :half], biases, norm_gain[0], w_proj[0], gate_bias[0], w_out[0], out_bias[0]
        )

        part = ncol // nr
        moved = first.reshape(nrow, ng, nr, part, CH).transpose(2, 1, 0, 3, 4)
        moved = moved.reshape(nr, ng, nrow * part, CH)
        normed = normalize(first, norm_gain[1])
        local = jnp.einsum("mqc,ch->mhq", normed, w_bias[1], preferred_element_type=jnp.float32)
        local = local.astype(jnp.bfloat16).reshape(nrow, HEADS, nr, half // nr).transpose(2, 0, 1, 3)
        local = local.reshape(nr, 1, -1, CH)
        brow = local.shape[2]
        message = jnp.concatenate(
            [
                moved,
                jnp.broadcast_to(local, (nr, ng, brow, CH)),
                jnp.zeros((nr, ng, -(brow + nrow * part) % 16, CH), jnp.bfloat16),
            ],
            axis=2,
        ).reshape(nr * ng, -1, CH)
        got = lax.all_to_all(
            message, ("row", "col"), 0, 0, tiled=True, axis_index_groups=same_core_all
        )
        x_own = got[:, : nrow * part].reshape(keys, part, CH).transpose(1, 0, 2)
        x_other = lax.ppermute(x_own, "col", swap_core)
        bias = got[:, nrow * part : nrow * part + brow].reshape(2, half, half // 2)
        bias = jnp.concatenate([bias[0], bias[1]], axis=1)
        biases, ids = spread(bias)
        x = jnp.concatenate([x_own, x_other])
        xq = x.reshape(2 * part, ng, 2, ncol, CH)
        xq = jnp.where(core == 0, xq[:, :, 0], xq[:, :, 1]).reshape(2 * part, half, CH)
        last = attention(
            ids, x, xq, biases, norm_gain[1], w_proj[1], gate_bias[1], w_out[1], out_bias[1]
        )

        own = last[:part]
        other = lax.ppermute(last[part:], "col", swap_core)
        both = jnp.stack([jnp.where(core == 0, own, other), jnp.where(core == 0, other, own)])
        both = both.reshape(2, part, nr, half // nr, CH).transpose(2, 0, 1, 3, 4)
        got = lax.all_to_all(both.reshape(nr, -1, CH), "row", 0, 0, tiled=True)
        got = got.reshape(nr, 2, part, 2, ncol, CH)
        return got.transpose(3, 1, 4, 0, 2, 5).reshape(pair.shape)

    return jax.shard_map(
        per_device,
        mesh=mesh,
        in_specs=(P("row", "col", None), P(), P(), P(), P(), P(), P()),
        out_specs=P("row", "col", None),
        check_vma=False,
    )
```

time: 430 us -> 265 us (0.62)
  waiting for transfers between devices: 135 us -> 46.2 us
  Pallas kernels: 0 us -> 78.8 us
  matrix products: 78.4 us -> 2.43 us
  blocking collectives: 150 us -> 93.1 us
  starting transfers between devices: 15 us -> 31.8 us
  local copies, waits for them, and re-layouts: 22.7 us -> 6.62 us
  between operations: 13.6 us -> 0.5 us
  other arithmetic: 14.3 us -> 5.33 us
    all_gather x2 -> x0, waiting for transfers between devices: 114 us -> none  [the longest x1 71.3 us: per_device(): end_bias = lax.all_gather(end_partial, 'col', axis=1, tiled=True)]
    pallas_call x0 -> x2, Pallas kernels: none -> 78.8 us  [attention(): pl.pallas_call(functools.partial(attention_kernel, nblk), grid_spec=pltpu...]
    all_gather x2 -> x0, blocking collectives: 62 us -> none  [the longest x1 31.8 us: per_device(): partial_bias = lax.all_gather(local_bias, 'row', axis=1, tiled=True)]
    ppermute x0 -> x18, waiting for transfers between devices: none -> 46.2 us  [the longest x14 44.1 us: spread(): lax.ppermute(bias, 'row', [(i, turned(i, dx, dy)) for i in range(nr)])]
    dot_general x16 -> x2, matrix products: 47.3 us -> 2.43 us  [the longest x1 1.43 us: per_device(): jnp.einsum('qmc,ch->mhq', normed, w_bias[0], preferred_element_type=jnp.f...]
    ppermute x0 -> x18, starting transfers between devices: none -> 31.8 us  [the longest x14 22.9 us: spread(): lax.ppermute(bias, 'row', [(i, turned(i, dx, dy)) for i in range(nr)])]
    sub x6 -> x0, matrix products: 31.1 us -> none  [one_row(): weights = jax.nn.softmax(scores, axis=-1).astype(jnp.bfloat16)]
    all_to_all x1 -> x0, waiting for transfers between devices: 20.4 us -> none  [per_device(): lax.all_to_all(normed, 'col', split_axis=0, concat_axis=1, tiled=True)]
  transfers between devices with their start and end apart: 3 -> 18, of which waited for: 3 -> 11; matrix products, arithmetic and copies ran while one was open for 0% -> 1% of each run, Pallas kernels for 0% -> 0%
where the time goes in v1:
time: 265 us
  blocking collectives  93.1 us (35%)
  Pallas kernels  78.8 us (30%)
  waiting for transfers between devices  46.2 us (17%)
  starting transfers between devices  31.8 us (12%)
  local copies, waits for them, and re-layouts  6.62 us (2%)
  other arithmetic  5.33 us (2%)
    pallas_call x2, Pallas kernels, attention(): pl.pallas_call(functools.partial(attention_kernel, nblk), grid_spec=pltpu...  78.8 us
    ppermute x14, waiting for transfers between devices, spread(): lax.ppermute(bias, 'row', [(i, turned(i, dx, dy)) for i in range(nr)])  44.1 us
    all_to_all x1, blocking collectives, per_device(): lax.all_to_all(message, ('row', 'col'), 0, 0, tiled=True, axis_index_grou...  42.4 us
    all_to_all x1, blocking collectives, per_device(): lax.all_to_all(message, 'col', 0, 0, tiled=True, axis_index_groups=same_c...  32.1 us
    ppermute x14, starting transfers between devices, spread(): lax.ppermute(bias, 'row', [(i, turned(i, dx, dy)) for i in range(nr)])  22.9 us
    all_to_all x1, blocking collectives, per_device(): got = lax.all_to_all(both.reshape(nr, -1, CH), 'row', 0, 0, tiled=True)  18.7 us
  transfers between devices with their start and end apart: 18, of which 11 were waited for; matrix products, arithmetic and copies ran while one was open for 1% of the time, Pallas kernels for 0%

profile of v1, /device:TPU:1, one launch (start us, length us, event | category | flops | bytes accessed | tf_op | source)
XLA Modules:
  0.0 264.8 jit_solution(16040150263477478799)
XLA Ops:
  2.2 1.8 fusion.7
  6.3 32.1 %all_to_all.15 = bf16[16,224,128]{2,1,0:T(8,128)(2,1)S(1)} all-to-all(bf16[16,224,128]{2,1,0:T(8,128)(2,1)S(1)} %maximum_maximum_fusion.1), channel_id=1, replica_groups={{0,2,4,6,8,10,12,14,16,18,20,22,24,26,28,30},{1,3,5,7,9,11,13,15,17,19,..., dimensions={0} | all-to-all | bytes 1835008 | tf_op jit(solution)/shard_map/all_to_all | solution.py:149
  39.2 2.6 collective-permute-start.1
  44.4 1.5 collective-permute-start.3
  46.2 2.5 collective-permute-start.4
  48.8 1.6 collective-permute-start.5
  50.3 2.4 collective-permute-done.2.refs_1_
  52.7 2.1 collective-permute-start.6
  54.8 3.1 %collective-permute-start.7 = (bf16[384,384]{1,0:T(8,128)(2,1)S(1)}, bf16[384,384]{1,0:T(8,128)(2,1)S(1)}, u32[]{:S(2)}, u32[]{:S(2)}) collective-permute-start(bf16[384,384]{1,0:T(8,128)(2,1)S(1)} %pad_maximum_fusion.2.refs_0_), channel_id=1, source_target_pairs={{0,224},{32,128},{64,160},{96,192},{128,96},{160,0},{192,32},{224,... | collective-permute-start | bytes 884744 | tf_op jit(solution)/shard_map/ppermute | solution.py:126
  57.9 2.5 collective-permute-start.8
  60.9 3.3 %collective-permute-done.5.refs_4_ = bf16[384,384]{1,0:T(8,128)(2,1)S(1)} collective-permute-done((bf16[384,384]{1,0:T(8,128)(2,1)S(1)}, bf16[384,384]{1,0:T(8,128)(2,1)S(1)}, u32[]{:S(2)}, u32[]{:S(2)}) %collective-permute-start.5) | collective-permute-done | bytes 294944 | tf_op jit(solution)/shard_map/ppermute | solution.py:126
  65.1 7.9 %collective-permute-done.8.refs_7_ = bf16[384,384]{1,0:T(8,128)(2,1)S(1)} collective-permute-done((bf16[384,384]{1,0:T(8,128)(2,1)S(1)}, bf16[384,384]{1,0:T(8,128)(2,1)S(1)}, u32[]{:S(2)}, u32[]{:S(2)}) %collective-permute-start.8) | collective-permute-done | bytes 294944 | tf_op jit(solution)/shard_map/ppermute | solution.py:126
  73.0 39.4 %shard_map.73 = bf16[6,384,128]{2,1,0:T(8,128)(2,1)S(1)} custom-call(s32[8]{0:T(128)S(1)} %stack.62.blk_ref, bf16[6,768,128]{2,1,0:T(8,128)(2,1)S(1)} %bitcast.76, bf16[6,384,128]{2,1,0:T(8,128)(2,1)S(1)} %slice.104.xq_ref, bf16[384,384]{1,0:T(8,128)(2,1)S(1)} %pad_maximum_fusion.2.refs_0_, bf16[384,384]{1,0:T(8,128)(2,1)S(1)} %collective-permute-done.2.refs_1_, ...), custom_call_target="tpu_custom_call" | custom-call | flops 7247757312 | bytes 6291456 | tf_op jit(solution)/shard_map/pallas_call | solution.py:90
  116.2 42.4 %all_to_all.16 = bf16[128,32,128]{2,1,0:T(8,128)(2,1)S(1)} all-to-all(bf16[128,32,128]{2,1,0:T(8,128)(2,1)S(1)} %copy.35), channel_id=1, replica_groups={{0,2,4,6,8,10,12,14,16,18,20,22,24,26,28,30,32,34,36,38,40,42,44,46,48,..., dimensions={0} | all-to-all | bytes 2097152 | tf_op jit(solution)/shard_map/all_to_all | solution.py:178
  159.2 4.5 %collective-permute-start.9 = (bf16[3,768,128]{2,1,0:T(8,128)(2,1)S(1)}, bf16[3,768,128]{2,1,0:T(8,128)(2,1)S(1)}, u32[]{:S(2)}, u32[]{:S(2)}) collective-permute-start(bf16[3,768,128]{2,1,0:T(8,128)(2,1)S(1)} %bitcast.84), channel_id=1, source_target_pairs={{0,1},{1,0},{2,3},{3,2},{4,5},{5,4},{6,7},{7,6},{8,9},{9,8},{10,11... | collective-permute-start | bytes 1769480 | tf_op jit(solution)/shard_map/ppermute | solution.py:182
  164.6 2.7 %collective-permute-start.11 = (bf16[384,384]{1,0:T(8,128)(2,1)S(1)}, bf16[384,384]{1,0:T(8,128)(2,1)S(1)}, u32[]{:S(2)}, u32[]{:S(2)}) collective-permute-start(bf16[384,384]{1,0:T(8,128)(2,1)S(1)} %pad_maximum_fusion.3.refs_0_), channel_id=1, source_target_pairs={{0,96},{32,0},{64,32},{96,64},{128,224},{160,128},{192,160},{224,1... | collective-permute-start | bytes 884744 | tf_op jit(solution)/shard_map/ppermute | solution.py:126
  167.6 13.1 %collective-permute-done.10.refs_1_ = bf16[384,384]{1,0:T(8,128)(2,1)S(1)} collective-permute-done((bf16[384,384]{1,0:T(8,128)(2,1)S(1)}, bf16[384,384]{1,0:T(8,128)(2,1)S(1)}, u32[]{:S(2)}, u32[]{:S(2)}) %collective-permute-start.10) | collective-permute-done | bytes 294944 | tf_op jit(solution)/shard_map/ppermute | solution.py:126
  180.8 5.1 %collective-permute-start.15 = (bf16[384,384]{1,0:T(8,128)(2,1)S(1)}, bf16[384,384]{1,0:T(8,128)(2,1)S(1)}, u32[]{:S(2)}, u32[]{:S(2)}) collective-permute-start(bf16[384,384]{1,0:T(8,128)(2,1)S(1)} %pad_maximum_fusion.3.refs_0_), channel_id=1, source_target_pairs={{0,224},{32,128},{64,160},{96,192},{128,96},{160,0},{192,32},{224,... | collective-permute-start | bytes 884744 | tf_op jit(solution)/shard_map/ppermute | solution.py:126
  186.0 6.1 %collective-permute-done.14.refs_5_ = bf16[384,384]{1,0:T(8,128)(2,1)S(1)} collective-permute-done((bf16[384,384]{1,0:T(8,128)(2,1)S(1)}, bf16[384,384]{1,0:T(8,128)(2,1)S(1)}, u32[]{:S(2)}, u32[]{:S(2)}) %collective-permute-start.14) | collective-permute-done | bytes 294944 | tf_op jit(solution)/shard_map/ppermute | solution.py:126
  192.1 2.7 %collective-permute-done.15.refs_6_ = bf16[384,384]{1,0:T(8,128)(2,1)S(1)} collective-permute-done((bf16[384,384]{1,0:T(8,128)(2,1)S(1)}, bf16[384,384]{1,0:T(8,128)(2,1)S(1)}, u32[]{:S(2)}, u32[]{:S(2)}) %collective-permute-start.15) | collective-permute-done | bytes 294944 | tf_op jit(solution)/shard_map/ppermute | solution.py:126
  194.8 7.7 %collective-permute-done.16.refs_7_ = bf16[384,384]{1,0:T(8,128)(2,1)S(1)} collective-permute-done((bf16[384,384]{1,0:T(8,128)(2,1)S(1)}, bf16[384,384]{1,0:T(8,128)(2,1)S(1)}, u32[]{:S(2)}, u32[]{:S(2)}) %collective-permute-start.16) | collective-permute-done | bytes 294944 | tf_op jit(solution)/shard_map/ppermute | solution.py:126
  202.5 39.4 %shard_map.74 = bf16[6,384,128]{2,1,0:T(8,128)(2,1)S(1)} custom-call(s32[8]{0:T(128)S(1)} %stack.62.blk_ref, bf16[6,768,128]{2,1,0:T(8,128)(2,1)S(1)} %pad_maximum_fusion.x_ref, bf16[6,384,128]{2,1,0:T(8,128)(2,1)S(1)} %bitcast.77, bf16[384,384]{1,0:T(8,128)(2,1)S(1)} %pad_maximum_fusion.3.refs_0_, bf16[384,384]{1,0:T(8,128)(2,1)S(1)} %collective-permute-done.10.refs_1_, ...), custom_call_target="tpu_custom_call" | custom-call | flops 7247757312 | bytes 6291456 | tf_op jit(solution)/shard_map/pallas_call | solution.py:90
  241.9 1.7 collective-permute-start.17
  245.0 18.7 %all_to_all.17 = bf16[8,288,128]{2,1,0:T(8,128)(2,1)S(1)} all-to-all(bf16[8,288,128]{2,1,0:T(8,128)(2,1)S(1)} %bitcast.80), channel_id=1, replica_groups=mesh['row'=8,'col'=32] {'row'}, dimensions={0} | all-to-all | bytes 1179648 | tf_op jit(solution)/shard_map/all_to_all | solution.py:197
  (87 shorter events, 17.5 us)
Async XLA Ops:
  0.0 4.0 %copy-start = (bf16[96,24,128]{2,1,0:T(8,128)(2,1)S(1)}, bf16[96,24,128]{2,1,0:T(8,128)(2,1)}, u32[]{:S(2)}) copy-start(bf16[96,24,128]{2,1,0:T(8,128)(2,1)} %param.7) | copy-start | bytes 1769476
  0.0 4.0 %copy-start.5 = (bf16[2,128,4]{1,2,0:T(4,128)(2,1)S(1)}, bf16[2,128,4]{1,2,0:T(4,128)(2,1)}, u32[]{:S(2)}) copy-start(bf16[2,128,4]{1,2,0:T(4,128)(2,1)} %param.10) | copy-start | bytes 6148
  39.2 6.7 %copy-start.2 = (bf16[2,128,128]{2,1,0:T(8,128)(2,1)S(1)}, bf16[2,128,128]{2,1,0:T(8,128)(2,1)}, u32[]{:S(2)}) copy-start(bf16[2,128,128]{2,1,0:T(8,128)(2,1)} %param.12) | copy-start | bytes 196612
  39.2 7.0 %copy-start.1 = (bf16[2,128,512]{2,1,0:T(8,128)(2,1)S(1)}, bf16[2,128,512]{2,1,0:T(8,128)(2,1)}, u32[]{:S(2)}) copy-start(bf16[2,128,512]{2,1,0:T(8,128)(2,1)} %param.9) | copy-start | bytes 786436
  39.2 3.7 %collective-permute-start.1 = (bf16[384,192]{1,0:T(8,128)(2,1)S(1)}, bf16[384,192]{1,0:T(8,128)(2,1)S(1)}, u32[]{:S(2)}, u32[]{:S(2)}) collective-permute-start(bf16[384,192]{1,0:T(8,128)(2,1)S(1)} %bitcast.94), channel_id=1, source_target_pairs={{0,1},{1,0},{2,3},{3,2},{4,5},{5,4},{6,7},{7,6},{8,9},{9,8},{10,11... | collective-permute-start | bytes 442376 | tf_op jit(solution)/shard_map/ppermute | solution.py:153
  41.9 18.5 %copy-start.3 = (f32[2,128]{1,0:T(2,128)S(1)}, f32[2,128]{1,0:T(2,128)}, u32[]{:S(2)}) copy-start(f32[2,128]{1,0:T(2,128)} %param.13) | copy-start | bytes 3076
  41.9 18.5 %copy-start.4 = (f32[2,128]{1,0:T(2,128)S(1)}, f32[2,128]{1,0:T(2,128)}, u32[]{:S(2)}) copy-start(f32[2,128]{1,0:T(2,128)} %param.11) | copy-start | bytes 3076
  41.9 16.0 %collective-permute-start = (bf16[16,144,128]{2,1,0:T(8,128)(2,1)S(1)}, bf16[16,144,128]{2,1,0:T(8,128)(2,1)S(1)}, u32[]{:S(2)}, u32[]{:S(2)}) collective-permute-start(bf16[16,144,128]{2,1,0:T(8,128)(2,1)S(1)} %slice.103), channel_id=1, source_target_pairs={{0,1},{1,0},{2,3},{3,2},{4,5},{5,4},{6,7},{7,6},{8,9},{9,8},{10,11... | collective-permute-start | bytes 1769480 | tf_op jit(solution)/shard_map/ppermute | solution.py:151
  43.0 9.6 %collective-permute-start.2 = (bf16[384,384]{1,0:T(8,128)(2,1)S(1)}, bf16[384,384]{1,0:T(8,128)(2,1)S(1)}, u32[]{:S(2)}, u32[]{:S(2)}) collective-permute-start(bf16[384,384]{1,0:T(8,128)(2,1)S(1)} %pad_maximum_fusion.2.refs_0_), channel_id=1, source_target_pairs={{0,32},{32,64},{64,96},{96,0},{128,160},{160,192},{192,224},{224,1... | collective-permute-start | bytes 884744 | tf_op jit(solution)/shard_map/ppermute | solution.py:126
  44.4 10.4 %collective-permute-start.3 = (bf16[384,384]{1,0:T(8,128)(2,1)S(1)}, bf16[384,384]{1,0:T(8,128)(2,1)S(1)}, u32[]{:S(2)}, u32[]{:S(2)}) collective-permute-start(bf16[384,384]{1,0:T(8,128)(2,1)S(1)} %pad_maximum_fusion.2.refs_0_), channel_id=1, source_target_pairs={{0,96},{32,0},{64,32},{96,64},{128,224},{160,128},{192,160},{224,1... | collective-permute-start | bytes 884744 | tf_op jit(solution)/shard_map/ppermute | solution.py:126
  46.2 14.6 %collective-permute-start.4 = (bf16[384,384]{1,0:T(8,128)(2,1)S(1)}, bf16[384,384]{1,0:T(8,128)(2,1)S(1)}, u32[]{:S(2)}, u32[]{:S(2)}) collective-permute-start(bf16[384,384]{1,0:T(8,128)(2,1)S(1)} %pad_maximum_fusion.2.refs_0_), channel_id=1, source_target_pairs={{0,128},{32,160},{64,192},{96,224},{128,0},{160,32},{192,64},{224,... | collective-permute-start | bytes 884744 | tf_op jit(solution)/shard_map/ppermute | solution.py:126
  48.8 15.4 %collective-permute-start.5 = (bf16[384,384]{1,0:T(8,128)(2,1)S(1)}, bf16[384,384]{1,0:T(8,128)(2,1)S(1)}, u32[]{:S(2)}, u32[]{:S(2)}) collective-permute-start(bf16[384,384]{1,0:T(8,128)(2,1)S(1)} %pad_maximum_fusion.2.refs_0_), channel_id=1, source_target_pairs={{0,64},{32,96},{64,0},{96,32},{128,192},{160,224},{192,128},{224,1... | collective-permute-start | bytes 884744 | tf_op jit(solution)/shard_map/ppermute | solution.py:126
  52.7 12.0 %collective-permute-start.6 = (bf16[384,384]{1,0:T(8,128)(2,1)S(1)}, bf16[384,384]{1,0:T(8,128)(2,1)S(1)}, u32[]{:S(2)}, u32[]{:S(2)}) collective-permute-start(bf16[384,384]{1,0:T(8,128)(2,1)S(1)} %pad_maximum_fusion.2.refs_0_), channel_id=1, source_target_pairs={{0,160},{32,192},{64,224},{96,128},{128,32},{160,64},{192,96},{224... | collective-permute-start | bytes 884744 | tf_op jit(solution)/shard_map/ppermute | solution.py:126
  54.8 10.3 %collective-permute-start.7 = (bf16[384,384]{1,0:T(8,128)(2,1)S(1)}, bf16[384,384]{1,0:T(8,128)(2,1)S(1)}, u32[]{:S(2)}, u32[]{:S(2)}) collective-permute-start(bf16[384,384]{1,0:T(8,128)(2,1)S(1)} %pad_maximum_fusion.2.refs_0_), channel_id=1, source_target_pairs={{0,224},{32,128},{64,160},{96,192},{128,96},{160,0},{192,32},{224,... | collective-permute-start | bytes 884744 | tf_op jit(solution)/shard_map/ppermute | solution.py:126
  57.9 15.1 %collective-permute-start.8 = (bf16[384,384]{1,0:T(8,128)(2,1)S(1)}, bf16[384,384]{1,0:T(8,128)(2,1)S(1)}, u32[]{:S(2)}, u32[]{:S(2)}) collective-permute-start(bf16[384,384]{1,0:T(8,128)(2,1)S(1)} %pad_maximum_fusion.2.refs_0_), channel_id=1, source_target_pairs={{0,192},{32,224},{64,128},{96,160},{128,64},{160,96},{192,0},{224,... | collective-permute-start | bytes 884744 | tf_op jit(solution)/shard_map/ppermute | solution.py:126
  159.2 26.6 %collective-permute-start.9 = (bf16[3,768,128]{2,1,0:T(8,128)(2,1)S(1)}, bf16[3,768,128]{2,1,0:T(8,128)(2,1)S(1)}, u32[]{:S(2)}, u32[]{:S(2)}) collective-permute-start(bf16[3,768,128]{2,1,0:T(8,128)(2,1)S(1)} %bitcast.84), channel_id=1, source_target_pairs={{0,1},{1,0},{2,3},{3,2},{4,5},{5,4},{6,7},{7,6},{8,9},{9,8},{10,11... | collective-permute-start | bytes 1769480 | tf_op jit(solution)/shard_map/ppermute | solution.py:182
  164.5 16.2 %collective-permute-start.10 = (bf16[384,384]{1,0:T(8,128)(2,1)S(1)}, bf16[384,384]{1,0:T(8,128)(2,1)S(1)}, u32[]{:S(2)}, u32[]{:S(2)}) collective-permute-start(bf16[384,384]{1,0:T(8,128)(2,1)S(1)} %pad_maximum_fusion.3.refs_0_), channel_id=1, source_target_pairs={{0,32},{32,64},{64,96},{96,0},{128,160},{160,192},{192,224},{224,1... | collective-permute-start | bytes 884744 | tf_op jit(solution)/shard_map/ppermute | solution.py:126
  164.6 16.1 %collective-permute-start.11 = (bf16[384,384]{1,0:T(8,128)(2,1)S(1)}, bf16[384,384]{1,0:T(8,128)(2,1)S(1)}, u32[]{:S(2)}, u32[]{:S(2)}) collective-permute-start(bf16[384,384]{1,0:T(8,128)(2,1)S(1)} %pad_maximum_fusion.3.refs_0_), channel_id=1, source_target_pairs={{0,96},{32,0},{64,32},{96,64},{128,224},{160,128},{192,160},{224,1... | collective-permute-start | bytes 884744 | tf_op jit(solution)/shard_map/ppermute | solution.py:126
  167.3 18.7 %collective-permute-start.12 = (bf16[384,384]{1,0:T(8,128)(2,1)S(1)}, bf16[384,384]{1,0:T(8,128)(2,1)S(1)}, u32[]{:S(2)}, u32[]{:S(2)}) collective-permute-start(bf16[384,384]{1,0:T(8,128)(2,1)S(1)} %pad_maximum_fusion.3.refs_0_), channel_id=1, source_target_pairs={{0,128},{32,160},{64,192},{96,224},{128,0},{160,32},{192,64},{224,... | collective-permute-start | bytes 884744 | tf_op jit(solution)/shard_map/ppermute | solution.py:126
  167.4 18.6 %collective-permute-start.13 = (bf16[384,384]{1,0:T(8,128)(2,1)S(1)}, bf16[384,384]{1,0:T(8,128)(2,1)S(1)}, u32[]{:S(2)}, u32[]{:S(2)}) collective-permute-start(bf16[384,384]{1,0:T(8,128)(2,1)S(1)} %pad_maximum_fusion.3.refs_0_), channel_id=1, source_target_pairs={{0,64},{32,96},{64,0},{96,32},{128,192},{160,224},{192,128},{224,1... | collective-permute-start | bytes 884744 | tf_op jit(solution)/shard_map/ppermute | solution.py:126
  180.8 11.3 %collective-permute-start.14 = (bf16[384,384]{1,0:T(8,128)(2,1)S(1)}, bf16[384,384]{1,0:T(8,128)(2,1)S(1)}, u32[]{:S(2)}, u32[]{:S(2)}) collective-permute-start(bf16[384,384]{1,0:T(8,128)(2,1)S(1)} %pad_maximum_fusion.3.refs_0_), channel_id=1, source_target_pairs={{0,160},{32,192},{64,224},{96,128},{128,32},{160,64},{192,96},{224... | collective-permute-start | bytes 884744 | tf_op jit(solution)/shard_map/ppermute | solution.py:126
  180.8 14.1 %collective-permute-start.15 = (bf16[384,384]{1,0:T(8,128)(2,1)S(1)}, bf16[384,384]{1,0:T(8,128)(2,1)S(1)}, u32[]{:S(2)}, u32[]{:S(2)}) collective-permute-start(bf16[384,384]{1,0:T(8,128)(2,1)S(1)} %pad_maximum_fusion.3.refs_0_), channel_id=1, source_target_pairs={{0,224},{32,128},{64,160},{96,192},{128,96},{160,0},{192,32},{224,... | collective-permute-start | bytes 884744 | tf_op jit(solution)/shard_map/ppermute | solution.py:126
  185.8 16.6 %collective-permute-start.16 = (bf16[384,384]{1,0:T(8,128)(2,1)S(1)}, bf16[384,384]{1,0:T(8,128)(2,1)S(1)}, u32[]{:S(2)}, u32[]{:S(2)}) collective-permute-start(bf16[384,384]{1,0:T(8,128)(2,1)S(1)} %pad_maximum_fusion.3.refs_0_), channel_id=1, source_target_pairs={{0,192},{32,224},{64,128},{96,160},{128,64},{160,96},{192,0},{224,... | collective-permute-start | bytes 884744 | tf_op jit(solution)/shard_map/ppermute | solution.py:126
  241.9 2.9 %collective-permute-start.17 = (bf16[3,384,128]{2,1,0:T(8,128)(2,1)S(1)}, bf16[3,384,128]{2,1,0:T(8,128)(2,1)S(1)}, u32[]{:S(2)}, u32[]{:S(2)}) collective-permute-start(bf16[3,384,128]{2,1,0:T(8,128)(2,1)S(1)} %slice.114), channel_id=1, source_target_pairs={{0,1},{1,0},{2,3},{3,2},{4,5},{5,4},{6,7},{7,6},{8,9},{9,8},{10,11... | collective-permute-start | bytes 884744 | tf_op jit(solution)/shard_map/ppermute | solution.py:194

commit v2 on v1

--- a/solution.py
+++ b/solution.py
@@ -11,6 +11,7 @@
 WIDTH = 32
 CH = 128
 LOG2E = 1.4426950408889634
+CALLS = (4, 4)
 NT = (((1,), (1,)), ((), ()))
 
 
@@ -21,15 +22,61 @@
     return ((values - center) * lax.rsqrt(spread + 1e-05) * gain).astype(jnp.bfloat16)
 
 
-def attention_kernel(
-    nblk, blk_ref, x_ref, xq_ref, *refs
-):
+def whole(a):
+    return pl.BlockSpec(a.shape, lambda i, *_: (0,) * a.ndim)
+
+
+def by_row(a):
+    return pl.BlockSpec((1,) + a.shape[1:], lambda i, *_: (i, 0, 0))
+
+
+def prepare_kernel(x_ref, xq_ref, gain_ref, wp_ref, gb_ref, kt_ref, v_ref, q_ref, gate_ref):
+    gain = gain_ref[...]
+    xn = normalize(x_ref[0], gain)
+    k = jnp.dot(xn, wp_ref[:, CH : 2 * CH], preferred_element_type=jnp.float32)
+    kt_ref[0] = k.astype(jnp.bfloat16).T
+    v = jnp.dot(xn, wp_ref[:, 2 * CH : 3 * CH], preferred_element_type=jnp.float32)
+    v_ref[0] = v.astype(jnp.bfloat16)
+    xqn = normalize(xq_ref[0], gain)
+    q = jnp.dot(xqn, wp_ref[:, :CH], preferred_element_type=jnp.float32)
+    q_ref[0] = q.astype(jnp.bfloat16)
+    gate = jnp.dot(xqn, wp_ref[:, 3 * CH :], preferred_element_type=jnp.float32)
+    gate_ref[0] = jax.nn.sigmoid(gate + gb_ref[...])
+
+
+def prepare(x, xq, gain, wp, gb):
+    nrow, keys, _ = x.shape
+    nq = xq.shape[1]
+    outs = [
+        jax.ShapeDtypeStruct((nrow, CH, keys), jnp.bfloat16),
+        jax.ShapeDtypeStruct((nrow, keys, CH), jnp.bfloat16),
+        jax.ShapeDtypeStruct((nrow, nq, CH), jnp.bfloat16),
+        jax.ShapeDtypeStruct((nrow, nq, CH), jnp.float32),
+    ]
+    small = [gain[None], wp, gb[None]]
+    return pl.pallas_call(
+        prepare_kernel,
+        grid=(nrow,),
+        in_specs=[by_row(x), by_row(xq)] + [whole(a) for a in small],
+        out_specs=[by_row(a) for a in outs],
+        out_shape=outs,
+        compiler_params=pltpu.CompilerParams(vmem_limit_bytes=16 << 20),
+        cost_estimate=pl.CostEstimate(
+            flops=4 * 10**9, bytes_accessed=6 << 20, transcendentals=nrow * nq * CH
+        ),
+        name="prepare",
+    )(x, xq, *small)
+
+
+def attention_kernel(nblk, ndone, stack, blk_ref, done_blk_ref, kt_ref, v_ref, q_ref, gate_ref, xq_ref, *refs):
     bias_refs = refs[:nblk]
-    gain_ref, wp_ref, gb_ref, wo_ref, ob_ref, out_ref, biasf = refs[nblk:]
-    keys = x_ref.shape[1]
+    wo_ref, ob_ref = refs[nblk : nblk + 2]
+    done_refs = refs[nblk + 2 : nblk + 2 + ndone]
+    out_ref, biasf = refs[nblk + 2 + ndone :]
     half = bias_refs[0].shape[0]
     rows = bias_refs[0].shape[1] // 2
     block = rows // HEADS
+    nq = nblk * block
 
     @pl.when(pl.program_id(0) == 0)
     def _():
@@ -38,74 +85,96 @@
         for s in range(2):
             pick = (to == at + s * rows).astype(jnp.bfloat16)
             for b in range(nblk):
-                biasf[b, :, s * half : (s + 1) * half] = (
-                    lax.dot_general(pick, bias_refs[b][...], NT, preferred_element_type=jnp.float32)
-                    * LOG2E
+                part = lax.dot_general(
+                    pick, bias_refs[b][...], NT, preferred_element_type=jnp.float32
                 )
-
-    gain = gain_ref[...]
-    xn = normalize(x_ref[0], gain)
-    kv = jnp.dot(xn, wp_ref[:, CH : 3 * CH], preferred_element_type=jnp.float32).astype(jnp.bfloat16)
-    k2 = jnp.concatenate([kv[:, :CH], kv[:, :CH]], axis=1)
-    v1 = jnp.concatenate([kv[:, CH:], jnp.ones((keys, CH), jnp.bfloat16)], axis=1)
-    head_of = lax.broadcasted_iota(jnp.int32, (block, CH), 1) // WIDTH
-
-    for b in range(nblk):
-        q0 = pl.multiple_of(blk_ref[b] * block, 16)
-        xq = xq_ref[0, pl.ds(q0, block), :]
-        xqn = normalize(xq, gain)
-        q = jnp.dot(xqn, wp_ref[:, :CH], preferred_element_type=jnp.float32)
-        gate = jnp.dot(xqn, wp_ref[:, 3 * CH :], preferred_element_type=jnp.float32)
-        qs = q.astype(jnp.bfloat16).astype(jnp.float32) * (WIDTH**-0.5 * LOG2E)
-        qh = qs.astype(jnp.bfloat16).astype(jnp.float32)
-        ql = qs - qh
-        qm = jnp.concatenate(
-            [
-                jnp.concatenate([jnp.where(head_of == h, t, 0.0) for t in (qh, ql)], axis=1)
-                for h in range(HEADS)
-            ],
-            axis=0,
-        ).astype(jnp.bfloat16)
-        s = lax.dot_general(qm, k2, NT, preferred_element_type=jnp.float32) + biasf[b]
-        top = jnp.max(s, axis=-1, keepdims=True)
-        p = jnp.exp2(s - top).astype(jnp.bfloat16)
-        o = jnp.dot(p, v1, preferred_element_type=jnp.float32)
-        o = o[:, :CH] / o[:, CH:]
-        mixed = jnp.zeros((block, CH), jnp.float32)
-        for h in range(HEADS):
-            mixed = jnp.where(head_of == h, o[h * block : (h + 1) * block], mixed)
-        gated = (mixed * jax.nn.sigmoid(gate + gb_ref[...])).astype(jnp.bfloat16)
-        y = jnp.dot(gated, wo_ref[...], preferred_element_type=jnp.float32) + ob_ref[...]
-        out_ref[0, pl.ds(q0, block), :] = (xq.astype(jnp.float32) + y).astype(jnp.bfloat16)
-
-
-def attention(blocks, x, xq, biases, gain, wp, gb, wo, ob):
-    nrow, keys, _ = x.shape
-    nq = xq.shape[1]
+                for h in range(HEADS):
+                    biasf[
+                        pl.ds(h * nq + b * block, block), pl.ds(s * half, half)
+                    ] = part[h * block : (h + 1) * block] * LOG2E
+
+    kt = kt_ref[0]
+    v = v_ref[0]
+    starts = [pl.multiple_of(blk_ref[b] * block, 16) for b in range(nblk)]
+    q = jnp.concatenate([q_ref[0, pl.ds(t, block), :] for t in starts], axis=0)
+    head_of = lax.broadcasted_iota(jnp.int32, q.shape, 1) // WIDTH
+    mixed = jnp.zeros(q.shape, jnp.float32)
+    for h0 in range(0, HEADS, stack):
+        qh = jnp.concatenate(
+            [jnp.where(head_of == h, q, jnp.zeros_like(q)) for h in range(h0, h0 + stack)], axis=0
+        )
+        s = jnp.dot(qh, kt, preferred_element_type=jnp.float32)
+        s = s * (WIDTH**-0.5 * LOG2E) + biasf[h0 * nq : (h0 + stack) * nq]
+        e = jnp.exp2(s - jnp.max(s, axis=-1, keepdims=True))
+        p = (e * (1.0 / jnp.sum(e, axis=-1, keepdims=True))).astype(jnp.bfloat16)
+        o = jnp.dot(p, v, preferred_element_type=jnp.float32)
+        for t in range(stack):
+            mixed = jnp.where(head_of == h0 + t, o[t * nq : (t + 1) * nq], mixed)
+    gate = jnp.concatenate([gate_ref[0, pl.ds(t, block), :] for t in starts], axis=0)
+    xq = jnp.concatenate([xq_ref[0, pl.ds(t, block), :] for t in starts], axis=0)
+    gated = (mixed * gate).astype(jnp.bfloat16)
+    y = jnp.dot(gated, wo_ref[...], preferred_element_type=jnp.float32) + ob_ref[...]
+    y = (xq.astype(jnp.float32) + y).astype(jnp.bfloat16)
+    if out_ref.shape[1] == nq:
+        out_ref[0] = y
+    else:
+        for b in range(nblk):
+            out_ref[0, pl.ds(starts[b], block), :] = y[b * block : (b + 1) * block]
+        at = 0
+        for ref in done_refs:
+            for b in range(ref.shape[1] // block):
+                t = pl.multiple_of(done_blk_ref[at] * block, 16)
+                out_ref[0, pl.ds(t, block), :] = ref[0, b * block : (b + 1) * block, :]
+                at += 1
+
+
+def attend(ids, parts, xq, biases, wo, ob, done_ids, done, whole_out, stack):
+    nrow, _, keys = parts[0].shape
     nblk = len(biases)
-    rows = biases[0].shape[1] // 2
-    whole = lambda a: pl.BlockSpec(a.shape, lambda i, *_: (0,) * a.ndim)
-    small = [gain[None], wp, gb[None], wo, ob[None]]
-    flops = 2 * nrow * HEADS * nq * keys * 512
+    nq = nblk * biases[0].shape[1] // 2 // HEADS
+    out = jax.ShapeDtypeStruct((nrow, xq.shape[1] if whole_out else nq, CH), jnp.bfloat16)
+    small = [wo, ob[None]]
     return pl.pallas_call(
-        functools.partial(attention_kernel, nblk),
+        functools.partial(attention_kernel, nblk, len(done), stack),
         grid_spec=pltpu.PrefetchScalarGridSpec(
-            num_scalar_prefetch=1,
+            num_scalar_prefetch=2,
             grid=(nrow,),
-            in_specs=[
-                pl.BlockSpec((1, keys, CH), lambda i, *_: (i, 0, 0)),
-                pl.BlockSpec((1, nq, CH), lambda i, *_: (i, 0, 0)),
-            ]
-            + [whole(a) for a in list(biases) + small],
-            out_specs=pl.BlockSpec((1, nq, CH), lambda i, *_: (i, 0, 0)),
-            scratch_shapes=[pltpu.VMEM((nblk, rows, keys), jnp.float32)],
+            in_specs=[by_row(a) for a in parts]
+            + [by_row(xq)]
+            + [whole(a) for a in list(biases) + small]
+            + [by_row(a) for a in done],
+            out_specs=by_row(out),
+            scratch_shapes=[pltpu.VMEM((HEADS * nq, keys), jnp.float32)],
         ),
-        out_shape=jax.ShapeDtypeStruct((nrow, nq, CH), jnp.bfloat16),
+        out_shape=out,
         compiler_params=pltpu.CompilerParams(vmem_limit_bytes=40 << 20),
         cost_estimate=pl.CostEstimate(
-            flops=flops, bytes_accessed=6 << 20, transcendentals=nrow * HEADS * nq * keys
+            flops=nblk * 28 * 10**8, bytes_accessed=6 << 20, transcendentals=nrow * HEADS * nq * keys
         ),
-    )(blocks, x, xq, *biases, *small)
+        name="attend",
+    )(ids, done_ids, *parts, xq, *biases, *small, *done)
+
+
+def attention(ids, x, xq, biases, gain, wp, gb, wo, ob):
+    parts = prepare(x, xq, gain, wp, gb)
+    done, at = [], 0
+    for n in CALLS:
+        last = at + n == len(biases)
+        y = attend(
+            ids[at : at + n],
+            parts,
+            xq,
+            biases[at : at + n],
+            wo,
+            ob,
+            ids[: max(at, 1)],
+            done if last else [],
+            last,
+            min(HEADS, max(1, 8 // n)),
+        )
+        done.append(y)
+        at += n
+    return done[-1]
 
 
 def solution(mesh):

time: 265 us -> 203 us (0.77); the launches traced: 265 us -> 200 us
  blocking collectives: 93.1 us -> 59.4 us
  Pallas kernels: 78.8 us -> 46.9 us
  starting transfers between devices: 31.8 us -> 43.6 us
  waiting for transfers between devices: 46.2 us -> 34.6 us
    ppermute x14, waiting for transfers between devices: 44.1 us -> 10.1 us  [spread(): lax.ppermute(bias, 'row', [(i, turned(i, dx, dy)) for i in range(nr)])]
    all_to_all x1 -> x0, blocking collectives: 32.1 us -> none  [per_device(): lax.all_to_all(message, 'col', 0, 0, tiled=True, axis_index_groups=same_c...]
    pallas_call x2 -> x6, Pallas kernels: 78.8 us -> 46.9 us  [the longest x4 39.8 us: attend(): pl.pallas_call(functools.partial(attention_kernel, nblk, len(done), stack...]
    all_to_all x0 -> x1, waiting for transfers between devices: none -> 22.1 us  [per_device(): lax.all_to_all(message, 'col', 0, 0, tiled=True, axis_index_groups=same_c...]
    all_to_all x0 -> x1, starting transfers between devices: none -> 10.2 us  [per_device(): lax.all_to_all(message, 'col', 0, 0, tiled=True, axis_index_groups=same_c...]
    ppermute x1, starting transfers between devices: 1.68 us -> 6.8 us  [per_device(): other = lax.ppermute(last[part:], 'col', swap_core)]
    ppermute x14, starting transfers between devices: 22.9 us -> 19.6 us  [spread(): lax.ppermute(bias, 'row', [(i, turned(i, dx, dy)) for i in range(nr)])]
  transfers between devices with their start and end apart: 18 -> 19, of which waited for: 11 -> 7; matrix products, arithmetic and copies ran while one was open for 1% -> 1% of each run, Pallas kernels for 0% -> 14%
where the time goes in v2:
time: 203 us; the launch traced here: 200 us
  blocking collectives  59.4 us (29%)
  Pallas kernels  46.9 us (23%)
  starting transfers between devices  43.6 us (21%)
  waiting for transfers between devices  34.6 us (17%)
  other arithmetic  6.38 us (3%)
  local copies, waits for them, and re-layouts  5.8 us (3%)
  matrix products  2.43 us (1%)
    all_to_all x1, blocking collectives, per_device(): lax.all_to_all(message, ('row', 'col'), 0, 0, tiled=True, axis_index_grou...  40.5 us
    pallas_call x4, Pallas kernels, attend(): pl.pallas_call(functools.partial(attention_kernel, nblk, len(done), stack...  39.8 us
    all_to_all x1, waiting for transfers between devices, per_device(): lax.all_to_all(message, 'col', 0, 0, tiled=True, axis_index_groups=same_c...  22.1 us
    ppermute x14, starting transfers between devices, spread(): lax.ppermute(bias, 'row', [(i, turned(i, dx, dy)) for i in range(nr)])  19.6 us
    all_to_all x1, blocking collectives, per_device(): got = lax.all_to_all(both.reshape(nr, -1, CH), 'row', 0, 0, tiled=True)  18.9 us
    all_to_all x1, starting transfers between devices, per_device(): lax.all_to_all(message, 'col', 0, 0, tiled=True, axis_index_groups=same_c...  10.2 us
    ppermute x14, waiting for transfers between devices, spread(): lax.ppermute(bias, 'row', [(i, turned(i, dx, dy)) for i in range(nr)])  10.1 us
    pallas_call x2, Pallas kernels, prepare(): pl.pallas_call(prepare_kernel, grid=(nrow,), in_specs=[by_row(x), by_row(...  7.14 us
  transfers between devices with their start and end apart: 19, of which 7 were waited for; matrix products, arithmetic and copies ran while one was open for 1% of the time, Pallas kernels for 14%

profile of v2, /device:TPU:1, one launch (start us, length us, event | category | flops | bytes accessed | tf_op | source)
XLA Modules:
  0.0 199.7 jit_solution(3380524355867056171)
XLA Ops:
  0.0 1.5 convert_reduce_fusion.1
  1.6 1.8 fusion.7
  6.6 10.2 %all-to-all-start = ((bf16[16,224,128]{2,1,0:T(8,128)(2,1)}), bf16[16,224,128]{2,1,0:T(8,128)(2,1)S(1)}, u32[]{:S(2)}, u32[]{:S(2)}) async-start(bf16[16,224,128]{2,1,0:T(8,128)(2,1)} %maximum_maximum_fusion.1), calls=%async_computation | async-start | bytes 1835008 | tf_op jit(solution)/shard_map/all_to_all | solution.py:218
  16.8 22.1 %all-to-all-done = bf16[16,224,128]{2,1,0:T(8,128)(2,1)S(1)} async-done(((bf16[16,224,128]{2,1,0:T(8,128)(2,1)}), bf16[16,224,128]{2,1,0:T(8,128)(2,1)S(1)}, u32[]{:S(2)}, u32[]{:S(2)}) %all-to-all-start) | async-done | bytes 917536 | tf_op jit(solution)/shard_map/all_to_all | solution.py:218
  39.0 2.9 %collective-permute-start = (bf16[16,144,128]{2,1,0:T(8,128)(2,1)S(1)}, bf16[16,144,128]{2,1,0:T(8,128)(2,1)S(1)}, u32[]{:S(2)}, u32[]{:S(2)}) collective-permute-start(bf16[16,144,128]{2,1,0:T(8,128)(2,1)S(1)} %slice.111), channel_id=1, source_target_pairs={{0,1},{1,0},{2,3},{3,2},{4,5},{5,4},{6,7},{7,6},{8,9},{9,8},{10,11... | collective-permute-start | bytes 1769480 | tf_op jit(solution)/shard_map/ppermute | solution.py:220
  45.8 1.5 collective-permute-start.7
  47.4 2.5 %collective-permute-start.8 = (bf16[384,384]{1,0:T(8,128)(2,1)S(1)}, bf16[384,384]{1,0:T(8,128)(2,1)S(1)}, u32[]{:S(2)}, u32[]{:S(2)}) collective-permute-start(bf16[384,384]{1,0:T(8,128)(2,1)S(1)} %pad_maximum_fusion.2.refs_0_), channel_id=1, source_target_pairs={{0,128},{32,160},{64,192},{96,224},{128,0},{160,32},{192,64},{224,... | collective-permute-start | bytes 884744 | tf_op jit(solution)/shard_map/ppermute | solution.py:195
  49.8 1.6 collective-permute-start.2
  52.4 3.6 %prepare.2 = (bf16[6,128,768]{2,1,0:T(8,128)(2,1)S(1)}, bf16[6,768,128]{2,1,0:T(8,128)(2,1)S(1)}, bf16[6,384,128]{2,1,0:T(8,128)(2,1)S(1)}, f32[6,384,128]{2,1,0:T(8,128)S(1)}) custom-call(bf16[6,768,128]{2,1,0:T(8,128)(2,1)S(1)} %bitcast.76, bf16[6,384,128]{2,1,0:T(8,128)(2,1)S(1)} %slice.112.xq_ref, f32[1,128]{1,0:T(1,128)S(1)} %get-tuple-element.39.gain_ref, ...), custom_call_target="tpu_custom_call" | custom-call | flops 4000000000 | bytes 6291456 | tf_op jit(solution)/shard_map/prepare/pallas_call | solution.py:57
  56.0 4.5 %collective-permute-start.4 = (bf16[384,384]{1,0:T(8,128)(2,1)S(1)}, bf16[384,384]{1,0:T(8,128)(2,1)S(1)}, u32[]{:S(2)}, u32[]{:S(2)}) collective-permute-start(bf16[384,384]{1,0:T(8,128)(2,1)S(1)} %pad_maximum_fusion.2.refs_0_), channel_id=1, source_target_pairs={{0,224},{32,128},{64,160},{96,192},{128,96},{160,0},{192,32},{224,... | collective-permute-start | bytes 884744 | tf_op jit(solution)/shard_map/ppermute | solution.py:195
  61.0 9.8 %attend.4.refs_6_ = bf16[6,192,128]{2,1,0:T(8,128)(2,1)S(1)} custom-call(s32[4]{0:T(128)S(1)} %get-tuple-element.44.blk_ref.done_blk_ref, s32[1]{0:T(128)} %bitcast.4.done_blk_ref, bf16[6,128,768]{2,1,0:T(8,128)(2,1)S(1)} %get-tuple-element.13.kt_ref, bf16[6,768,128]{2,1,0:T(8,128)(2,1)S(1)} %get-tuple-element.14.v_ref, ...), custom_call_target="tpu_custom_call" | custom-call | flops 11200000000 | bytes 6291456 | tf_op jit(solution)/shard_map/attend/pallas_call | solution.py:137
  70.9 3.7 %collective-permute-done.5.refs_3_ = bf16[384,384]{1,0:T(8,128)(2,1)S(1)} collective-permute-done((bf16[384,384]{1,0:T(8,128)(2,1)S(1)}, bf16[384,384]{1,0:T(8,128)(2,1)S(1)}, u32[]{:S(2)}, u32[]{:S(2)}) %collective-permute-start.5) | collective-permute-done | bytes 294944 | tf_op jit(solution)/shard_map/ppermute | solution.py:195
  74.6 10.0 %attend.5 = bf16[6,384,128]{2,1,0:T(8,128)(2,1)S(1)} custom-call(s32[4]{0:T(128)S(1)} %get-tuple-element.43.blk_ref, s32[4]{0:T(128)S(1)} %get-tuple-element.44.blk_ref.done_blk_ref, bf16[6,128,768]{2,1,0:T(8,128)(2,1)S(1)} %get-tuple-element.13.kt_ref, bf16[6,768,128]{2,1,0:T(8,128)(2,1)S(1)} %get-tuple-element.14.v_ref, ...), custom_call_target="tpu_custom_call" | custom-call | flops 11200000000 | bytes 6291456 | tf_op jit(solution)/shard_map/attend/pallas_call | solution.py:137
  88.3 40.5 %all_to_all.15 = bf16[128,32,128]{2,1,0:T(8,128)(2,1)S(1)} all-to-all(bf16[128,32,128]{2,1,0:T(8,128)(2,1)S(1)} %copy.35), channel_id=1, replica_groups={{0,2,4,6,8,10,12,14,16,18,20,22,24,26,28,30,32,34,36,38,40,42,44,46,48,..., dimensions={0} | all-to-all | bytes 2097152 | tf_op jit(solution)/shard_map/all_to_all | solution.py:247
  129.4 4.0 %collective-permute-start.9 = (bf16[3,768,128]{2,1,0:T(8,128)(2,1)S(1)}, bf16[3,768,128]{2,1,0:T(8,128)(2,1)S(1)}, u32[]{:S(2)}, u32[]{:S(2)}) collective-permute-start(bf16[3,768,128]{2,1,0:T(8,128)(2,1)S(1)} %bitcast.86), channel_id=1, source_target_pairs={{0,1},{1,0},{2,3},{3,2},{4,5},{5,4},{6,7},{7,6},{8,9},{9,8},{10,11... | collective-permute-start | bytes 1769480 | tf_op jit(solution)/shard_map/ppermute | solution.py:251
  134.3 2.7 %collective-permute-start.15 = (bf16[384,384]{1,0:T(8,128)(2,1)S(1)}, bf16[384,384]{1,0:T(8,128)(2,1)S(1)}, u32[]{:S(2)}, u32[]{:S(2)}) collective-permute-start(bf16[384,384]{1,0:T(8,128)(2,1)S(1)} %pad_maximum_fusion.3.refs_0_), channel_id=1, source_target_pairs={{0,96},{32,0},{64,32},{96,64},{128,224},{160,128},{192,160},{224,1... | collective-permute-start | bytes 884744 | tf_op jit(solution)/shard_map/ppermute | solution.py:195
  137.3 2.9 %collective-permute-start.11 = (bf16[384,384]{1,0:T(8,128)(2,1)S(1)}, bf16[384,384]{1,0:T(8,128)(2,1)S(1)}, u32[]{:S(2)}, u32[]{:S(2)}) collective-permute-start(bf16[384,384]{1,0:T(8,128)(2,1)S(1)} %pad_maximum_fusion.3.refs_0_), channel_id=1, source_target_pairs={{0,160},{32,192},{64,224},{96,128},{128,32},{160,64},{192,96},{224... | collective-permute-start | bytes 884744 | tf_op jit(solution)/shard_map/ppermute | solution.py:195
  140.4 3.6 %prepare.3 = (bf16[6,128,768]{2,1,0:T(8,128)(2,1)S(1)}, bf16[6,768,128]{2,1,0:T(8,128)(2,1)S(1)}, bf16[6,384,128]{2,1,0:T(8,128)(2,1)S(1)}, f32[6,384,128]{2,1,0:T(8,128)S(1)}) custom-call(bf16[6,768,128]{2,1,0:T(8,128)(2,1)S(1)} %pad_maximum_fusion.x_ref, bf16[6,384,128]{2,1,0:T(8,128)(2,1)S(1)} %bitcast.77, f32[1,128]{1,0:T(1,128)S(1)} %get-tuple-element.42.gain_ref, ...), custom_call_target="tpu_custom_call" | custom-call | flops 4000000000 | bytes 6291456 | tf_op jit(solution)/shard_map/prepare/pallas_call | solution.py:57
  143.9 3.2 %collective-permute-done.14.refs_1_ = bf16[384,384]{1,0:T(8,128)(2,1)S(1)} collective-permute-done((bf16[384,384]{1,0:T(8,128)(2,1)S(1)}, bf16[384,384]{1,0:T(8,128)(2,1)S(1)}, u32[]{:S(2)}, u32[]{:S(2)}) %collective-permute-start.14) | collective-permute-done | bytes 294944 | tf_op jit(solution)/shard_map/ppermute | solution.py:195
  147.2 2.0 %collective-permute-done.15.refs_2_ = bf16[384,384]{1,0:T(8,128)(2,1)S(1)} collective-permute-done((bf16[384,384]{1,0:T(8,128)(2,1)S(1)}, bf16[384,384]{1,0:T(8,128)(2,1)S(1)}, u32[]{:S(2)}, u32[]{:S(2)}) %collective-permute-start.15) | collective-permute-done | bytes 294944 | tf_op jit(solution)/shard_map/ppermute | solution.py:195
  150.3 10.0 %attend.6.refs_6_ = bf16[6,192,128]{2,1,0:T(8,128)(2,1)S(1)} custom-call(s32[4]{0:T(128)S(1)} %get-tuple-element.44.blk_ref.done_blk_ref, s32[1]{0:T(128)} %bitcast.4.done_blk_ref, bf16[6,128,768]{2,1,0:T(8,128)(2,1)S(1)} %get-tuple-element.17.kt_ref, bf16[6,768,128]{2,1,0:T(8,128)(2,1)S(1)} %get-tuple-element.18.v_ref, ...), custom_call_target="tpu_custom_call" | custom-call | flops 11200000000 | bytes 6291456 | tf_op jit(solution)/shard_map/attend/pallas_call | solution.py:137
  161.5 10.0 %attend.7 = bf16[6,384,128]{2,1,0:T(8,128)(2,1)S(1)} custom-call(s32[4]{0:T(128)S(1)} %get-tuple-element.43.blk_ref, s32[4]{0:T(128)S(1)} %get-tuple-element.44.blk_ref.done_blk_ref, bf16[6,128,768]{2,1,0:T(8,128)(2,1)S(1)} %get-tuple-element.17.kt_ref, bf16[6,768,128]{2,1,0:T(8,128)(2,1)S(1)} %get-tuple-element.18.v_ref, ...), custom_call_target="tpu_custom_call" | custom-call | flops 11200000000 | bytes 6291456 | tf_op jit(solution)/shard_map/attend/pallas_call | solution.py:137
  171.5 6.8 %collective-permute-start.17 = (bf16[3,384,128]{2,1,0:T(8,128)(2,1)S(1)}, bf16[3,384,128]{2,1,0:T(8,128)(2,1)S(1)}, u32[]{:S(2)}, u32[]{:S(2)}) collective-permute-start(bf16[3,384,128]{2,1,0:T(8,128)(2,1)S(1)} %slice.122), channel_id=1, source_target_pairs={{0,1},{1,0},{2,3},{3,2},{4,5},{5,4},{6,7},{7,6},{8,9},{9,8},{10,11... | collective-permute-start | bytes 884744 | tf_op jit(solution)/shard_map/ppermute | solution.py:263
  179.7 18.9 %all_to_all.16 = bf16[8,288,128]{2,1,0:T(8,128)(2,1)S(1)} all-to-all(bf16[8,288,128]{2,1,0:T(8,128)(2,1)S(1)} %bitcast.82), channel_id=1, replica_groups=mesh['row'=8,'col'=32] {'row'}, dimensions={0} | all-to-all | bytes 1179648 | tf_op jit(solution)/shard_map/all_to_all | solution.py:266
  (94 shorter events, 18.9 us)
Async XLA Ops:
  0.0 3.4 %copy-start = (bf16[96,24,128]{2,1,0:T(8,128)(2,1)S(1)}, bf16[96,24,128]{2,1,0:T(8,128)(2,1)}, u32[]{:S(2)}) copy-start(bf16[96,24,128]{2,1,0:T(8,128)(2,1)} %param.7) | copy-start | bytes 1769476
  0.0 3.4 %copy-start.4 = (f32[2,128]{1,0:T(2,128)S(1)}, f32[2,128]{1,0:T(2,128)}, u32[]{:S(2)}) copy-start(f32[2,128]{1,0:T(2,128)} %param.8) | copy-start | bytes 3076
  0.0 3.4 %copy-start.6 = (bf16[2,128,4]{1,2,0:T(4,128)(2,1)S(1)}, bf16[2,128,4]{1,2,0:T(4,128)(2,1)}, u32[]{:S(2)}) copy-start(bf16[2,128,4]{1,2,0:T(4,128)(2,1)} %param.10) | copy-start | bytes 6148
  6.6 10.2 %copy-start.2 = (bf16[2,128,128]{2,1,0:T(8,128)(2,1)S(1)}, bf16[2,128,128]{2,1,0:T(8,128)(2,1)}, u32[]{:S(2)}) copy-start(bf16[2,128,128]{2,1,0:T(8,128)(2,1)} %param.12) | copy-start | bytes 196612
  6.6 10.2 %copy-start.1 = (bf16[2,128,512]{2,1,0:T(8,128)(2,1)S(1)}, bf16[2,128,512]{2,1,0:T(8,128)(2,1)}, u32[]{:S(2)}) copy-start(bf16[2,128,512]{2,1,0:T(8,128)(2,1)} %param.9) | copy-start | bytes 786436
  6.6 32.4 %all-to-all-start = ((bf16[16,224,128]{2,1,0:T(8,128)(2,1)}), bf16[16,224,128]{2,1,0:T(8,128)(2,1)S(1)}, u32[]{:S(2)}, u32[]{:S(2)}) async-start(bf16[16,224,128]{2,1,0:T(8,128)(2,1)} %maximum_maximum_fusion.1), calls=%async_computation | async-start | bytes 1835008 | tf_op jit(solution)/shard_map/all_to_all | solution.py:218
  39.0 12.4 %collective-permute-start = (bf16[16,144,128]{2,1,0:T(8,128)(2,1)S(1)}, bf16[16,144,128]{2,1,0:T(8,128)(2,1)S(1)}, u32[]{:S(2)}, u32[]{:S(2)}) collective-permute-start(bf16[16,144,128]{2,1,0:T(8,128)(2,1)S(1)} %slice.111), channel_id=1, source_target_pairs={{0,1},{1,0},{2,3},{3,2},{4,5},{5,4},{6,7},{7,6},{8,9},{9,8},{10,11... | collective-permute-start | bytes 1769480 | tf_op jit(solution)/shard_map/ppermute | solution.py:220
  42.8 1.5 collective-permute-start.1
  44.5 11.6 %collective-permute-start.6 = (bf16[384,384]{1,0:T(8,128)(2,1)S(1)}, bf16[384,384]{1,0:T(8,128)(2,1)S(1)}, u32[]{:S(2)}, u32[]{:S(2)}) collective-permute-start(bf16[384,384]{1,0:T(8,128)(2,1)S(1)} %pad_maximum_fusion.2.refs_0_), channel_id=1, source_target_pairs={{0,32},{32,64},{64,96},{96,0},{128,160},{160,192},{192,224},{224,1... | collective-permute-start | bytes 884744 | tf_op jit(solution)/shard_map/ppermute | solution.py:195
  45.8 14.7 %collective-permute-start.7 = (bf16[384,384]{1,0:T(8,128)(2,1)S(1)}, bf16[384,384]{1,0:T(8,128)(2,1)S(1)}, u32[]{:S(2)}, u32[]{:S(2)}) collective-permute-start(bf16[384,384]{1,0:T(8,128)(2,1)S(1)} %pad_maximum_fusion.2.refs_0_), channel_id=1, source_target_pairs={{0,96},{32,0},{64,32},{96,64},{128,224},{160,128},{192,160},{224,1... | collective-permute-start | bytes 884744 | tf_op jit(solution)/shard_map/ppermute | solution.py:195
  47.4 13.6 %collective-permute-start.8 = (bf16[384,384]{1,0:T(8,128)(2,1)S(1)}, bf16[384,384]{1,0:T(8,128)(2,1)S(1)}, u32[]{:S(2)}, u32[]{:S(2)}) collective-permute-start(bf16[384,384]{1,0:T(8,128)(2,1)S(1)} %pad_maximum_fusion.2.refs_0_), channel_id=1, source_target_pairs={{0,128},{32,160},{64,192},{96,224},{128,0},{160,32},{192,64},{224,... | collective-permute-start | bytes 884744 | tf_op jit(solution)/shard_map/ppermute | solution.py:195
  49.8 21.0 %collective-permute-start.2 = (bf16[384,384]{1,0:T(8,128)(2,1)S(1)}, bf16[384,384]{1,0:T(8,128)(2,1)S(1)}, u32[]{:S(2)}, u32[]{:S(2)}) collective-permute-start(bf16[384,384]{1,0:T(8,128)(2,1)S(1)} %pad_maximum_fusion.2.refs_0_), channel_id=1, source_target_pairs={{0,64},{32,96},{64,0},{96,32},{128,192},{160,224},{192,128},{224,1... | collective-permute-start | bytes 884744 | tf_op jit(solution)/shard_map/ppermute | solution.py:195
  51.4 19.5 %collective-permute-start.3 = (bf16[384,384]{1,0:T(8,128)(2,1)S(1)}, bf16[384,384]{1,0:T(8,128)(2,1)S(1)}, u32[]{:S(2)}, u32[]{:S(2)}) collective-permute-start(bf16[384,384]{1,0:T(8,128)(2,1)S(1)} %pad_maximum_fusion.2.refs_0_), channel_id=1, source_target_pairs={{0,160},{32,192},{64,224},{96,128},{128,32},{160,64},{192,96},{224... | collective-permute-start | bytes 884744 | tf_op jit(solution)/shard_map/ppermute | solution.py:195
  56.0 14.8 %collective-permute-start.4 = (bf16[384,384]{1,0:T(8,128)(2,1)S(1)}, bf16[384,384]{1,0:T(8,128)(2,1)S(1)}, u32[]{:S(2)}, u32[]{:S(2)}) collective-permute-start(bf16[384,384]{1,0:T(8,128)(2,1)S(1)} %pad_maximum_fusion.2.refs_0_), channel_id=1, source_target_pairs={{0,224},{32,128},{64,160},{96,192},{128,96},{160,0},{192,32},{224,... | collective-permute-start | bytes 884744 | tf_op jit(solution)/shard_map/ppermute | solution.py:195
  60.6 14.0 %collective-permute-start.5 = (bf16[384,384]{1,0:T(8,128)(2,1)S(1)}, bf16[384,384]{1,0:T(8,128)(2,1)S(1)}, u32[]{:S(2)}, u32[]{:S(2)}) collective-permute-start(bf16[384,384]{1,0:T(8,128)(2,1)S(1)} %pad_maximum_fusion.2.refs_0_), channel_id=1, source_target_pairs={{0,192},{32,224},{64,128},{96,160},{128,64},{160,96},{192,0},{224,... | collective-permute-start | bytes 884744 | tf_op jit(solution)/shard_map/ppermute | solution.py:195
  129.4 7.9 %collective-permute-start.9 = (bf16[3,768,128]{2,1,0:T(8,128)(2,1)S(1)}, bf16[3,768,128]{2,1,0:T(8,128)(2,1)S(1)}, u32[]{:S(2)}, u32[]{:S(2)}) collective-permute-start(bf16[3,768,128]{2,1,0:T(8,128)(2,1)S(1)} %bitcast.86), channel_id=1, source_target_pairs={{0,1},{1,0},{2,3},{3,2},{4,5},{5,4},{6,7},{7,6},{8,9},{9,8},{10,11... | collective-permute-start | bytes 1769480 | tf_op jit(solution)/shard_map/ppermute | solution.py:251
  134.2 13.0 %collective-permute-start.14 = (bf16[384,384]{1,0:T(8,128)(2,1)S(1)}, bf16[384,384]{1,0:T(8,128)(2,1)S(1)}, u32[]{:S(2)}, u32[]{:S(2)}) collective-permute-start(bf16[384,384]{1,0:T(8,128)(2,1)S(1)} %pad_maximum_fusion.3.refs_0_), channel_id=1, source_target_pairs={{0,32},{32,64},{64,96},{96,0},{128,160},{160,192},{192,224},{224,1... | collective-permute-start | bytes 884744 | tf_op jit(solution)/shard_map/ppermute | solution.py:195
  134.3 14.9 %collective-permute-start.15 = (bf16[384,384]{1,0:T(8,128)(2,1)S(1)}, bf16[384,384]{1,0:T(8,128)(2,1)S(1)}, u32[]{:S(2)}, u32[]{:S(2)}) collective-permute-start(bf16[384,384]{1,0:T(8,128)(2,1)S(1)} %pad_maximum_fusion.3.refs_0_), channel_id=1, source_target_pairs={{0,96},{32,0},{64,32},{96,64},{128,224},{160,128},{192,160},{224,1... | collective-permute-start | bytes 884744 | tf_op jit(solution)/shard_map/ppermute | solution.py:195
  136.9 13.4 %collective-permute-start.16 = (bf16[384,384]{1,0:T(8,128)(2,1)S(1)}, bf16[384,384]{1,0:T(8,128)(2,1)S(1)}, u32[]{:S(2)}, u32[]{:S(2)}) collective-permute-start(bf16[384,384]{1,0:T(8,128)(2,1)S(1)} %pad_maximum_fusion.3.refs_0_), channel_id=1, source_target_pairs={{0,128},{32,160},{64,192},{96,224},{128,0},{160,32},{192,64},{224,... | collective-permute-start | bytes 884744 | tf_op jit(solution)/shard_map/ppermute | solution.py:195
  137.1 23.2 %collective-permute-start.10 = (bf16[384,384]{1,0:T(8,128)(2,1)S(1)}, bf16[384,384]{1,0:T(8,128)(2,1)S(1)}, u32[]{:S(2)}, u32[]{:S(2)}) collective-permute-start(bf16[384,384]{1,0:T(8,128)(2,1)S(1)} %pad_maximum_fusion.3.refs_0_), channel_id=1, source_target_pairs={{0,64},{32,96},{64,0},{96,32},{128,192},{160,224},{192,128},{224,1... | collective-permute-start | bytes 884744 | tf_op jit(solution)/shard_map/ppermute | solution.py:195
  137.3 23.0 %collective-permute-start.11 = (bf16[384,384]{1,0:T(8,128)(2,1)S(1)}, bf16[384,384]{1,0:T(8,128)(2,1)S(1)}, u32[]{:S(2)}, u32[]{:S(2)}) collective-permute-start(bf16[384,384]{1,0:T(8,128)(2,1)S(1)} %pad_maximum_fusion.3.refs_0_), channel_id=1, source_target_pairs={{0,160},{32,192},{64,224},{96,128},{128,32},{160,64},{192,96},{224... | collective-permute-start | bytes 884744 | tf_op jit(solution)/shard_map/ppermute | solution.py:195
  147.2 13.1 %collective-permute-start.12 = (bf16[384,384]{1,0:T(8,128)(2,1)S(1)}, bf16[384,384]{1,0:T(8,128)(2,1)S(1)}, u32[]{:S(2)}, u32[]{:S(2)}) collective-permute-start(bf16[384,384]{1,0:T(8,128)(2,1)S(1)} %pad_maximum_fusion.3.refs_0_), channel_id=1, source_target_pairs={{0,224},{32,128},{64,160},{96,192},{128,96},{160,0},{192,32},{224,... | collective-permute-start | bytes 884744 | tf_op jit(solution)/shard_map/ppermute | solution.py:195
  149.2 12.3 %collective-permute-start.13 = (bf16[384,384]{1,0:T(8,128)(2,1)S(1)}, bf16[384,384]{1,0:T(8,128)(2,1)S(1)}, u32[]{:S(2)}, u32[]{:S(2)}) collective-permute-start(bf16[384,384]{1,0:T(8,128)(2,1)S(1)} %pad_maximum_fusion.3.refs_0_), channel_id=1, source_target_pairs={{0,192},{32,224},{64,128},{96,160},{128,64},{160,96},{192,0},{224,... | collective-permute-start | bytes 884744 | tf_op jit(solution)/shard_map/ppermute | solution.py:195
  171.5 8.0 %collective-permute-start.17 = (bf16[3,384,128]{2,1,0:T(8,128)(2,1)S(1)}, bf16[3,384,128]{2,1,0:T(8,128)(2,1)S(1)}, u32[]{:S(2)}, u32[]{:S(2)}) collective-permute-start(bf16[3,384,128]{2,1,0:T(8,128)(2,1)S(1)} %slice.122), channel_id=1, source_target_pairs={{0,1},{1,0},{2,3},{3,2},{4,5},{5,4},{6,7},{7,6},{8,9},{9,8},{10,11... | collective-permute-start | bytes 884744 | tf_op jit(solution)/shard_map/ppermute | solution.py:263
  (2 other events, 4.1 us)

commit v3 on v2

--- a/solution.py
+++ b/solution.py
@@ -11,7 +11,7 @@
 WIDTH = 32
 CH = 128
 LOG2E = 1.4426950408889634
-CALLS = (4, 4)
+CALLS = (3, 3, 2)
 NT = (((1,), (1,)), ((), ()))
 
 
@@ -28,6 +28,10 @@
 
 def by_row(a):
     return pl.BlockSpec((1,) + a.shape[1:], lambda i, *_: (i, 0, 0))
+
+
+def by_block(a):
+    return pl.BlockSpec((a.shape[0], 1) + a.shape[2:], lambda i, *_: (0, i, 0, 0))
 
 
 def prepare_kernel(x_ref, xq_ref, gain_ref, wp_ref, gb_ref, kt_ref, v_ref, q_ref, gate_ref):
@@ -115,16 +119,17 @@
     gated = (mixed * gate).astype(jnp.bfloat16)
     y = jnp.dot(gated, wo_ref[...], preferred_element_type=jnp.float32) + ob_ref[...]
     y = (xq.astype(jnp.float32) + y).astype(jnp.bfloat16)
-    if out_ref.shape[1] == nq:
-        out_ref[0] = y
+    if len(out_ref.shape) == 4:
+        for b in range(nblk):
+            out_ref[b, 0] = y[b * block : (b + 1) * block]
     else:
         for b in range(nblk):
             out_ref[0, pl.ds(starts[b], block), :] = y[b * block : (b + 1) * block]
         at = 0
         for ref in done_refs:
-            for b in range(ref.shape[1] // block):
+            for b in range(ref.shape[0]):
                 t = pl.multiple_of(done_blk_ref[at] * block, 16)
-                out_ref[0, pl.ds(t, block), :] = ref[0, b * block : (b + 1) * block, :]
+                out_ref[0, pl.ds(t, block), :] = ref[b, 0]
                 at += 1
 
 
@@ -132,7 +137,8 @@
     nrow, _, keys = parts[0].shape
     nblk = len(biases)
     nq = nblk * biases[0].shape[1] // 2 // HEADS
-    out = jax.ShapeDtypeStruct((nrow, xq.shape[1] if whole_out else nq, CH), jnp.bfloat16)
+    shape = xq.shape if whole_out else (nblk, nrow, nq // nblk, CH)
+    out = jax.ShapeDtypeStruct(shape, jnp.bfloat16)
     small = [wo, ob[None]]
     return pl.pallas_call(
         functools.partial(attention_kernel, nblk, len(done), stack),
@@ -142,8 +148,8 @@
             in_specs=[by_row(a) for a in parts]
             + [by_row(xq)]
             + [whole(a) for a in list(biases) + small]
-            + [by_row(a) for a in done],
-            out_specs=by_row(out),
+            + [by_block(a) for a in done],
+            out_specs=by_row(out) if whole_out else by_block(out),
             scratch_shapes=[pltpu.VMEM((HEADS * nq, keys), jnp.float32)],
         ),
         out_shape=out,
@@ -183,18 +189,25 @@
     same_core_col = [[2 * g + c for g in range(ng)] for c in range(2)]
     same_core_all = [[r * nc + 2 * g + c for r in range(nr) for g in range(ng)] for c in range(2)]
     swap_core = [(i, i ^ 1) for i in range(nc)]
-    turns = ((0, 1), (0, 3), (1, 0), (0, 2), (1, 1), (1, 3), (1, 2))
-
-    def turned(i, dx, dy):
-        return ((i // 4) ^ dx) * 4 + (i % 4 + dy) % 4
+    across = [
+        (r * nc + c, (r ^ (nr // 2)) * nc + (c ^ (nc // 2))) for r in range(nr) for c in range(nc)
+    ]
+    ny = nr // 2
+
+    def along_y(block, dy):
+        return lax.ppermute(
+            block, "row", [(i, i // ny * ny + (i + dy) % ny) for i in range(nr)]
+        )
 
     def spread(bias):
         me = lax.axis_index("row")
-        got, ids = [bias], [me]
-        for dx, dy in turns:
-            got.append(lax.ppermute(bias, "row", [(i, turned(i, dx, dy)) for i in range(nr)]))
-            ids.append(((me // 4) ^ dx) * 4 + (me % 4 - dy + 4) % 4)
-        return got, jnp.stack(ids).astype(jnp.int32)
+        ids = lambda dx, dy: ((me // ny) ^ dx) * ny + (me + ny - dy) % ny
+        over = lax.ppermute(bias, ("row", "col"), across)
+        got = [bias, along_y(bias, 1), along_y(bias, 3), over, along_y(bias, 2)]
+        got += [along_y(over, dy) for dy in (1, 3, 2)]
+        order = [ids(0, 0), ids(0, 1), ids(0, 3), ids(1, 0), ids(0, 2)]
+        order += [ids(1, dy) for dy in (1, 3, 2)]
+        return got, jnp.stack(order).astype(jnp.int32)
 
     def per_device(pair, norm_gain, w_proj, w_bias, gate_bias, w_out, out_bias):
         core = lax.axis_index("col") % 2

time: 203 us -> 205 us (level)
  waiting for transfers between devices: 34.6 us -> 49.2 us
  starting transfers between devices: 43.6 us -> 33.6 us
  blocking collectives: 59.4 us -> 49.9 us
  Pallas kernels: 46.9 us -> 55.6 us
    ppermute x14, waiting for transfers between devices: 10.1 us -> 24.7 us  [the longest x12 14.5 us: along_y(): lax.ppermute(block, 'row', [(i, i // ny * ny + (i + dy) % ny) for i in ra...]
    pallas_call x4 -> x6, Pallas kernels: 39.8 us -> 48.5 us  [attend(): pl.pallas_call(functools.partial(attention_kernel, nblk, len(done), stack...]
    all_to_all x1, blocking collectives: 40.5 us -> 35.3 us  [per_device(): lax.all_to_all(message, ('row', 'col'), 0, 0, tiled=True, axis_index_grou...]
    ppermute x1, starting transfers between devices: 6.8 us -> 1.76 us  [per_device(): other = lax.ppermute(last[part:], 'col', swap_core)]
    ppermute x14, starting transfers between devices: 19.6 us -> 14.6 us  [the longest x12 12.7 us: along_y(): lax.ppermute(block, 'row', [(i, i // ny * ny + (i + dy) % ny) for i in ra...]
    all_to_all x1, blocking collectives: 18.9 us -> 14.7 us  [per_device(): got = lax.all_to_all(both.reshape(nr, -1, CH), 'row', 0, 0, tiled=True)]
  transfers between devices with their start and end apart: 19 -> 19, of which waited for: 7 -> 8; matrix products, arithmetic and copies ran while one was open for 1% -> 1% of each run, Pallas kernels for 14% -> 20%
where the time goes in v3:
time: 205 us; the launch traced here: 204 us
  Pallas kernels  55.6 us (27%)
  blocking collectives  49.9 us (24%)
  waiting for transfers between devices  49.2 us (24%)
  starting transfers between devices  33.6 us (16%)
  other arithmetic  6.45 us (3%)
  local copies, waits for them, and re-layouts  5.85 us (3%)
  matrix products  2.43 us (1%)
    pallas_call x6, Pallas kernels, attend(): pl.pallas_call(functools.partial(attention_kernel, nblk, len(done), stack...  48.5 us
    all_to_all x1, blocking collectives, per_device(): lax.all_to_all(message, ('row', 'col'), 0, 0, tiled=True, axis_index_grou...  35.3 us
    all_to_all x1, waiting for transfers between devices, per_device(): lax.all_to_all(message, 'col', 0, 0, tiled=True, axis_index_groups=same_c...  22.2 us
    all_to_all x1, blocking collectives, per_device(): got = lax.all_to_all(both.reshape(nr, -1, CH), 'row', 0, 0, tiled=True)  14.7 us
    ppermute x12, waiting for transfers between devices, along_y(): lax.ppermute(block, 'row', [(i, i // ny * ny + (i + dy) % ny) for i in ra...  14.5 us
    ppermute x12, starting transfers between devices, along_y(): lax.ppermute(block, 'row', [(i, i // ny * ny + (i + dy) % ny) for i in ra...  12.7 us
    ppermute x2, waiting for transfers between devices, spread(): over = lax.ppermute(bias, ('row', 'col'), across)  10.2 us
    all_to_all x1, starting transfers between devices, per_device(): lax.all_to_all(message, 'col', 0, 0, tiled=True, axis_index_groups=same_c...  10.2 us
  transfers between devices with their start and end apart: 19, of which 8 were waited for; matrix products, arithmetic and copies ran while one was open for 1% of the time, Pallas kernels for 20%

profile of v3, /device:TPU:1, one launch (start us, length us, event | category | flops | bytes accessed | tf_op | source)
XLA Modules:
  0.0 203.6 jit_solution(6157197235220793227)
XLA Ops:
  1.5 1.8 fusion.7
  6.6 10.2 %all-to-all-start = ((bf16[16,224,128]{2,1,0:T(8,128)(2,1)}), bf16[16,224,128]{2,1,0:T(8,128)(2,1)S(1)}, u32[]{:S(2)}, u32[]{:S(2)}) async-start(bf16[16,224,128]{2,1,0:T(8,128)(2,1)} %maximum_maximum_fusion.1), calls=%async_computation | async-start | bytes 1835008 | tf_op jit(solution)/shard_map/all_to_all | solution.py:231
  16.8 22.2 %all-to-all-done = bf16[16,224,128]{2,1,0:T(8,128)(2,1)S(1)} async-done(((bf16[16,224,128]{2,1,0:T(8,128)(2,1)}), bf16[16,224,128]{2,1,0:T(8,128)(2,1)S(1)}, u32[]{:S(2)}, u32[]{:S(2)}) %all-to-all-start) | async-done | bytes 917536 | tf_op jit(solution)/shard_map/all_to_all | solution.py:231
  39.0 2.9 %collective-permute-start = (bf16[16,144,128]{2,1,0:T(8,128)(2,1)S(1)}, bf16[16,144,128]{2,1,0:T(8,128)(2,1)S(1)}, u32[]{:S(2)}, u32[]{:S(2)}) collective-permute-start(bf16[16,144,128]{2,1,0:T(8,128)(2,1)S(1)} %slice.117), channel_id=1, source_target_pairs={{0,1},{1,0},{2,3},{3,2},{4,5},{5,4},{6,7},{7,6},{8,9},{9,8},{10,11... | collective-permute-start | bytes 1769480 | tf_op jit(solution)/shard_map/ppermute | solution.py:233
  44.5 1.8 collective-permute-start.2
  49.3 1.6 collective-permute-start.7
  50.9 3.4 %collective-permute-done.2.refs_0_ = bf16[384,384]{1,0:T(8,128)(2,1)S(1)} collective-permute-done((bf16[384,384]{1,0:T(8,128)(2,1)S(1)}, bf16[384,384]{1,0:T(8,128)(2,1)S(1)}, u32[]{:S(2)}, u32[]{:S(2)}) %collective-permute-start.2) | collective-permute-done | bytes 294944 | tf_op jit(solution)/shard_map/ppermute | solution.py:205
  54.2 2.7 %collective-permute-start.3 = (bf16[384,384]{1,0:T(8,128)(2,1)S(1)}, bf16[384,384]{1,0:T(8,128)(2,1)S(1)}, u32[]{:S(2)}, u32[]{:S(2)}) collective-permute-start(bf16[384,384]{1,0:T(8,128)(2,1)S(1)} %collective-permute-done.2.refs_0_), channel_id=1, source_target_pairs={{0,96},{32,0},{64,32},{96,64},{128,224},{160,128},{192,160},{224,1... | collective-permute-start | bytes 884744 | tf_op jit(solution)/shard_map/ppermute | solution.py:198
  57.8 3.6 %prepare.2 = (bf16[6,128,768]{2,1,0:T(8,128)(2,1)S(1)}, bf16[6,768,128]{2,1,0:T(8,128)(2,1)S(1)}, bf16[6,384,128]{2,1,0:T(8,128)(2,1)S(1)}, f32[6,384,128]{2,1,0:T(8,128)S(1)}) custom-call(bf16[6,768,128]{2,1,0:T(8,128)(2,1)S(1)} %bitcast.76, bf16[6,384,128]{2,1,0:T(8,128)(2,1)S(1)} %slice.118.xq_ref, f32[1,128]{1,0:T(1,128)S(1)} %get-tuple-element.39.gain_ref, ...), custom_call_target="tpu_custom_call" | custom-call | flops 4000000000 | bytes 6291456 | tf_op jit(solution)/shard_map/prepare/pallas_call | solution.py:61
  62.3 8.4 %attend.6.refs_4_ = bf16[3,6,48,128]{3,2,1,0:T(8,128)(2,1)S(1)} custom-call(s32[3]{0:T(128)S(1)} %get-tuple-element.43.blk_ref.done_blk_ref, s32[1]{0:T(128)} %bitcast.2.done_blk_ref, bf16[6,128,768]{2,1,0:T(8,128)(2,1)S(1)} %get-tuple-element.13.kt_ref, bf16[6,768,128]{2,1,0:T(8,128)(2,1)S(1)} %get-tuple-element.14.v_ref, ...), custom_call_target="tpu_custom_call" | custom-call | flops 8400000000 | bytes 6291456 | tf_op jit(solution)/shard_map/attend/pallas_call | solution.py:143
  70.7 6.1 %collective-permute-done.8.refs_2_ = bf16[384,384]{1,0:T(8,128)(2,1)S(1)} collective-permute-done((bf16[384,384]{1,0:T(8,128)(2,1)S(1)}, bf16[384,384]{1,0:T(8,128)(2,1)S(1)}, u32[]{:S(2)}, u32[]{:S(2)}) %collective-permute-start.8) | collective-permute-done | bytes 294944 | tf_op jit(solution)/shard_map/ppermute | solution.py:198
  76.8 8.4 %attend.7.refs_5_ = bf16[3,6,48,128]{3,2,1,0:T(8,128)(2,1)S(1)} custom-call(s32[3]{0:T(128)S(1)} %get-tuple-element.44.blk_ref, s32[3]{0:T(128)S(1)} %get-tuple-element.43.blk_ref.done_blk_ref, bf16[6,128,768]{2,1,0:T(8,128)(2,1)S(1)} %get-tuple-element.13.kt_ref, bf16[6,768,128]{2,1,0:T(8,128)(2,1)S(1)} %get-tuple-element.14.v_ref, ...), custom_call_target="tpu_custom_call" | custom-call | flops 8400000000 | bytes 6291456 | tf_op jit(solution)/shard_map/attend/pallas_call | solution.py:143
  85.3 7.3 %attend.8 = bf16[6,384,128]{2,1,0:T(8,128)(2,1)S(1)} custom-call(s32[2]{0:T(128)S(1)} %pad_add_fusion.blk_ref, s32[6]{0:T(128)S(1)} %stack.69.done_blk_ref, bf16[6,128,768]{2,1,0:T(8,128)(2,1)S(1)} %get-tuple-element.13.kt_ref, bf16[6,768,128]{2,1,0:T(8,128)(2,1)S(1)} %get-tuple-element.14.v_ref, bf16[6,384,128]{2,1,0:T(8,128)(2,1)S(1)} %get-tuple-element.15.q_ref, ...), custom_call_target="tpu_custom_call" | custom-call | flops 5600000000 | bytes 6291456 | tf_op jit(solution)/shard_map/attend/pallas_call | solution.py:143
  96.3 35.3 %all_to_all.15 = bf16[128,32,128]{2,1,0:T(8,128)(2,1)S(1)} all-to-all(bf16[128,32,128]{2,1,0:T(8,128)(2,1)S(1)} %copy.35), channel_id=1, replica_groups={{0,2,4,6,8,10,12,14,16,18,20,22,24,26,28,30,32,34,36,38,40,42,44,46,48,..., dimensions={0} | all-to-all | bytes 2097152 | tf_op jit(solution)/shard_map/all_to_all | solution.py:260
  132.2 4.0 %collective-permute-start.9 = (bf16[3,768,128]{2,1,0:T(8,128)(2,1)S(1)}, bf16[3,768,128]{2,1,0:T(8,128)(2,1)S(1)}, u32[]{:S(2)}, u32[]{:S(2)}) collective-permute-start(bf16[3,768,128]{2,1,0:T(8,128)(2,1)S(1)} %bitcast.87), channel_id=1, source_target_pairs={{0,1},{1,0},{2,3},{3,2},{4,5},{5,4},{6,7},{7,6},{8,9},{9,8},{10,11... | collective-permute-start | bytes 1769480 | tf_op jit(solution)/shard_map/ppermute | solution.py:264
  137.4 2.7 %collective-permute-start.14 = (bf16[384,384]{1,0:T(8,128)(2,1)S(1)}, bf16[384,384]{1,0:T(8,128)(2,1)S(1)}, u32[]{:S(2)}, u32[]{:S(2)}) collective-permute-start(bf16[384,384]{1,0:T(8,128)(2,1)S(1)} %pad_maximum_fusion.3.refs_0_), channel_id=1, source_target_pairs={{0,96},{32,0},{64,32},{96,64},{128,224},{160,128},{192,160},{224,1... | collective-permute-start | bytes 884744 | tf_op jit(solution)/shard_map/ppermute | solution.py:198
  140.1 6.8 %collective-permute-done.10.refs_0_ = bf16[384,384]{1,0:T(8,128)(2,1)S(1)} collective-permute-done((bf16[384,384]{1,0:T(8,128)(2,1)S(1)}, bf16[384,384]{1,0:T(8,128)(2,1)S(1)}, u32[]{:S(2)}, u32[]{:S(2)}) %collective-permute-start.10) | collective-permute-done | bytes 294944 | tf_op jit(solution)/shard_map/ppermute | solution.py:205
  148.3 3.6 %prepare.3 = (bf16[6,128,768]{2,1,0:T(8,128)(2,1)S(1)}, bf16[6,768,128]{2,1,0:T(8,128)(2,1)S(1)}, bf16[6,384,128]{2,1,0:T(8,128)(2,1)S(1)}, f32[6,384,128]{2,1,0:T(8,128)S(1)}) custom-call(bf16[6,768,128]{2,1,0:T(8,128)(2,1)S(1)} %pad_maximum_fusion.x_ref, bf16[6,384,128]{2,1,0:T(8,128)(2,1)S(1)} %bitcast.77, f32[1,128]{1,0:T(1,128)S(1)} %get-tuple-element.42.gain_ref, ...), custom_call_target="tpu_custom_call" | custom-call | flops 4000000000 | bytes 6291456 | tf_op jit(solution)/shard_map/prepare/pallas_call | solution.py:61
  151.9 8.0 %collective-permute-done.13.refs_1_ = bf16[384,384]{1,0:T(8,128)(2,1)S(1)} collective-permute-done((bf16[384,384]{1,0:T(8,128)(2,1)S(1)}, bf16[384,384]{1,0:T(8,128)(2,1)S(1)}, u32[]{:S(2)}, u32[]{:S(2)}) %collective-permute-start.13) | collective-permute-done | bytes 294944 | tf_op jit(solution)/shard_map/ppermute | solution.py:198
  159.9 8.5 %attend.9.refs_4_ = bf16[3,6,48,128]{3,2,1,0:T(8,128)(2,1)S(1)} custom-call(s32[3]{0:T(128)S(1)} %get-tuple-element.43.blk_ref.done_blk_ref, s32[1]{0:T(128)} %bitcast.2.done_blk_ref, bf16[6,128,768]{2,1,0:T(8,128)(2,1)S(1)} %get-tuple-element.17.kt_ref, bf16[6,768,128]{2,1,0:T(8,128)(2,1)S(1)} %get-tuple-element.18.v_ref, ...), custom_call_target="tpu_custom_call" | custom-call | flops 8400000000 | bytes 6291456 | tf_op jit(solution)/shard_map/attend/pallas_call | solution.py:143
  168.8 8.5 %attend.10.refs_5_ = bf16[3,6,48,128]{3,2,1,0:T(8,128)(2,1)S(1)} custom-call(s32[3]{0:T(128)S(1)} %get-tuple-element.44.blk_ref, s32[3]{0:T(128)S(1)} %get-tuple-element.43.blk_ref.done_blk_ref, bf16[6,128,768]{2,1,0:T(8,128)(2,1)S(1)} %get-tuple-element.17.kt_ref, bf16[6,768,128]{2,1,0:T(8,128)(2,1)S(1)} %get-tuple-element.18.v_ref, ...), custom_call_target="tpu_custom_call" | custom-call | flops 8400000000 | bytes 6291456 | tf_op jit(solution)/shard_map/attend/pallas_call | solution.py:143
  177.4 7.3 %attend.11 = bf16[6,384,128]{2,1,0:T(8,128)(2,1)S(1)} custom-call(s32[2]{0:T(128)S(1)} %pad_add_fusion.blk_ref, s32[6]{0:T(128)S(1)} %stack.69.done_blk_ref, bf16[6,128,768]{2,1,0:T(8,128)(2,1)S(1)} %get-tuple-element.17.kt_ref, bf16[6,768,128]{2,1,0:T(8,128)(2,1)S(1)} %get-tuple-element.18.v_ref, bf16[6,384,128]{2,1,0:T(8,128)(2,1)S(1)} %get-tuple-element.19.q_ref, ...), custom_call_target="tpu_custom_call" | custom-call | flops 5600000000 | bytes 6291456 | tf_op jit(solution)/shard_map/attend/pallas_call | solution.py:143
  184.7 1.8 collective-permute-start.17
  187.9 14.7 %all_to_all.16 = bf16[8,288,128]{2,1,0:T(8,128)(2,1)S(1)} all-to-all(bf16[8,288,128]{2,1,0:T(8,128)(2,1)S(1)} %bitcast.83), channel_id=1, replica_groups=mesh['row'=8,'col'=32] {'row'}, dimensions={0} | all-to-all | bytes 1179648 | tf_op jit(solution)/shard_map/all_to_all | solution.py:279
  (98 shorter events, 21.6 us)
Async XLA Ops:
  0.0 3.4 %copy-start = (bf16[96,24,128]{2,1,0:T(8,128)(2,1)S(1)}, bf16[96,24,128]{2,1,0:T(8,128)(2,1)}, u32[]{:S(2)}) copy-start(bf16[96,24,128]{2,1,0:T(8,128)(2,1)} %param.7) | copy-start | bytes 1769476
  0.0 3.3 %copy-start.4 = (f32[2,128]{1,0:T(2,128)S(1)}, f32[2,128]{1,0:T(2,128)}, u32[]{:S(2)}) copy-start(f32[2,128]{1,0:T(2,128)} %param.8) | copy-start | bytes 3076
  0.0 3.4 %copy-start.6 = (bf16[2,128,4]{1,2,0:T(4,128)(2,1)S(1)}, bf16[2,128,4]{1,2,0:T(4,128)(2,1)}, u32[]{:S(2)}) copy-start(bf16[2,128,4]{1,2,0:T(4,128)(2,1)} %param.10) | copy-start | bytes 6148
  6.6 10.2 %copy-start.2 = (bf16[2,128,128]{2,1,0:T(8,128)(2,1)S(1)}, bf16[2,128,128]{2,1,0:T(8,128)(2,1)}, u32[]{:S(2)}) copy-start(bf16[2,128,128]{2,1,0:T(8,128)(2,1)} %param.12) | copy-start | bytes 196612
  6.6 32.4 %all-to-all-start = ((bf16[16,224,128]{2,1,0:T(8,128)(2,1)}), bf16[16,224,128]{2,1,0:T(8,128)(2,1)S(1)}, u32[]{:S(2)}, u32[]{:S(2)}) async-start(bf16[16,224,128]{2,1,0:T(8,128)(2,1)} %maximum_maximum_fusion.1), calls=%async_computation | async-start | bytes 1835008 | tf_op jit(solution)/shard_map/all_to_all | solution.py:231
  39.0 18.0 %collective-permute-start = (bf16[16,144,128]{2,1,0:T(8,128)(2,1)S(1)}, bf16[16,144,128]{2,1,0:T(8,128)(2,1)S(1)}, u32[]{:S(2)}, u32[]{:S(2)}) collective-permute-start(bf16[16,144,128]{2,1,0:T(8,128)(2,1)S(1)} %slice.117), channel_id=1, source_target_pairs={{0,1},{1,0},{2,3},{3,2},{4,5},{5,4},{6,7},{7,6},{8,9},{9,8},{10,11... | collective-permute-start | bytes 1769480 | tf_op jit(solution)/shard_map/ppermute | solution.py:233
  42.8 3.6 %copy-start.1 = (bf16[2,128,512]{2,1,0:T(8,128)(2,1)S(1)}, bf16[2,128,512]{2,1,0:T(8,128)(2,1)}, u32[]{:S(2)}) copy-start(bf16[2,128,512]{2,1,0:T(8,128)(2,1)} %param.9) | copy-start | bytes 786436
  42.8 1.5 collective-permute-start.1
  44.5 9.8 %collective-permute-start.2 = (bf16[384,384]{1,0:T(8,128)(2,1)S(1)}, bf16[384,384]{1,0:T(8,128)(2,1)S(1)}, u32[]{:S(2)}, u32[]{:S(2)}) collective-permute-start(bf16[384,384]{1,0:T(8,128)(2,1)S(1)} %pad_maximum_fusion.2.refs_0_), channel_id=1, source_target_pairs={{0,144},{1,145},{2,146},{3,147},{4,148},{5,149},{6,150},{7,151},{8... | collective-permute-start | bytes 884744 | tf_op jit(solution)/shard_map/ppermute | solution.py:205
  46.4 14.9 %collective-permute-start.5 = (bf16[384,384]{1,0:T(8,128)(2,1)S(1)}, bf16[384,384]{1,0:T(8,128)(2,1)S(1)}, u32[]{:S(2)}, u32[]{:S(2)}) collective-permute-start(bf16[384,384]{1,0:T(8,128)(2,1)S(1)} %pad_maximum_fusion.2.refs_0_), channel_id=1, source_target_pairs={{0,32},{32,64},{64,96},{96,0},{128,160},{160,192},{192,224},{224,1... | collective-permute-start | bytes 884744 | tf_op jit(solution)/shard_map/ppermute | solution.py:198
  47.8 14.5 %collective-permute-start.6 = (bf16[384,384]{1,0:T(8,128)(2,1)S(1)}, bf16[384,384]{1,0:T(8,128)(2,1)S(1)}, u32[]{:S(2)}, u32[]{:S(2)}) collective-permute-start(bf16[384,384]{1,0:T(8,128)(2,1)S(1)} %pad_maximum_fusion.2.refs_0_), channel_id=1, source_target_pairs={{0,96},{32,0},{64,32},{96,64},{128,224},{160,128},{192,160},{224,1... | collective-permute-start | bytes 884744 | tf_op jit(solution)/shard_map/ppermute | solution.py:198
  49.3 21.4 %collective-permute-start.7 = (bf16[384,384]{1,0:T(8,128)(2,1)S(1)}, bf16[384,384]{1,0:T(8,128)(2,1)S(1)}, u32[]{:S(2)}, u32[]{:S(2)}) collective-permute-start(bf16[384,384]{1,0:T(8,128)(2,1)S(1)} %pad_maximum_fusion.2.refs_0_), channel_id=1, source_target_pairs={{0,64},{32,96},{64,0},{96,32},{128,192},{160,224},{192,128},{224,1... | collective-permute-start | bytes 884744 | tf_op jit(solution)/shard_map/ppermute | solution.py:198
  54.2 31.0 %collective-permute-start.3 = (bf16[384,384]{1,0:T(8,128)(2,1)S(1)}, bf16[384,384]{1,0:T(8,128)(2,1)S(1)}, u32[]{:S(2)}, u32[]{:S(2)}) collective-permute-start(bf16[384,384]{1,0:T(8,128)(2,1)S(1)} %collective-permute-done.2.refs_0_), channel_id=1, source_target_pairs={{0,96},{32,0},{64,32},{96,64},{128,224},{160,128},{192,160},{224,1... | collective-permute-start | bytes 884744 | tf_op jit(solution)/shard_map/ppermute | solution.py:198
  57.0 28.3 %collective-permute-start.4 = (bf16[384,384]{1,0:T(8,128)(2,1)S(1)}, bf16[384,384]{1,0:T(8,128)(2,1)S(1)}, u32[]{:S(2)}, u32[]{:S(2)}) collective-permute-start(bf16[384,384]{1,0:T(8,128)(2,1)S(1)} %collective-permute-done.2.refs_0_), channel_id=1, source_target_pairs={{0,64},{32,96},{64,0},{96,32},{128,192},{160,224},{192,128},{224,1... | collective-permute-start | bytes 884744 | tf_op jit(solution)/shard_map/ppermute | solution.py:198
  61.4 15.5 %collective-permute-start.8 = (bf16[384,384]{1,0:T(8,128)(2,1)S(1)}, bf16[384,384]{1,0:T(8,128)(2,1)S(1)}, u32[]{:S(2)}, u32[]{:S(2)}) collective-permute-start(bf16[384,384]{1,0:T(8,128)(2,1)S(1)} %collective-permute-done.2.refs_0_), channel_id=1, source_target_pairs={{0,32},{32,64},{64,96},{96,0},{128,160},{160,192},{192,224},{224,1... | collective-permute-start | bytes 884744 | tf_op jit(solution)/shard_map/ppermute | solution.py:198
  132.2 14.9 %collective-permute-start.9 = (bf16[3,768,128]{2,1,0:T(8,128)(2,1)S(1)}, bf16[3,768,128]{2,1,0:T(8,128)(2,1)S(1)}, u32[]{:S(2)}, u32[]{:S(2)}) collective-permute-start(bf16[3,768,128]{2,1,0:T(8,128)(2,1)S(1)} %bitcast.87), channel_id=1, source_target_pairs={{0,1},{1,0},{2,3},{3,2},{4,5},{5,4},{6,7},{7,6},{8,9},{9,8},{10,11... | collective-permute-start | bytes 1769480 | tf_op jit(solution)/shard_map/ppermute | solution.py:264
  137.0 9.9 %collective-permute-start.10 = (bf16[384,384]{1,0:T(8,128)(2,1)S(1)}, bf16[384,384]{1,0:T(8,128)(2,1)S(1)}, u32[]{:S(2)}, u32[]{:S(2)}) collective-permute-start(bf16[384,384]{1,0:T(8,128)(2,1)S(1)} %pad_maximum_fusion.3.refs_0_), channel_id=1, source_target_pairs={{0,144},{1,145},{2,146},{3,147},{4,148},{5,149},{6,150},{7,151},{8... | collective-permute-start | bytes 884744 | tf_op jit(solution)/shard_map/ppermute | solution.py:205
  137.1 22.8 %collective-permute-start.13 = (bf16[384,384]{1,0:T(8,128)(2,1)S(1)}, bf16[384,384]{1,0:T(8,128)(2,1)S(1)}, u32[]{:S(2)}, u32[]{:S(2)}) collective-permute-start(bf16[384,384]{1,0:T(8,128)(2,1)S(1)} %pad_maximum_fusion.3.refs_0_), channel_id=1, source_target_pairs={{0,32},{32,64},{64,96},{96,0},{128,160},{160,192},{192,224},{224,1... | collective-permute-start | bytes 884744 | tf_op jit(solution)/shard_map/ppermute | solution.py:198
  137.4 22.5 %collective-permute-start.14 = (bf16[384,384]{1,0:T(8,128)(2,1)S(1)}, bf16[384,384]{1,0:T(8,128)(2,1)S(1)}, u32[]{:S(2)}, u32[]{:S(2)}) collective-permute-start(bf16[384,384]{1,0:T(8,128)(2,1)S(1)} %pad_maximum_fusion.3.refs_0_), channel_id=1, source_target_pairs={{0,96},{32,0},{64,32},{96,64},{128,224},{160,128},{192,160},{224,1... | collective-permute-start | bytes 884744 | tf_op jit(solution)/shard_map/ppermute | solution.py:198
  140.1 28.3 %collective-permute-start.15 = (bf16[384,384]{1,0:T(8,128)(2,1)S(1)}, bf16[384,384]{1,0:T(8,128)(2,1)S(1)}, u32[]{:S(2)}, u32[]{:S(2)}) collective-permute-start(bf16[384,384]{1,0:T(8,128)(2,1)S(1)} %pad_maximum_fusion.3.refs_0_), channel_id=1, source_target_pairs={{0,64},{32,96},{64,0},{96,32},{128,192},{160,224},{192,128},{224,1... | collective-permute-start | bytes 884744 | tf_op jit(solution)/shard_map/ppermute | solution.py:198
  146.9 30.4 %collective-permute-start.11 = (bf16[384,384]{1,0:T(8,128)(2,1)S(1)}, bf16[384,384]{1,0:T(8,128)(2,1)S(1)}, u32[]{:S(2)}, u32[]{:S(2)}) collective-permute-start(bf16[384,384]{1,0:T(8,128)(2,1)S(1)} %collective-permute-done.10.refs_0_), channel_id=1, source_target_pairs={{0,96},{32,0},{64,32},{96,64},{128,224},{160,128},{192,160},{224,1... | collective-permute-start | bytes 884744 | tf_op jit(solution)/shard_map/ppermute | solution.py:198
  147.2 30.2 %collective-permute-start.12 = (bf16[384,384]{1,0:T(8,128)(2,1)S(1)}, bf16[384,384]{1,0:T(8,128)(2,1)S(1)}, u32[]{:S(2)}, u32[]{:S(2)}) collective-permute-start(bf16[384,384]{1,0:T(8,128)(2,1)S(1)} %collective-permute-done.10.refs_0_), channel_id=1, source_target_pairs={{0,64},{32,96},{64,0},{96,32},{128,192},{160,224},{192,128},{224,1... | collective-permute-start | bytes 884744 | tf_op jit(solution)/shard_map/ppermute | solution.py:198
  159.9 8.9 %collective-permute-start.16 = (bf16[384,384]{1,0:T(8,128)(2,1)S(1)}, bf16[384,384]{1,0:T(8,128)(2,1)S(1)}, u32[]{:S(2)}, u32[]{:S(2)}) collective-permute-start(bf16[384,384]{1,0:T(8,128)(2,1)S(1)} %collective-permute-done.10.refs_0_), channel_id=1, source_target_pairs={{0,32},{32,64},{64,96},{96,0},{128,160},{160,192},{192,224},{224,1... | collective-permute-start | bytes 884744 | tf_op jit(solution)/shard_map/ppermute | solution.py:198
  184.7 3.0 %collective-permute-start.17 = (bf16[3,384,128]{2,1,0:T(8,128)(2,1)S(1)}, bf16[3,384,128]{2,1,0:T(8,128)(2,1)S(1)}, u32[]{:S(2)}, u32[]{:S(2)}) collective-permute-start(bf16[3,384,128]{2,1,0:T(8,128)(2,1)S(1)} %slice.128), channel_id=1, source_target_pairs={{0,1},{1,0},{2,3},{3,2},{4,5},{5,4},{6,7},{7,6},{8,9},{9,8},{10,11... | collective-permute-start | bytes 884744 | tf_op jit(solution)/shard_map/ppermute | solution.py:276
  (2 other events, 4.1 us)

commit v4 on v3

--- a/solution.py
+++ b/solution.py
@@ -11,7 +11,7 @@
 WIDTH = 32
 CH = 128
 LOG2E = 1.4426950408889634
-CALLS = (3, 3, 2)
+CALLS = (4, 2, 2)
 NT = (((1,), (1,)), ((), ()))
 
 
@@ -30,8 +30,12 @@
     return pl.BlockSpec((1,) + a.shape[1:], lambda i, *_: (i, 0, 0))
 
 
+def by_pair(a):
+    return pl.BlockSpec((2,) + a.shape[1:], lambda i, *_: (i, 0, 0))
+
+
 def by_block(a):
-    return pl.BlockSpec((a.shape[0], 1) + a.shape[2:], lambda i, *_: (0, i, 0, 0))
+    return pl.BlockSpec((a.shape[0], 2) + a.shape[2:], lambda i, *_: (0, i, 0, 0))
 
 
 def prepare_kernel(x_ref, xq_ref, gain_ref, wp_ref, gb_ref, kt_ref, v_ref, q_ref, gate_ref):
@@ -72,11 +76,12 @@
     )(x, xq, *small)
 
 
-def attention_kernel(nblk, ndone, stack, blk_ref, done_blk_ref, kt_ref, v_ref, q_ref, gate_ref, xq_ref, *refs):
+def attention_kernel(nblk, ndone, stack, nnext, blk_ref, done_blk_ref, kt_ref, v_ref, q_ref, gate_ref, xq_ref, *refs):
     bias_refs = refs[:nblk]
     wo_ref, ob_ref = refs[nblk : nblk + 2]
     done_refs = refs[nblk + 2 : nblk + 2 + ndone]
-    out_ref, biasf = refs[nblk + 2 + ndone :]
+    next_refs = refs[nblk + 2 + ndone : nblk + 2 + ndone + nnext]
+    out_ref, *next_out, biasf = refs[nblk + 2 + ndone + nnext :]
     half = bias_refs[0].shape[0]
     rows = bias_refs[0].shape[1] // 2
     block = rows // HEADS
@@ -84,72 +89,92 @@
 
     @pl.when(pl.program_id(0) == 0)
     def _():
-        at = lax.broadcasted_iota(jnp.int32, (rows, 2 * rows), 0)
-        to = lax.broadcasted_iota(jnp.int32, (rows, 2 * rows), 1)
-        for s in range(2):
-            pick = (to == at + s * rows).astype(jnp.bfloat16)
-            for b in range(nblk):
-                part = lax.dot_general(
-                    pick, bias_refs[b][...], NT, preferred_element_type=jnp.float32
-                )
+        for b in range(nblk):
+            part = bias_refs[b][...].astype(jnp.float32).T * LOG2E
+            for s in range(2):
                 for h in range(HEADS):
-                    biasf[
-                        pl.ds(h * nq + b * block, block), pl.ds(s * half, half)
-                    ] = part[h * block : (h + 1) * block] * LOG2E
-
-    kt = kt_ref[0]
-    v = v_ref[0]
+                    at = s * rows + h * block
+                    biasf[pl.ds(h * nq + b * block, block), pl.ds(s * half, half)] = part[
+                        at : at + block
+                    ]
+
+    pair = range(2)
+    kt = jnp.concatenate([kt_ref[u] for u in pair], axis=0)
+    v = jnp.concatenate([v_ref[u] for u in pair], axis=1)
     starts = [pl.multiple_of(blk_ref[b] * block, 16) for b in range(nblk)]
-    q = jnp.concatenate([q_ref[0, pl.ds(t, block), :] for t in starts], axis=0)
-    head_of = lax.broadcasted_iota(jnp.int32, q.shape, 1) // WIDTH
-    mixed = jnp.zeros(q.shape, jnp.float32)
+
+    def picked(ref, u):
+        return jnp.concatenate([ref[u, pl.ds(t, block), :] for t in starts], axis=0)
+
+    q = [picked(q_ref, u) for u in pair]
+    head_of = lax.broadcasted_iota(jnp.int32, q[0].shape, 1) // WIDTH
+    zero = jnp.zeros_like(q[0])
+    mixed = [jnp.zeros(q[0].shape, jnp.float32) for _ in pair]
     for h0 in range(0, HEADS, stack):
+        heads = range(h0, h0 + stack)
+        here = [jnp.where(head_of == h, q[0], zero) for h in heads]
+        there = [jnp.where(head_of == h, q[1], zero) for h in heads]
         qh = jnp.concatenate(
-            [jnp.where(head_of == h, q, jnp.zeros_like(q)) for h in range(h0, h0 + stack)], axis=0
+            [jnp.concatenate([t, zero], axis=1) for t in here]
+            + [jnp.concatenate([zero, t], axis=1) for t in there],
+            axis=0,
         )
         s = jnp.dot(qh, kt, preferred_element_type=jnp.float32)
-        s = s * (WIDTH**-0.5 * LOG2E) + biasf[h0 * nq : (h0 + stack) * nq]
+        bias = biasf[h0 * nq : (h0 + stack) * nq]
+        s = s * (WIDTH**-0.5 * LOG2E) + jnp.concatenate([bias, bias], axis=0)
         e = jnp.exp2(s - jnp.max(s, axis=-1, keepdims=True))
         p = (e * (1.0 / jnp.sum(e, axis=-1, keepdims=True))).astype(jnp.bfloat16)
         o = jnp.dot(p, v, preferred_element_type=jnp.float32)
-        for t in range(stack):
-            mixed = jnp.where(head_of == h0 + t, o[t * nq : (t + 1) * nq], mixed)
-    gate = jnp.concatenate([gate_ref[0, pl.ds(t, block), :] for t in starts], axis=0)
-    xq = jnp.concatenate([xq_ref[0, pl.ds(t, block), :] for t in starts], axis=0)
-    gated = (mixed * gate).astype(jnp.bfloat16)
-    y = jnp.dot(gated, wo_ref[...], preferred_element_type=jnp.float32) + ob_ref[...]
-    y = (xq.astype(jnp.float32) + y).astype(jnp.bfloat16)
-    if len(out_ref.shape) == 4:
+        for u in pair:
+            for n, h in enumerate(heads):
+                at = (u * stack + n) * nq
+                part = o[at : at + nq, u * CH : (u + 1) * CH]
+                mixed[u] = jnp.where(head_of == h, part, mixed[u])
+    for u in pair:
+        gated = (mixed[u] * picked(gate_ref, u)).astype(jnp.bfloat16)
+        y = jnp.dot(gated, wo_ref[...], preferred_element_type=jnp.float32) + ob_ref[...]
+        y = (picked(xq_ref, u).astype(jnp.float32) + y).astype(jnp.bfloat16)
         for b in range(nblk):
-            out_ref[b, 0] = y[b * block : (b + 1) * block]
-    else:
-        for b in range(nblk):
-            out_ref[0, pl.ds(starts[b], block), :] = y[b * block : (b + 1) * block]
+            part = y[b * block : (b + 1) * block]
+            if len(out_ref.shape) == 4:
+                out_ref[b, u] = part
+            else:
+                out_ref[u, pl.ds(starts[b], block), :] = part
         at = 0
         for ref in done_refs:
             for b in range(ref.shape[0]):
                 t = pl.multiple_of(done_blk_ref[at] * block, 16)
-                out_ref[0, pl.ds(t, block), :] = ref[b, 0]
+                out_ref[u, pl.ds(t, block), :] = ref[b, u]
                 at += 1
-
-
-def attend(ids, parts, xq, biases, wo, ob, done_ids, done, whole_out, stack):
+        if nnext:
+            normed = normalize(out_ref[u], next_refs[0][...])
+            next_out[0][u] = lax.dot_general(
+                next_refs[1][...], normed, NT, preferred_element_type=jnp.float32
+            ).astype(jnp.bfloat16)
+
+
+def attend(ids, parts, xq, biases, wo, ob, done_ids, done, whole_out, stack, following):
     nrow, _, keys = parts[0].shape
     nblk = len(biases)
     nq = nblk * biases[0].shape[1] // 2 // HEADS
     shape = xq.shape if whole_out else (nblk, nrow, nq // nblk, CH)
-    out = jax.ShapeDtypeStruct(shape, jnp.bfloat16)
+    out = [jax.ShapeDtypeStruct(shape, jnp.bfloat16)]
+    out_specs = [by_pair(out[0]) if whole_out else by_block(out[0])]
+    if following:
+        out.append(jax.ShapeDtypeStruct((nrow, 8, xq.shape[1]), jnp.bfloat16))
+        out_specs.append(by_pair(out[1]))
     small = [wo, ob[None]]
     return pl.pallas_call(
-        functools.partial(attention_kernel, nblk, len(done), stack),
+        functools.partial(attention_kernel, nblk, len(done), stack, len(following)),
         grid_spec=pltpu.PrefetchScalarGridSpec(
             num_scalar_prefetch=2,
-            grid=(nrow,),
-            in_specs=[by_row(a) for a in parts]
-            + [by_row(xq)]
+            grid=(nrow // 2,),
+            in_specs=[by_pair(a) for a in parts]
+            + [by_pair(xq)]
             + [whole(a) for a in list(biases) + small]
-            + [by_block(a) for a in done],
-            out_specs=by_row(out) if whole_out else by_block(out),
+            + [by_block(a) for a in done]
+            + [whole(a) for a in following],
+            out_specs=out_specs,
             scratch_shapes=[pltpu.VMEM((HEADS * nq, keys), jnp.float32)],
         ),
         out_shape=out,
@@ -158,15 +183,15 @@
             flops=nblk * 28 * 10**8, bytes_accessed=6 << 20, transcendentals=nrow * HEADS * nq * keys
         ),
         name="attend",
-    )(ids, done_ids, *parts, xq, *biases, *small, *done)
-
-
-def attention(ids, x, xq, biases, gain, wp, gb, wo, ob):
+    )(ids, done_ids, *parts, xq, *biases, *small, *done, *following)
+
+
+def attention(ids, x, xq, biases, gain, wp, gb, wo, ob, following):
     parts = prepare(x, xq, gain, wp, gb)
     done, at = [], 0
     for n in CALLS:
         last = at + n == len(biases)
-        y = attend(
+        out = attend(
             ids[at : at + n],
             parts,
             xq,
@@ -176,11 +201,12 @@
             ids[: max(at, 1)],
             done if last else [],
             last,
-            min(HEADS, max(1, 8 // n)),
-        )
-        done.append(y)
+            1 if n > 2 else 2,
+            following if last else [],
+        )
+        done.append(out[0])
         at += n
-    return done[-1]
+    return out
 
 
 def solution(mesh):
@@ -189,25 +215,24 @@
     same_core_col = [[2 * g + c for g in range(ng)] for c in range(2)]
     same_core_all = [[r * nc + 2 * g + c for r in range(nr) for g in range(ng)] for c in range(2)]
     swap_core = [(i, i ^ 1) for i in range(nc)]
-    across = [
-        (r * nc + c, (r ^ (nr // 2)) * nc + (c ^ (nc // 2))) for r in range(nr) for c in range(nc)
-    ]
     ny = nr // 2
+    across = [(r * nc + c, (r + ny) % nr * nc + (c ^ ng)) for r in range(nr) for c in range(nc)]
 
     def along_y(block, dy):
         return lax.ppermute(
             block, "row", [(i, i // ny * ny + (i + dy) % ny) for i in range(nr)]
         )
 
+    def to_neighbour(block):
+        return lax.ppermute(block, ("row", "col"), across)
+
     def spread(bias):
-        me = lax.axis_index("row")
-        ids = lambda dx, dy: ((me // ny) ^ dx) * ny + (me + ny - dy) % ny
-        over = lax.ppermute(bias, ("row", "col"), across)
-        got = [bias, along_y(bias, 1), along_y(bias, 3), over, along_y(bias, 2)]
-        got += [along_y(over, dy) for dy in (1, 3, 2)]
-        order = [ids(0, 0), ids(0, 1), ids(0, 3), ids(1, 0), ids(0, 2)]
-        order += [ids(1, dy) for dy in (1, 3, 2)]
-        return got, jnp.stack(order).astype(jnp.int32)
+        near, far, over, two = along_y(bias, 1), along_y(bias, 3), to_neighbour(bias), along_y(bias, 2)
+        got = [bias, near, far, over, two, along_y(over, 1), along_y(over, 3), to_neighbour(two)]
+        x, y = lax.axis_index("row") // ny, lax.axis_index("row") % ny
+        turns = ((0, 0), (0, 1), (0, 3), (1, 0), (0, 2), (1, 1), (1, 3), (1, 2))
+        ids = [(x ^ dx) * ny + (y + ny - dy) % ny for dx, dy in turns]
+        return got, jnp.stack(ids).astype(jnp.int32)
 
     def per_device(pair, norm_gain, w_proj, w_bias, gate_bias, w_out, out_bias):
         core = lax.axis_index("col") % 2
@@ -237,16 +262,14 @@
         biases, ids = spread(bias)
         x = jnp.stack([x_own, x_other]).reshape(2, ng, nrow, ncol, CH)
         x = x.transpose(2, 0, 1, 3, 4).reshape(nrow, keys, CH)
-        first = attention(
-            ids, x, x[:, :half], biases, norm_gain[0], w_proj[0], gate_bias[0], w_out[0], out_bias[0]
-        )
+        following = [norm_gain[1][None], jnp.pad(w_bias[1].T, ((0, 8 - HEADS), (0, 0)))]
+        args = (norm_gain[0], w_proj[0], gate_bias[0], w_out[0], out_bias[0], following)
+        first, local = attention(ids, x, x[:, :half], biases, *args)
 
         part = ncol // nr
         moved = first.reshape(nrow, ng, nr, part, CH).transpose(2, 1, 0, 3, 4)
         moved = moved.reshape(nr, ng, nrow * part, CH)
-        normed = normalize(first, norm_gain[1])
-        local = jnp.einsum("mqc,ch->mhq", normed, w_bias[1], preferred_element_type=jnp.float32)
-        local = local.astype(jnp.bfloat16).reshape(nrow, HEADS, nr, half // nr).transpose(2, 0, 1, 3)
+        local = local[:, :HEADS].reshape(nrow, HEADS, nr, half // nr).transpose(2, 0, 1, 3)
         local = local.reshape(nr, 1, -1, CH)
         brow = local.shape[2]
         message = jnp.concatenate(
@@ -268,9 +291,8 @@
         x = jnp.concatenate([x_own, x_other])
         xq = x.reshape(2 * part, ng, 2, ncol, CH)
         xq = jnp.where(core == 0, xq[:, :, 0], xq[:, :, 1]).reshape(2 * part, half, CH)
-        last = attention(
-            ids, x, xq, biases, norm_gain[1], w_proj[1], gate_bias[1], w_out[1], out_bias[1]
-        )
+        args = (norm_gain[1], w_proj[1], gate_bias[1], w_out[1], out_bias[1], [])
+        (last,) = attention(ids, x, xq, biases, *args)
 
         own = last[:part]
         other = lax.ppermute(last[part:], "col", swap_core)

time: 205 us -> 184 us (0.90)
  waiting for transfers between devices: 49.2 us -> 33.9 us
  Pallas kernels: 55.6 us -> 46.3 us
  starting transfers between devices: 33.6 us -> 38.6 us
    ppermute x12 -> x10, waiting for transfers between devices: 14.5 us -> 1.26 us  [along_y(): lax.ppermute(block, 'row', [(i, i // ny * ny + (i + dy) % ny) for i in ra...]
    pallas_call x6, Pallas kernels: 48.5 us -> 39.1 us  [attend(): pl.pallas_call(functools.partial(attention_kernel, nblk, len(done), stack...]
    ppermute x12 -> x10, starting transfers between devices: 12.7 us -> 15.6 us  [along_y(): lax.ppermute(block, 'row', [(i, i // ny * ny + (i + dy) % ny) for i in ra...]
    ppermute x2 -> x4, waiting for transfers between devices: 10.2 us -> 8.33 us  [to_neighbour(): return lax.ppermute(block, ('row', 'col'), across)]
  transfers between devices with their start and end apart: 19 -> 19, of which waited for: 8 -> 8; matrix products, arithmetic and copies ran while one was open for 1% -> 2% of each run, Pallas kernels for 20% -> 18%
where the time goes in v4:
time: 184 us; the launch traced here: 183 us
  blocking collectives  50.9 us (28%)
  Pallas kernels  46.3 us (25%)
  starting transfers between devices  38.6 us (21%)
  waiting for transfers between devices  33.9 us (18%)
  local copies, waits for them, and re-layouts  5.87 us (3%)
  other arithmetic  5.56 us (3%)
    pallas_call x6, Pallas kernels, attend(): pl.pallas_call(functools.partial(attention_kernel, nblk, len(done), stack...  39.1 us
    all_to_all x1, blocking collectives, per_device(): lax.all_to_all(message, ('row', 'col'), 0, 0, tiled=True, axis_index_grou...  36.8 us
    all_to_all x1, waiting for transfers between devices, per_device(): lax.all_to_all(message, 'col', 0, 0, tiled=True, axis_index_groups=same_c...  22.1 us
    ppermute x10, starting transfers between devices, along_y(): lax.ppermute(block, 'row', [(i, i // ny * ny + (i + dy) % ny) for i in ra...  15.6 us
    all_to_all x1, blocking collectives, per_device(): got = lax.all_to_all(both.reshape(nr, -1, CH), 'row', 0, 0, tiled=True)  14.1 us
    all_to_all x1, starting transfers between devices, per_device(): lax.all_to_all(message, 'col', 0, 0, tiled=True, axis_index_groups=same_c...  10.2 us
    ppermute x4, waiting for transfers between devices, to_neighbour(): return lax.ppermute(block, ('row', 'col'), across)  8.33 us
    ppermute x2, starting transfers between devices, per_device(): x_other = lax.ppermute(x_own, 'col', swap_core)  7.23 us
  transfers between devices with their start and end apart: 19, of which 8 were waited for; matrix products, arithmetic and copies ran while one was open for 2% of the time, Pallas kernels for 18%

profile of v4, /device:TPU:1, one launch (start us, length us, event | category | flops | bytes accessed | tf_op | source)
XLA Modules:
  0.0 183.2 jit_solution(9890154686909773903)
XLA Ops:
  1.6 1.8 fusion.2
  6.6 10.2 %all-to-all-start = ((bf16[16,224,128]{2,1,0:T(8,128)(2,1)}), bf16[16,224,128]{2,1,0:T(8,128)(2,1)S(1)}, u32[]{:S(2)}, u32[]{:S(2)}) async-start(bf16[16,224,128]{2,1,0:T(8,128)(2,1)} %maximum_maximum_fusion.1), calls=%async_computation | async-start | bytes 1835008 | tf_op jit(solution)/shard_map/all_to_all | solution.py:256
  16.9 22.1 %all-to-all-done = bf16[16,224,128]{2,1,0:T(8,128)(2,1)S(1)} async-done(((bf16[16,224,128]{2,1,0:T(8,128)(2,1)}), bf16[16,224,128]{2,1,0:T(8,128)(2,1)S(1)}, u32[]{:S(2)}, u32[]{:S(2)}) %all-to-all-start) | async-done | bytes 917536 | tf_op jit(solution)/shard_map/all_to_all | solution.py:256
  39.0 2.9 %collective-permute-start = (bf16[16,144,128]{2,1,0:T(8,128)(2,1)S(1)}, bf16[16,144,128]{2,1,0:T(8,128)(2,1)S(1)}, u32[]{:S(2)}, u32[]{:S(2)}) collective-permute-start(bf16[16,144,128]{2,1,0:T(8,128)(2,1)S(1)} %slice.121), channel_id=1, source_target_pairs={{0,1},{1,0},{2,3},{3,2},{4,5},{5,4},{6,7},{7,6},{8,9},{9,8},{10,11... | collective-permute-start | bytes 1769480 | tf_op jit(solution)/shard_map/ppermute | solution.py:258
  44.4 1.8 %collective-permute-start.2 = (bf16[384,384]{1,0:T(8,128)(2,1)S(1)}, bf16[384,384]{1,0:T(8,128)(2,1)S(1)}, u32[]{:S(2)}, u32[]{:S(2)}) collective-permute-start(bf16[384,384]{1,0:T(8,128)(2,1)S(1)} %pad_maximum_fusion.2.refs_0_), channel_id=1, source_target_pairs={{0,144},{1,145},{2,146},{3,147},{4,148},{5,149},{6,150},{7,151},{8... | collective-permute-start | bytes 884744 | tf_op jit(solution)/shard_map/ppermute | solution.py:227
  46.3 2.9 %collective-permute-start.4 = (bf16[384,384]{1,0:T(8,128)(2,1)S(1)}, bf16[384,384]{1,0:T(8,128)(2,1)S(1)}, u32[]{:S(2)}, u32[]{:S(2)}) collective-permute-start(bf16[384,384]{1,0:T(8,128)(2,1)S(1)} %pad_maximum_fusion.2.refs_0_), channel_id=1, source_target_pairs={{0,64},{32,96},{64,0},{96,32},{128,192},{160,224},{192,128},{224,1... | collective-permute-start | bytes 884744 | tf_op jit(solution)/shard_map/ppermute | solution.py:222
  49.8 2.3 %collective-permute-start.7 = (bf16[384,384]{1,0:T(8,128)(2,1)S(1)}, bf16[384,384]{1,0:T(8,128)(2,1)S(1)}, u32[]{:S(2)}, u32[]{:S(2)}) collective-permute-start(bf16[384,384]{1,0:T(8,128)(2,1)S(1)} %pad_maximum_fusion.2.refs_0_), channel_id=1, source_target_pairs={{0,96},{32,0},{64,32},{96,64},{128,224},{160,128},{192,160},{224,1... | collective-permute-start | bytes 884744 | tf_op jit(solution)/shard_map/ppermute | solution.py:222
  52.0 2.2 %collective-permute-done.2.refs_3_ = bf16[384,384]{1,0:T(8,128)(2,1)S(1)} collective-permute-done((bf16[384,384]{1,0:T(8,128)(2,1)S(1)}, bf16[384,384]{1,0:T(8,128)(2,1)S(1)}, u32[]{:S(2)}, u32[]{:S(2)}) %collective-permute-start.2) | collective-permute-done | bytes 294944 | tf_op jit(solution)/shard_map/ppermute | solution.py:227
  56.0 2.7 %collective-permute-start.3 = (bf16[384,384]{1,0:T(8,128)(2,1)S(1)}, bf16[384,384]{1,0:T(8,128)(2,1)S(1)}, u32[]{:S(2)}, u32[]{:S(2)}) collective-permute-start(bf16[384,384]{1,0:T(8,128)(2,1)S(1)} %collective-permute-done.2.refs_3_), channel_id=1, source_target_pairs={{0,96},{32,0},{64,32},{96,64},{128,224},{160,128},{192,160},{224,1... | collective-permute-start | bytes 884744 | tf_op jit(solution)/shard_map/ppermute | solution.py:222
  60.1 3.6 %prepare.2 = (bf16[6,128,768]{2,1,0:T(8,128)(2,1)S(1)}, bf16[6,768,128]{2,1,0:T(8,128)(2,1)S(1)}, bf16[6,384,128]{2,1,0:T(8,128)(2,1)S(1)}, f32[6,384,128]{2,1,0:T(8,128)S(1)}) custom-call(bf16[6,768,128]{2,1,0:T(8,128)(2,1)S(1)} %bitcast.72, bf16[6,384,128]{2,1,0:T(8,128)(2,1)S(1)} %slice.122.xq_ref, f32[1,128]{1,0:T(1,128)S(1)} %get-tuple-element.42.gain_ref, ...), custom_call_target="tpu_custom_call" | custom-call | flops 4000000000 | bytes 6291456 | tf_op jit(solution)/shard_map/prepare/pallas_call | solution.py:65
  63.7 8.0 %attend.6.refs_4_ = bf16[4,6,48,128]{3,2,1,0:T(8,128)(2,1)S(1)} custom-call(s32[4]{0:T(128)S(1)} %pad_add_fusion.1.blk_ref.done_blk_ref, s32[1]{0:T(128)} %bitcast.2.done_blk_ref, bf16[6,128,768]{2,1,0:T(8,128)(2,1)S(1)} %get-tuple-element.15.kt_ref, bf16[6,768,128]{2,1,0:T(8,128)(2,1)S(1)} %get-tuple-element.16.v_ref, ...), custom_call_target="tpu_custom_call" | custom-call | flops 11200000000 | bytes 6291456 | tf_op jit(solution)/shard_map/attend/pallas_call | solution.py:167
  71.7 5.1 %attend.7.refs_5_ = bf16[2,6,48,128]{3,2,1,0:T(8,128)(2,1)S(1)} custom-call(s32[2]{0:T(128)S(1)} %pad_add_fusion.2.blk_ref, s32[4]{0:T(128)S(1)} %pad_add_fusion.1.blk_ref.done_blk_ref, bf16[6,128,768]{2,1,0:T(8,128)(2,1)S(1)} %get-tuple-element.15.kt_ref, bf16[6,768,128]{2,1,0:T(8,128)(2,1)S(1)} %get-tuple-element.16.v_ref, ...), custom_call_target="tpu_custom_call" | custom-call | flops 5600000000 | bytes 6291456 | tf_op jit(solution)/shard_map/attend/pallas_call | solution.py:167
  76.8 7.5 %attend.8 = (bf16[6,384,128]{2,1,0:T(8,128)(2,1)S(1)}, bf16[6,8,384]{2,1,0:T(8,128)(2,1)S(1)}) custom-call(s32[2]{0:T(128)S(1)} %pad_add_fusion.blk_ref, s32[6]{0:T(128)S(1)} %stack.69.done_blk_ref, bf16[6,128,768]{2,1,0:T(8,128)(2,1)S(1)} %get-tuple-element.15.kt_ref, bf16[6,768,128]{2,1,0:T(8,128)(2,1)S(1)} %get-tuple-element.16.v_ref, ...), custom_call_target="tpu_custom_call" | custom-call | flops 5600000000 | bytes 6291456 | tf_op jit(solution)/shard_map/attend/pallas_call | solution.py:167
  86.1 36.8 %all_to_all.15 = bf16[128,32,128]{2,1,0:T(8,128)(2,1)S(1)} all-to-all(bf16[128,32,128]{2,1,0:T(8,128)(2,1)S(1)} %copy.35), channel_id=1, replica_groups={{0,2,4,6,8,10,12,14,16,18,20,22,24,26,28,30,32,34,36,38,40,42,44,46,48,..., dimensions={0} | all-to-all | bytes 2097152 | tf_op jit(solution)/shard_map/all_to_all | solution.py:283
  123.5 4.3 %collective-permute-start.9 = (bf16[3,768,128]{2,1,0:T(8,128)(2,1)S(1)}, bf16[3,768,128]{2,1,0:T(8,128)(2,1)S(1)}, u32[]{:S(2)}, u32[]{:S(2)}) collective-permute-start(bf16[3,768,128]{2,1,0:T(8,128)(2,1)S(1)} %bitcast.83), channel_id=1, source_target_pairs={{0,1},{1,0},{2,3},{3,2},{4,5},{5,4},{6,7},{7,6},{8,9},{9,8},{10,11... | collective-permute-start | bytes 1769480 | tf_op jit(solution)/shard_map/ppermute | solution.py:287
  130.3 2.3 %collective-permute-start.15 = (bf16[384,384]{1,0:T(8,128)(2,1)S(1)}, bf16[384,384]{1,0:T(8,128)(2,1)S(1)}, u32[]{:S(2)}, u32[]{:S(2)}) collective-permute-start(bf16[384,384]{1,0:T(8,128)(2,1)S(1)} %pad_maximum_fusion.3.refs_0_), channel_id=1, source_target_pairs={{0,96},{32,0},{64,32},{96,64},{128,224},{160,128},{192,160},{224,1... | collective-permute-start | bytes 884744 | tf_op jit(solution)/shard_map/ppermute | solution.py:222
  132.6 6.2 %collective-permute-done.10.refs_3_ = bf16[384,384]{1,0:T(8,128)(2,1)S(1)} collective-permute-done((bf16[384,384]{1,0:T(8,128)(2,1)S(1)}, bf16[384,384]{1,0:T(8,128)(2,1)S(1)}, u32[]{:S(2)}, u32[]{:S(2)}) %collective-permute-start.10) | collective-permute-done | bytes 294944 | tf_op jit(solution)/shard_map/ppermute | solution.py:227
  139.2 2.2 %collective-permute-start.11 = (bf16[384,384]{1,0:T(8,128)(2,1)S(1)}, bf16[384,384]{1,0:T(8,128)(2,1)S(1)}, u32[]{:S(2)}, u32[]{:S(2)}) collective-permute-start(bf16[384,384]{1,0:T(8,128)(2,1)S(1)} %collective-permute-done.10.refs_3_), channel_id=1, source_target_pairs={{0,96},{32,0},{64,32},{96,64},{128,224},{160,128},{192,160},{224,1... | collective-permute-start | bytes 884744 | tf_op jit(solution)/shard_map/ppermute | solution.py:222
  141.9 3.6 %prepare.3 = (bf16[6,128,768]{2,1,0:T(8,128)(2,1)S(1)}, bf16[6,768,128]{2,1,0:T(8,128)(2,1)S(1)}, bf16[6,384,128]{2,1,0:T(8,128)(2,1)S(1)}, f32[6,384,128]{2,1,0:T(8,128)S(1)}) custom-call(bf16[6,768,128]{2,1,0:T(8,128)(2,1)S(1)} %pad_maximum_fusion.x_ref, bf16[6,384,128]{2,1,0:T(8,128)(2,1)S(1)} %bitcast.73, ...), custom_call_target="tpu_custom_call" | custom-call | flops 4000000000 | bytes 6291456 | tf_op jit(solution)/shard_map/prepare/pallas_call | solution.py:65
  145.8 8.2 %attend.9.refs_4_ = bf16[4,6,48,128]{3,2,1,0:T(8,128)(2,1)S(1)} custom-call(s32[4]{0:T(128)S(1)} %pad_add_fusion.1.blk_ref.done_blk_ref, s32[1]{0:T(128)} %bitcast.2.done_blk_ref, bf16[6,128,768]{2,1,0:T(8,128)(2,1)S(1)} %get-tuple-element.21.kt_ref, bf16[6,768,128]{2,1,0:T(8,128)(2,1)S(1)} %get-tuple-element.22.v_ref, ...), custom_call_target="tpu_custom_call" | custom-call | flops 11200000000 | bytes 6291456 | tf_op jit(solution)/shard_map/attend/pallas_call | solution.py:167
  154.0 5.1 %attend.10.refs_5_ = bf16[2,6,48,128]{3,2,1,0:T(8,128)(2,1)S(1)} custom-call(s32[2]{0:T(128)S(1)} %pad_add_fusion.2.blk_ref, s32[4]{0:T(128)S(1)} %pad_add_fusion.1.blk_ref.done_blk_ref, bf16[6,128,768]{2,1,0:T(8,128)(2,1)S(1)} %get-tuple-element.21.kt_ref, bf16[6,768,128]{2,1,0:T(8,128)(2,1)S(1)} %get-tuple-element.22.v_ref, ...), custom_call_target="tpu_custom_call" | custom-call | flops 5600000000 | bytes 6291456 | tf_op jit(solution)/shard_map/attend/pallas_call | solution.py:167
  159.1 5.2 %attend.11 = bf16[6,384,128]{2,1,0:T(8,128)(2,1)S(1)} custom-call(s32[2]{0:T(128)S(1)} %pad_add_fusion.blk_ref, s32[6]{0:T(128)S(1)} %stack.69.done_blk_ref, bf16[6,128,768]{2,1,0:T(8,128)(2,1)S(1)} %get-tuple-element.21.kt_ref, bf16[6,768,128]{2,1,0:T(8,128)(2,1)S(1)} %get-tuple-element.22.v_ref, bf16[6,384,128]{2,1,0:T(8,128)(2,1)S(1)} %get-tuple-element.23.q_ref, ...), custom_call_target="tpu_custom_call" | custom-call | flops 5600000000 | bytes 6291456 | tf_op jit(solution)/shard_map/attend/pallas_call | solution.py:167
  164.4 2.2 %collective-permute-start.17 = (bf16[3,384,128]{2,1,0:T(8,128)(2,1)S(1)}, bf16[3,384,128]{2,1,0:T(8,128)(2,1)S(1)}, u32[]{:S(2)}, u32[]{:S(2)}) collective-permute-start(bf16[3,384,128]{2,1,0:T(8,128)(2,1)S(1)} %slice.132), channel_id=1, source_target_pairs={{0,1},{1,0},{2,3},{3,2},{4,5},{5,4},{6,7},{7,6},{8,9},{9,8},{10,11... | collective-permute-start | bytes 884744 | tf_op jit(solution)/shard_map/ppermute | solution.py:298
  168.0 14.1 %all_to_all.16 = bf16[8,288,128]{2,1,0:T(8,128)(2,1)S(1)} all-to-all(bf16[8,288,128]{2,1,0:T(8,128)(2,1)S(1)} %bitcast.79), channel_id=1, replica_groups=mesh['row'=8,'col'=32] {'row'}, dimensions={0} | all-to-all | bytes 1179648 | tf_op jit(solution)/shard_map/all_to_all | solution.py:301
  (97 shorter events, 19.4 us)
Async XLA Ops:
  0.0 3.4 %copy-start = (bf16[96,24,128]{2,1,0:T(8,128)(2,1)S(1)}, bf16[96,24,128]{2,1,0:T(8,128)(2,1)}, u32[]{:S(2)}) copy-start(bf16[96,24,128]{2,1,0:T(8,128)(2,1)} %param.7) | copy-start | bytes 1769476
  0.0 3.4 %copy-start.6 = (bf16[2,128,4]{1,2,0:T(4,128)(2,1)S(1)}, bf16[2,128,4]{1,2,0:T(4,128)(2,1)}, u32[]{:S(2)}) copy-start(bf16[2,128,4]{1,2,0:T(4,128)(2,1)} %param.10) | copy-start | bytes 6148
  6.6 10.3 %copy-start.3 = (f32[2,128]{1,0:T(2,128)S(1)}, f32[2,128]{1,0:T(2,128)}, u32[]{:S(2)}) copy-start(f32[2,128]{1,0:T(2,128)} %param.13) | copy-start | bytes 3076
  6.6 10.3 %copy-start.2 = (bf16[2,128,128]{2,1,0:T(8,128)(2,1)S(1)}, bf16[2,128,128]{2,1,0:T(8,128)(2,1)}, u32[]{:S(2)}) copy-start(bf16[2,128,128]{2,1,0:T(8,128)(2,1)} %param.12) | copy-start | bytes 196612
  6.6 32.4 %all-to-all-start = ((bf16[16,224,128]{2,1,0:T(8,128)(2,1)}), bf16[16,224,128]{2,1,0:T(8,128)(2,1)S(1)}, u32[]{:S(2)}, u32[]{:S(2)}) async-start(bf16[16,224,128]{2,1,0:T(8,128)(2,1)} %maximum_maximum_fusion.1), calls=%async_computation | async-start | bytes 1835008 | tf_op jit(solution)/shard_map/all_to_all | solution.py:256
  39.0 19.7 %collective-permute-start = (bf16[16,144,128]{2,1,0:T(8,128)(2,1)S(1)}, bf16[16,144,128]{2,1,0:T(8,128)(2,1)S(1)}, u32[]{:S(2)}, u32[]{:S(2)}) collective-permute-start(bf16[16,144,128]{2,1,0:T(8,128)(2,1)S(1)} %slice.121), channel_id=1, source_target_pairs={{0,1},{1,0},{2,3},{3,2},{4,5},{5,4},{6,7},{7,6},{8,9},{9,8},{10,11... | collective-permute-start | bytes 1769480 | tf_op jit(solution)/shard_map/ppermute | solution.py:258
  42.7 6.5 %copy-start.1 = (bf16[2,128,512]{2,1,0:T(8,128)(2,1)S(1)}, bf16[2,128,512]{2,1,0:T(8,128)(2,1)}, u32[]{:S(2)}) copy-start(bf16[2,128,512]{2,1,0:T(8,128)(2,1)} %param.9) | copy-start | bytes 786436
  42.8 1.5 collective-permute-start.1
  44.4 9.8 %collective-permute-start.2 = (bf16[384,384]{1,0:T(8,128)(2,1)S(1)}, bf16[384,384]{1,0:T(8,128)(2,1)S(1)}, u32[]{:S(2)}, u32[]{:S(2)}) collective-permute-start(bf16[384,384]{1,0:T(8,128)(2,1)S(1)} %pad_maximum_fusion.2.refs_0_), channel_id=1, source_target_pairs={{0,144},{1,145},{2,146},{3,147},{4,148},{5,149},{6,150},{7,151},{8... | collective-permute-start | bytes 884744 | tf_op jit(solution)/shard_map/ppermute | solution.py:227
  46.3 9.7 %collective-permute-start.4 = (bf16[384,384]{1,0:T(8,128)(2,1)S(1)}, bf16[384,384]{1,0:T(8,128)(2,1)S(1)}, u32[]{:S(2)}, u32[]{:S(2)}) collective-permute-start(bf16[384,384]{1,0:T(8,128)(2,1)S(1)} %pad_maximum_fusion.2.refs_0_), channel_id=1, source_target_pairs={{0,64},{32,96},{64,0},{96,32},{128,192},{160,224},{192,128},{224,1... | collective-permute-start | bytes 884744 | tf_op jit(solution)/shard_map/ppermute | solution.py:222
  49.3 14.4 %collective-permute-start.6 = (bf16[384,384]{1,0:T(8,128)(2,1)S(1)}, bf16[384,384]{1,0:T(8,128)(2,1)S(1)}, u32[]{:S(2)}, u32[]{:S(2)}) collective-permute-start(bf16[384,384]{1,0:T(8,128)(2,1)S(1)} %pad_maximum_fusion.2.refs_0_), channel_id=1, source_target_pairs={{0,32},{32,64},{64,96},{96,0},{128,160},{160,192},{192,224},{224,1... | collective-permute-start | bytes 884744 | tf_op jit(solution)/shard_map/ppermute | solution.py:222
  49.8 13.9 %collective-permute-start.7 = (bf16[384,384]{1,0:T(8,128)(2,1)S(1)}, bf16[384,384]{1,0:T(8,128)(2,1)S(1)}, u32[]{:S(2)}, u32[]{:S(2)}) collective-permute-start(bf16[384,384]{1,0:T(8,128)(2,1)S(1)} %pad_maximum_fusion.2.refs_0_), channel_id=1, source_target_pairs={{0,96},{32,0},{64,32},{96,64},{128,224},{160,128},{192,160},{224,1... | collective-permute-start | bytes 884744 | tf_op jit(solution)/shard_map/ppermute | solution.py:222
  54.2 17.5 %collective-permute-start.8 = (bf16[384,384]{1,0:T(8,128)(2,1)S(1)}, bf16[384,384]{1,0:T(8,128)(2,1)S(1)}, u32[]{:S(2)}, u32[]{:S(2)}) collective-permute-start(bf16[384,384]{1,0:T(8,128)(2,1)S(1)} %collective-permute-done.2.refs_3_), channel_id=1, source_target_pairs={{0,32},{32,64},{64,96},{96,0},{128,160},{160,192},{192,224},{224,1... | collective-permute-start | bytes 884744 | tf_op jit(solution)/shard_map/ppermute | solution.py:222
  56.0 20.9 %collective-permute-start.3 = (bf16[384,384]{1,0:T(8,128)(2,1)S(1)}, bf16[384,384]{1,0:T(8,128)(2,1)S(1)}, u32[]{:S(2)}, u32[]{:S(2)}) collective-permute-start(bf16[384,384]{1,0:T(8,128)(2,1)S(1)} %collective-permute-done.2.refs_3_), channel_id=1, source_target_pairs={{0,96},{32,0},{64,32},{96,64},{128,224},{160,128},{192,160},{224,1... | collective-permute-start | bytes 884744 | tf_op jit(solution)/shard_map/ppermute | solution.py:222
  58.7 18.1 %collective-permute-start.5 = (bf16[384,384]{1,0:T(8,128)(2,1)S(1)}, bf16[384,384]{1,0:T(8,128)(2,1)S(1)}, u32[]{:S(2)}, u32[]{:S(2)}) collective-permute-start(bf16[384,384]{1,0:T(8,128)(2,1)S(1)} %collective-permute-done.4.refs_0_), channel_id=1, source_target_pairs={{0,144},{1,145},{2,146},{3,147},{4,148},{5,149},{6,150},{7,151},{8... | collective-permute-start | bytes 884744 | tf_op jit(solution)/shard_map/ppermute | solution.py:227
  123.5 17.9 %collective-permute-start.9 = (bf16[3,768,128]{2,1,0:T(8,128)(2,1)S(1)}, bf16[3,768,128]{2,1,0:T(8,128)(2,1)S(1)}, u32[]{:S(2)}, u32[]{:S(2)}) collective-permute-start(bf16[3,768,128]{2,1,0:T(8,128)(2,1)S(1)} %bitcast.83), channel_id=1, source_target_pairs={{0,1},{1,0},{2,3},{3,2},{4,5},{5,4},{6,7},{7,6},{8,9},{9,8},{10,11... | collective-permute-start | bytes 1769480 | tf_op jit(solution)/shard_map/ppermute | solution.py:287
  128.6 10.1 %collective-permute-start.10 = (bf16[384,384]{1,0:T(8,128)(2,1)S(1)}, bf16[384,384]{1,0:T(8,128)(2,1)S(1)}, u32[]{:S(2)}, u32[]{:S(2)}) collective-permute-start(bf16[384,384]{1,0:T(8,128)(2,1)S(1)} %pad_maximum_fusion.3.refs_0_), channel_id=1, source_target_pairs={{0,144},{1,145},{2,146},{3,147},{4,148},{5,149},{6,150},{7,151},{8... | collective-permute-start | bytes 884744 | tf_op jit(solution)/shard_map/ppermute | solution.py:227
  128.9 10.3 %collective-permute-start.12 = (bf16[384,384]{1,0:T(8,128)(2,1)S(1)}, bf16[384,384]{1,0:T(8,128)(2,1)S(1)}, u32[]{:S(2)}, u32[]{:S(2)}) collective-permute-start(bf16[384,384]{1,0:T(8,128)(2,1)S(1)} %pad_maximum_fusion.3.refs_0_), channel_id=1, source_target_pairs={{0,64},{32,96},{64,0},{96,32},{128,192},{160,224},{192,128},{224,1... | collective-permute-start | bytes 884744 | tf_op jit(solution)/shard_map/ppermute | solution.py:222
  129.9 15.9 %collective-permute-start.14 = (bf16[384,384]{1,0:T(8,128)(2,1)S(1)}, bf16[384,384]{1,0:T(8,128)(2,1)S(1)}, u32[]{:S(2)}, u32[]{:S(2)}) collective-permute-start(bf16[384,384]{1,0:T(8,128)(2,1)S(1)} %pad_maximum_fusion.3.refs_0_), channel_id=1, source_target_pairs={{0,32},{32,64},{64,96},{96,0},{128,160},{160,192},{192,224},{224,1... | collective-permute-start | bytes 884744 | tf_op jit(solution)/shard_map/ppermute | solution.py:222
  130.3 15.5 %collective-permute-start.15 = (bf16[384,384]{1,0:T(8,128)(2,1)S(1)}, bf16[384,384]{1,0:T(8,128)(2,1)S(1)}, u32[]{:S(2)}, u32[]{:S(2)}) collective-permute-start(bf16[384,384]{1,0:T(8,128)(2,1)S(1)} %pad_maximum_fusion.3.refs_0_), channel_id=1, source_target_pairs={{0,96},{32,0},{64,32},{96,64},{128,224},{160,128},{192,160},{224,1... | collective-permute-start | bytes 884744 | tf_op jit(solution)/shard_map/ppermute | solution.py:222
  138.8 15.2 %collective-permute-start.16 = (bf16[384,384]{1,0:T(8,128)(2,1)S(1)}, bf16[384,384]{1,0:T(8,128)(2,1)S(1)}, u32[]{:S(2)}, u32[]{:S(2)}) collective-permute-start(bf16[384,384]{1,0:T(8,128)(2,1)S(1)} %collective-permute-done.10.refs_3_), channel_id=1, source_target_pairs={{0,32},{32,64},{64,96},{96,0},{128,160},{160,192},{192,224},{224,1... | collective-permute-start | bytes 884744 | tf_op jit(solution)/shard_map/ppermute | solution.py:222
  139.2 19.9 %collective-permute-start.11 = (bf16[384,384]{1,0:T(8,128)(2,1)S(1)}, bf16[384,384]{1,0:T(8,128)(2,1)S(1)}, u32[]{:S(2)}, u32[]{:S(2)}) collective-permute-start(bf16[384,384]{1,0:T(8,128)(2,1)S(1)} %collective-permute-done.10.refs_3_), channel_id=1, source_target_pairs={{0,96},{32,0},{64,32},{96,64},{128,224},{160,128},{192,160},{224,1... | collective-permute-start | bytes 884744 | tf_op jit(solution)/shard_map/ppermute | solution.py:222
  141.4 17.7 %collective-permute-start.13 = (bf16[384,384]{1,0:T(8,128)(2,1)S(1)}, bf16[384,384]{1,0:T(8,128)(2,1)S(1)}, u32[]{:S(2)}, u32[]{:S(2)}) collective-permute-start(bf16[384,384]{1,0:T(8,128)(2,1)S(1)} %collective-permute-done.12.refs_0_), channel_id=1, source_target_pairs={{0,144},{1,145},{2,146},{3,147},{4,148},{5,149},{6,150},{7,151},{8... | collective-permute-start | bytes 884744 | tf_op jit(solution)/shard_map/ppermute | solution.py:227
  164.4 3.4 %collective-permute-start.17 = (bf16[3,384,128]{2,1,0:T(8,128)(2,1)S(1)}, bf16[3,384,128]{2,1,0:T(8,128)(2,1)S(1)}, u32[]{:S(2)}, u32[]{:S(2)}) collective-permute-start(bf16[3,384,128]{2,1,0:T(8,128)(2,1)S(1)} %slice.132), channel_id=1, source_target_pairs={{0,1},{1,0},{2,3},{3,2},{4,5},{5,4},{6,7},{7,6},{8,9},{9,8},{10,11... | collective-permute-start | bytes 884744 | tf_op jit(solution)/shard_map/ppermute | solution.py:298
  (2 other events, 6.7 us)

commit v5 on v4

--- a/solution.py
+++ b/solution.py
@@ -11,7 +11,7 @@
 WIDTH = 32
 CH = 128
 LOG2E = 1.4426950408889634
-CALLS = (4, 2, 2)
+CALLS = (4, 4)
 NT = (((1,), (1,)), ((), ()))
 
 
@@ -186,8 +186,7 @@
     )(ids, done_ids, *parts, xq, *biases, *small, *done, *following)
 
 
-def attention(ids, x, xq, biases, gain, wp, gb, wo, ob, following):
-    parts = prepare(x, xq, gain, wp, gb)
+def attention(ids, parts, xq, biases, wo, ob, following):
     done, at = [], 0
     for n in CALLS:
         last = at + n == len(biases)
@@ -227,12 +226,21 @@
         return lax.ppermute(block, ("row", "col"), across)
 
     def spread(bias):
-        near, far, over, two = along_y(bias, 1), along_y(bias, 3), to_neighbour(bias), along_y(bias, 2)
+        return [along_y(bias, 1), along_y(bias, 3), to_neighbour(bias), along_y(bias, 2)]
+
+    def spread_on(bias, first, parts):
+        near, far, over, two = first
+        over, two, parts = lax.optimization_barrier((over, two, parts))
         got = [bias, near, far, over, two, along_y(over, 1), along_y(over, 3), to_neighbour(two)]
         x, y = lax.axis_index("row") // ny, lax.axis_index("row") % ny
         turns = ((0, 0), (0, 1), (0, 3), (1, 0), (0, 2), (1, 1), (1, 3), (1, 2))
         ids = [(x ^ dx) * ny + (y + ny - dy) % ny for dx, dy in turns]
-        return got, jnp.stack(ids).astype(jnp.int32)
+        return got, jnp.stack(ids).astype(jnp.int32), parts
+
+    def all_to_all_16(message):
+        return lax.all_to_all(
+            message, "col", 0, 0, tiled=True, axis_index_groups=same_core_col
+        )
 
     def per_device(pair, norm_gain, w_proj, w_bias, gate_bias, w_out, out_bias):
         core = lax.axis_index("col") % 2
@@ -243,28 +251,26 @@
         normed = normalize(pair, norm_gain[0])
         local = jnp.einsum("qmc,ch->mhq", normed, w_bias[0], preferred_element_type=jnp.float32)
         local = local.astype(jnp.bfloat16).reshape(ncol, HEADS, 2, 2, ncol).transpose(0, 3, 1, 2, 4)
-        local = jnp.where(core == 0, local, local[:, ::-1]).reshape(-1, CH)
+        local = local.reshape(ncol, 2, -1)
+        own = jnp.where(core == 0, local[:, 0], local[:, 1])
+        other = jnp.where(core == 0, local[:, 1], local[:, 0])
+        other = lax.ppermute(other, "col", swap_core)
+        local = jnp.concatenate([own, other], axis=1).reshape(-1, CH)
         brow = local.shape[0]
-        message = jnp.concatenate(
-            [
-                pair.reshape(ng, nrow * ncol, CH),
-                jnp.broadcast_to(local[None], (ng, brow, CH)),
-                jnp.zeros((ng, -brow % 16, CH), jnp.bfloat16),
-            ],
-            axis=1,
-        )
-        got = lax.all_to_all(message, "col", 0, 0, tiled=True, axis_index_groups=same_core_col)
+        message = jnp.broadcast_to(local[None], (ng,) + local.shape)
+        message = jnp.concatenate([pair.reshape(ng, nrow * ncol, CH), message], axis=1)
+        got = all_to_all_16(message)
         x_own = got[:, : nrow * ncol]
         x_other = lax.ppermute(x_own, "col", swap_core)
-        bias = got[:, nrow * ncol : nrow * ncol + brow].reshape(half, 2, half // 2)
-        bias_other = lax.ppermute(bias[:, 1], "col", swap_core)
-        bias = jnp.concatenate([bias[:, 0], bias_other], axis=1)
-        biases, ids = spread(bias)
+        bias = got[:, nrow * ncol :].reshape(half, half)
+        first_biases = spread(bias)
         x = jnp.stack([x_own, x_other]).reshape(2, ng, nrow, ncol, CH)
         x = x.transpose(2, 0, 1, 3, 4).reshape(nrow, keys, CH)
         following = [norm_gain[1][None], jnp.pad(w_bias[1].T, ((0, 8 - HEADS), (0, 0)))]
-        args = (norm_gain[0], w_proj[0], gate_bias[0], w_out[0], out_bias[0], following)
-        first, local = attention(ids, x, x[:, :half], biases, *args)
+        xq = x[:, :half]
+        parts = prepare(x, xq, norm_gain[0], w_proj[0], gate_bias[0])
+        biases, ids, parts = spread_on(bias, first_biases, parts)
+        first, local = attention(ids, parts, xq, biases, w_out[0], out_bias[0], following)
 
         part = ncol // nr
         moved = first.reshape(nrow, ng, nr, part, CH).transpose(2, 1, 0, 3, 4)
@@ -287,12 +293,13 @@
         x_other = lax.ppermute(x_own, "col", swap_core)
         bias = got[:, nrow * part : nrow * part + brow].reshape(2, half, half // 2)
         bias = jnp.concatenate([bias[0], bias[1]], axis=1)
-        biases, ids = spread(bias)
+        first_biases = spread(bias)
         x = jnp.concatenate([x_own, x_other])
         xq = x.reshape(2 * part, ng, 2, ncol, CH)
         xq = jnp.where(core == 0, xq[:, :, 0], xq[:, :, 1]).reshape(2 * part, half, CH)
-        args = (norm_gain[1], w_proj[1], gate_bias[1], w_out[1], out_bias[1], [])
-        (last,) = attention(ids, x, xq, biases, *args)
+        parts = prepare(x, xq, norm_gain[1], w_proj[1], gate_bias[1])
+        biases, ids, parts = spread_on(bias, first_biases, parts)
+        (last,) = attention(ids, parts, xq, biases, w_out[1], out_bias[1], [])
 
         own = last[:part]
         other = lax.ppermute(last[part:], "col", swap_core)

time: 184 us -> 176 us (0.957)
  Pallas kernels: 46.3 us -> 41.9 us
  starting transfers between devices: 38.6 us -> 35 us
  blocking collectives: 50.9 us -> 53.4 us
    ppermute x10, waiting for transfers between devices: 1.26 us -> 9.62 us  [along_y(): lax.ppermute(block, 'row', [(i, i // ny * ny + (i + dy) % ny) for i in ra...]
    ppermute x4, waiting for transfers between devices: 8.33 us -> 0.01 us  [to_neighbour(): return lax.ppermute(block, ('row', 'col'), across)]
    pallas_call x6 -> x4, Pallas kernels: 39.1 us -> 34.7 us  [attend(): pl.pallas_call(functools.partial(attention_kernel, nblk, len(done), stack...]
    ppermute x1, starting transfers between devices: 0.11 us -> 3.31 us  [per_device(): other = lax.ppermute(other, 'col', swap_core)]
    all_to_all x1, starting transfers between devices: 10.2 us -> 7.63 us  [all_to_all_16(): lax.all_to_all(message, 'col', 0, 0, tiled=True, axis_index_groups=same_c...]
    all_to_all x1, blocking collectives: 36.8 us -> 39.2 us  [per_device(): lax.all_to_all(message, ('row', 'col'), 0, 0, tiled=True, axis_index_grou...]
  transfers between devices with their start and end apart: 19 -> 19, of which waited for: 8 -> 7; matrix products, arithmetic and copies ran while one was open for 2% -> 1% of each run, Pallas kernels for 18% -> 13%
where the time goes in v5:
time: 176 us; the launch traced here: 175 us
  blocking collectives  53.4 us (30%)
  Pallas kernels  41.9 us (24%)
  starting transfers between devices  35 us (20%)
  waiting for transfers between devices  33 us (19%)
  other arithmetic  5.15 us (3%)
  local copies, waits for them, and re-layouts  5 us (3%)
    all_to_all x1, blocking collectives, per_device(): lax.all_to_all(message, ('row', 'col'), 0, 0, tiled=True, axis_index_grou...  39.2 us
    pallas_call x4, Pallas kernels, attend(): pl.pallas_call(functools.partial(attention_kernel, nblk, len(done), stack...  34.7 us
    all_to_all x1, waiting for transfers between devices, all_to_all_16(): lax.all_to_all(message, 'col', 0, 0, tiled=True, axis_index_groups=same_c...  21.4 us
    all_to_all x1, blocking collectives, per_device(): got = lax.all_to_all(both.reshape(nr, -1, CH), 'row', 0, 0, tiled=True)  14.1 us
    ppermute x10, starting transfers between devices, along_y(): lax.ppermute(block, 'row', [(i, i // ny * ny + (i + dy) % ny) for i in ra...  13.8 us
    ppermute x10, waiting for transfers between devices, along_y(): lax.ppermute(block, 'row', [(i, i // ny * ny + (i + dy) % ny) for i in ra...  9.62 us
    all_to_all x1, starting transfers between devices, all_to_all_16(): lax.all_to_all(message, 'col', 0, 0, tiled=True, axis_index_groups=same_c...  7.63 us
    pallas_call x2, Pallas kernels, prepare(): pl.pallas_call(prepare_kernel, grid=(nrow,), in_specs=[by_row(x), by_row(...  7.14 us
  transfers between devices with their start and end apart: 19, of which 7 were waited for; matrix products, arithmetic and copies ran while one was open for 1% of the time, Pallas kernels for 13%

profile of v5, /device:TPU:1, one launch (start us, length us, event | category | flops | bytes accessed | tf_op | source)
XLA Modules:
  0.0 175.5 jit_solution(13575349153541356925)
XLA Ops:
  0.0 1.5 convert_reduce_fusion
  1.6 1.8 %fusion.2 = f32[96,24]{1,0:T(8,128)S(1)} fusion(bf16[96,24,128]{2,1,0:T(8,128)(2,1)} %param.7, f32[96,24]{1,0:T(8,128)S(1)} %broadcast_multiply_fusion), kind=kLoop, calls=%fused_computation.4 | loop fusion | flops 1177344 | bytes 608256 | tf_op jit(solution)/shard_map/reduce_sum | solution.py:21
  5.1 3.3 %collective-permute-start = (bf16[24,192]{1,0:T(8,128)(2,1)S(1)}, bf16[24,192]{1,0:T(8,128)(2,1)S(1)}, u32[]{:S(2)}, u32[]{:S(2)}) collective-permute-start(bf16[24,192]{1,0:T(8,128)(2,1)S(1)} %get-tuple-element.58), channel_id=1, source_target_pairs={{0,1},{1,0},{2,3},{3,2},{4,5},{5,4},{6,7},{7,6},{8,9},{9,8},{10,11... | collective-permute-start | bytes 27656 | tf_op jit(solution)/shard_map/ppermute | solution.py:257
  10.4 7.6 %all-to-all-start = ((bf16[16,216,128]{2,1,0:T(8,128)(2,1)}), bf16[16,216,128]{2,1,0:T(8,128)(2,1)S(1)}, u32[]{:S(2)}, u32[]{:S(2)}) async-start(bf16[16,216,128]{2,1,0:T(8,128)(2,1)} %pad_maximum_fusion.2), calls=%async_computation | async-start | bytes 1769472 | tf_op jit(solution)/shard_map/all_to_all | solution.py:241
  18.1 21.4 %all-to-all-done = bf16[16,216,128]{2,1,0:T(8,128)(2,1)S(1)} async-done(((bf16[16,216,128]{2,1,0:T(8,128)(2,1)}), bf16[16,216,128]{2,1,0:T(8,128)(2,1)S(1)}, u32[]{:S(2)}, u32[]{:S(2)}) %all-to-all-start) | async-done | bytes 884768 | tf_op jit(solution)/shard_map/all_to_all | solution.py:241
  39.6 3.3 %collective-permute-start.3 = (bf16[16,144,128]{2,1,0:T(8,128)(2,1)S(1)}, bf16[16,144,128]{2,1,0:T(8,128)(2,1)S(1)}, u32[]{:S(2)}, u32[]{:S(2)}) collective-permute-start(bf16[16,144,128]{2,1,0:T(8,128)(2,1)S(1)} %slice.120), channel_id=1, source_target_pairs={{0,1},{1,0},{2,3},{3,2},{4,5},{5,4},{6,7},{7,6},{8,9},{9,8},{10,11... | collective-permute-start | bytes 1769480 | tf_op jit(solution)/shard_map/ppermute | solution.py:264
  43.3 1.7 collective-permute-start.1
  45.0 2.9 %collective-permute-start.2 = (bf16[384,384]{1,0:T(8,128)(2,1)S(1)}, bf16[384,384]{1,0:T(8,128)(2,1)S(1)}, u32[]{:S(2)}, u32[]{:S(2)}) collective-permute-start(bf16[384,384]{1,0:T(8,128)(2,1)S(1)} %reshape.85.refs_0_), channel_id=1, source_target_pairs={{0,64},{32,96},{64,0},{96,32},{128,192},{160,224},{192,128},{224,1... | collective-permute-start | bytes 884744 | tf_op jit(solution)/shard_map/ppermute | solution.py:221
  48.3 2.3 %collective-permute-start.8 = (bf16[384,384]{1,0:T(8,128)(2,1)S(1)}, bf16[384,384]{1,0:T(8,128)(2,1)S(1)}, u32[]{:S(2)}, u32[]{:S(2)}) collective-permute-start(bf16[384,384]{1,0:T(8,128)(2,1)S(1)} %reshape.85.refs_0_), channel_id=1, source_target_pairs={{0,96},{32,0},{64,32},{96,64},{128,224},{160,128},{192,160},{224,1... | collective-permute-start | bytes 884744 | tf_op jit(solution)/shard_map/ppermute | solution.py:221
  51.0 3.6 %prepare.2 = (bf16[6,128,768]{2,1,0:T(8,128)(2,1)S(1)}, bf16[6,768,128]{2,1,0:T(8,128)(2,1)S(1)}, bf16[6,384,128]{2,1,0:T(8,128)(2,1)S(1)}, f32[6,384,128]{2,1,0:T(8,128)S(1)}) custom-call(bf16[6,768,128]{2,1,0:T(8,128)(2,1)S(1)} %bitcast.72, bf16[6,384,128]{2,1,0:T(8,128)(2,1)S(1)} %slice.121.xq_ref, f32[1,128]{1,0:T(1,128)S(1)} %get-tuple-element.66.gain_ref, ...), custom_call_target="tpu_custom_call" | custom-call | flops 4000000000 | bytes 6291456 | tf_op jit(solution)/shard_map/prepare/pallas_call | solution.py:65
  56.1 1.4 collective-permute-start.5
  58.7 3.1 %collective-permute-done.7.refs_1_ = bf16[384,384]{1,0:T(8,128)(2,1)S(1)} collective-permute-done((bf16[384,384]{1,0:T(8,128)(2,1)S(1)}, bf16[384,384]{1,0:T(8,128)(2,1)S(1)}, u32[]{:S(2)}, u32[]{:S(2)}) %collective-permute-start.7) | collective-permute-done | bytes 294944 | tf_op jit(solution)/shard_map/ppermute | solution.py:221
  61.7 8.0 %attend.4.refs_6_ = bf16[4,6,48,128]{3,2,1,0:T(8,128)(2,1)S(1)} custom-call(s32[4]{0:T(128)S(1)} %pad_add_fusion.1.blk_ref.done_blk_ref, s32[1]{0:T(128)} %bitcast.4.done_blk_ref, bf16[6,128,768]{2,1,0:T(8,128)(2,1)S(1)} %get-tuple-element.31.kt_ref, bf16[6,768,128]{2,1,0:T(8,128)(2,1)S(1)} %get-tuple-element.32.v_ref, ...), custom_call_target="tpu_custom_call" | custom-call | flops 11200000000 | bytes 6291456 | tf_op jit(solution)/shard_map/attend/pallas_call | solution.py:167
  69.8 10.4 %attend.5 = (bf16[6,384,128]{2,1,0:T(8,128)(2,1)S(1)}, bf16[6,8,384]{2,1,0:T(8,128)(2,1)S(1)}) custom-call(s32[4]{0:T(128)S(1)} %pad_add_fusion.blk_ref, s32[4]{0:T(128)S(1)} %pad_add_fusion.1.blk_ref.done_blk_ref, bf16[6,128,768]{2,1,0:T(8,128)(2,1)S(1)} %get-tuple-element.31.kt_ref, bf16[6,768,128]{2,1,0:T(8,128)(2,1)S(1)} %get-tuple-element.32.v_ref, ...), custom_call_target="tpu_custom_call" | custom-call | flops 11200000000 | bytes 6291456 | tf_op jit(solution)/shard_map/attend/pallas_call | solution.py:167
  82.0 39.2 %all_to_all.15 = bf16[128,32,128]{2,1,0:T(8,128)(2,1)S(1)} all-to-all(bf16[128,32,128]{2,1,0:T(8,128)(2,1)S(1)} %copy.35), channel_id=1, replica_groups={{0,2,4,6,8,10,12,14,16,18,20,22,24,26,28,30,32,34,36,38,40,42,44,46,48,..., dimensions={0} | all-to-all | bytes 2097152 | tf_op jit(solution)/shard_map/all_to_all | solution.py:289
  121.8 2.3 %collective-permute-start.11 = (bf16[3,768,128]{2,1,0:T(8,128)(2,1)S(1)}, bf16[3,768,128]{2,1,0:T(8,128)(2,1)S(1)}, u32[]{:S(2)}, u32[]{:S(2)}) collective-permute-start(bf16[3,768,128]{2,1,0:T(8,128)(2,1)S(1)} %bitcast.82), channel_id=1, source_target_pairs={{0,1},{1,0},{2,3},{3,2},{4,5},{5,4},{6,7},{7,6},{8,9},{9,8},{10,11... | collective-permute-start | bytes 1769480 | tf_op jit(solution)/shard_map/ppermute | solution.py:293
  126.4 2.3 %collective-permute-start.16 = (bf16[384,384]{1,0:T(8,128)(2,1)S(1)}, bf16[384,384]{1,0:T(8,128)(2,1)S(1)}, u32[]{:S(2)}, u32[]{:S(2)}) collective-permute-start(bf16[384,384]{1,0:T(8,128)(2,1)S(1)} %pad_maximum_fusion.4.refs_0_), channel_id=1, source_target_pairs={{0,96},{32,0},{64,32},{96,64},{128,224},{160,128},{192,160},{224,1... | collective-permute-start | bytes 884744 | tf_op jit(solution)/shard_map/ppermute | solution.py:221
  128.9 3.6 %prepare.3 = (bf16[6,128,768]{2,1,0:T(8,128)(2,1)S(1)}, bf16[6,768,128]{2,1,0:T(8,128)(2,1)S(1)}, bf16[6,384,128]{2,1,0:T(8,128)(2,1)S(1)}, f32[6,384,128]{2,1,0:T(8,128)S(1)}) custom-call(bf16[6,768,128]{2,1,0:T(8,128)(2,1)S(1)} %pad_maximum_fusion.1.x_ref, bf16[6,384,128]{2,1,0:T(8,128)(2,1)S(1)} %bitcast.73, ...), custom_call_target="tpu_custom_call" | custom-call | flops 4000000000 | bytes 6291456 | tf_op jit(solution)/shard_map/prepare/pallas_call | solution.py:65
  132.4 2.7 %collective-permute-done.10.refs_0_ = bf16[384,384]{1,0:T(8,128)(2,1)S(1)} collective-permute-done((bf16[384,384]{1,0:T(8,128)(2,1)S(1)}, bf16[384,384]{1,0:T(8,128)(2,1)S(1)}, u32[]{:S(2)}, u32[]{:S(2)}) %collective-permute-start.10) | collective-permute-done | bytes 294944 | tf_op jit(solution)/shard_map/ppermute | solution.py:221
  135.2 2.6 %collective-permute-start.13 = (bf16[384,384]{1,0:T(8,128)(2,1)S(1)}, bf16[384,384]{1,0:T(8,128)(2,1)S(1)}, u32[]{:S(2)}, u32[]{:S(2)}) collective-permute-start(bf16[384,384]{1,0:T(8,128)(2,1)S(1)} %collective-permute-done.9.refs_3_), channel_id=1, source_target_pairs={{0,96},{32,0},{64,32},{96,64},{128,224},{160,128},{192,160},{224,1... | collective-permute-start | bytes 884744 | tf_op jit(solution)/shard_map/ppermute | solution.py:221
  138.2 3.6 %collective-permute-done.15.refs_1_ = bf16[384,384]{1,0:T(8,128)(2,1)S(1)} collective-permute-done((bf16[384,384]{1,0:T(8,128)(2,1)S(1)}, bf16[384,384]{1,0:T(8,128)(2,1)S(1)}, u32[]{:S(2)}, u32[]{:S(2)}) %collective-permute-start.15) | collective-permute-done | bytes 294944 | tf_op jit(solution)/shard_map/ppermute | solution.py:221
  141.8 8.2 %attend.6.refs_6_ = bf16[4,6,48,128]{3,2,1,0:T(8,128)(2,1)S(1)} custom-call(s32[4]{0:T(128)S(1)} %pad_add_fusion.1.blk_ref.done_blk_ref, s32[1]{0:T(128)} %bitcast.4.done_blk_ref, bf16[6,128,768]{2,1,0:T(8,128)(2,1)S(1)} %get-tuple-element.43.kt_ref, bf16[6,768,128]{2,1,0:T(8,128)(2,1)S(1)} %get-tuple-element.44.v_ref, ...), custom_call_target="tpu_custom_call" | custom-call | flops 11200000000 | bytes 6291456 | tf_op jit(solution)/shard_map/attend/pallas_call | solution.py:167
  150.0 8.2 %attend.7 = bf16[6,384,128]{2,1,0:T(8,128)(2,1)S(1)} custom-call(s32[4]{0:T(128)S(1)} %pad_add_fusion.blk_ref, s32[4]{0:T(128)S(1)} %pad_add_fusion.1.blk_ref.done_blk_ref, bf16[6,128,768]{2,1,0:T(8,128)(2,1)S(1)} %get-tuple-element.43.kt_ref, bf16[6,768,128]{2,1,0:T(8,128)(2,1)S(1)} %get-tuple-element.44.v_ref, ...), custom_call_target="tpu_custom_call" | custom-call | flops 11200000000 | bytes 6291456 | tf_op jit(solution)/shard_map/attend/pallas_call | solution.py:167
  160.2 14.1 %all_to_all.16 = bf16[8,288,128]{2,1,0:T(8,128)(2,1)S(1)} all-to-all(bf16[8,288,128]{2,1,0:T(8,128)(2,1)S(1)} %bitcast.78), channel_id=1, replica_groups=mesh['row'=8,'col'=32] {'row'}, dimensions={0} | all-to-all | bytes 1179648 | tf_op jit(solution)/shard_map/all_to_all | solution.py:308
  (89 shorter events, 15.9 us)
Async XLA Ops:
  0.0 3.4 %copy-start = (bf16[96,24,128]{2,1,0:T(8,128)(2,1)S(1)}, bf16[96,24,128]{2,1,0:T(8,128)(2,1)}, u32[]{:S(2)}) copy-start(bf16[96,24,128]{2,1,0:T(8,128)(2,1)} %param.7) | copy-start | bytes 1769476
  0.0 3.4 %copy-start.6 = (bf16[2,128,4]{1,2,0:T(4,128)(2,1)S(1)}, bf16[2,128,4]{1,2,0:T(4,128)(2,1)}, u32[]{:S(2)}) copy-start(bf16[2,128,4]{1,2,0:T(4,128)(2,1)} %param.10) | copy-start | bytes 6148
  5.1 4.1 %collective-permute-start = (bf16[24,192]{1,0:T(8,128)(2,1)S(1)}, bf16[24,192]{1,0:T(8,128)(2,1)S(1)}, u32[]{:S(2)}, u32[]{:S(2)}) collective-permute-start(bf16[24,192]{1,0:T(8,128)(2,1)S(1)} %get-tuple-element.58), channel_id=1, source_target_pairs={{0,1},{1,0},{2,3},{3,2},{4,5},{5,4},{6,7},{7,6},{8,9},{9,8},{10,11... | collective-permute-start | bytes 27656 | tf_op jit(solution)/shard_map/ppermute | solution.py:257
  10.4 7.7 %copy-start.3 = (f32[2,128]{1,0:T(2,128)S(1)}, f32[2,128]{1,0:T(2,128)}, u32[]{:S(2)}) copy-start(f32[2,128]{1,0:T(2,128)} %param.13) | copy-start | bytes 3076
  10.4 32.7 %copy-start.2 = (bf16[2,128,128]{2,1,0:T(8,128)(2,1)S(1)}, bf16[2,128,128]{2,1,0:T(8,128)(2,1)}, u32[]{:S(2)}) copy-start(bf16[2,128,128]{2,1,0:T(8,128)(2,1)} %param.12) | copy-start | bytes 196612
  10.4 29.1 %all-to-all-start = ((bf16[16,216,128]{2,1,0:T(8,128)(2,1)}), bf16[16,216,128]{2,1,0:T(8,128)(2,1)S(1)}, u32[]{:S(2)}, u32[]{:S(2)}) async-start(bf16[16,216,128]{2,1,0:T(8,128)(2,1)} %pad_maximum_fusion.2), calls=%async_computation | async-start | bytes 1769472 | tf_op jit(solution)/shard_map/all_to_all | solution.py:241
  18.0 25.1 %copy-start.1 = (bf16[2,128,512]{2,1,0:T(8,128)(2,1)S(1)}, bf16[2,128,512]{2,1,0:T(8,128)(2,1)}, u32[]{:S(2)}) copy-start(bf16[2,128,512]{2,1,0:T(8,128)(2,1)} %param.9) | copy-start | bytes 786436
  39.6 11.0 %collective-permute-start.3 = (bf16[16,144,128]{2,1,0:T(8,128)(2,1)S(1)}, bf16[16,144,128]{2,1,0:T(8,128)(2,1)S(1)}, u32[]{:S(2)}, u32[]{:S(2)}) collective-permute-start(bf16[16,144,128]{2,1,0:T(8,128)(2,1)S(1)} %slice.120), channel_id=1, source_target_pairs={{0,1},{1,0},{2,3},{3,2},{4,5},{5,4},{6,7},{7,6},{8,9},{9,8},{10,11... | collective-permute-start | bytes 1769480 | tf_op jit(solution)/shard_map/ppermute | solution.py:264
  43.3 11.3 %collective-permute-start.1 = (bf16[384,384]{1,0:T(8,128)(2,1)S(1)}, bf16[384,384]{1,0:T(8,128)(2,1)S(1)}, u32[]{:S(2)}, u32[]{:S(2)}) collective-permute-start(bf16[384,384]{1,0:T(8,128)(2,1)S(1)} %reshape.85.refs_0_), channel_id=1, source_target_pairs={{0,144},{1,145},{2,146},{3,147},{4,148},{5,149},{6,150},{7,151},{8... | collective-permute-start | bytes 884744 | tf_op jit(solution)/shard_map/ppermute | solution.py:226
  45.0 9.9 %collective-permute-start.2 = (bf16[384,384]{1,0:T(8,128)(2,1)S(1)}, bf16[384,384]{1,0:T(8,128)(2,1)S(1)}, u32[]{:S(2)}, u32[]{:S(2)}) collective-permute-start(bf16[384,384]{1,0:T(8,128)(2,1)S(1)} %reshape.85.refs_0_), channel_id=1, source_target_pairs={{0,64},{32,96},{64,0},{96,32},{128,192},{160,224},{192,128},{224,1... | collective-permute-start | bytes 884744 | tf_op jit(solution)/shard_map/ppermute | solution.py:221
  47.9 13.8 %collective-permute-start.7 = (bf16[384,384]{1,0:T(8,128)(2,1)S(1)}, bf16[384,384]{1,0:T(8,128)(2,1)S(1)}, u32[]{:S(2)}, u32[]{:S(2)}) collective-permute-start(bf16[384,384]{1,0:T(8,128)(2,1)S(1)} %reshape.85.refs_0_), channel_id=1, source_target_pairs={{0,32},{32,64},{64,96},{96,0},{128,160},{160,192},{192,224},{224,1... | collective-permute-start | bytes 884744 | tf_op jit(solution)/shard_map/ppermute | solution.py:221
  48.3 13.4 %collective-permute-start.8 = (bf16[384,384]{1,0:T(8,128)(2,1)S(1)}, bf16[384,384]{1,0:T(8,128)(2,1)S(1)}, u32[]{:S(2)}, u32[]{:S(2)}) collective-permute-start(bf16[384,384]{1,0:T(8,128)(2,1)S(1)} %reshape.85.refs_0_), channel_id=1, source_target_pairs={{0,96},{32,0},{64,32},{96,64},{128,224},{160,128},{192,160},{224,1... | collective-permute-start | bytes 884744 | tf_op jit(solution)/shard_map/ppermute | solution.py:221
  54.8 15.0 %collective-permute-start.4 = (bf16[384,384]{1,0:T(8,128)(2,1)S(1)}, bf16[384,384]{1,0:T(8,128)(2,1)S(1)}, u32[]{:S(2)}, u32[]{:S(2)}) collective-permute-start(bf16[384,384]{1,0:T(8,128)(2,1)S(1)} %collective-permute-done.1.refs_3_), channel_id=1, source_target_pairs={{0,32},{32,64},{64,96},{96,0},{128,160},{160,192},{192,224},{224,1... | collective-permute-start | bytes 884744 | tf_op jit(solution)/shard_map/ppermute | solution.py:221
  56.1 13.7 %collective-permute-start.5 = (bf16[384,384]{1,0:T(8,128)(2,1)S(1)}, bf16[384,384]{1,0:T(8,128)(2,1)S(1)}, u32[]{:S(2)}, u32[]{:S(2)}) collective-permute-start(bf16[384,384]{1,0:T(8,128)(2,1)S(1)} %collective-permute-done.1.refs_3_), channel_id=1, source_target_pairs={{0,96},{32,0},{64,32},{96,64},{128,224},{160,128},{192,160},{224,1... | collective-permute-start | bytes 884744 | tf_op jit(solution)/shard_map/ppermute | solution.py:221
  57.6 12.2 %collective-permute-start.6 = (bf16[384,384]{1,0:T(8,128)(2,1)S(1)}, bf16[384,384]{1,0:T(8,128)(2,1)S(1)}, u32[]{:S(2)}, u32[]{:S(2)}) collective-permute-start(bf16[384,384]{1,0:T(8,128)(2,1)S(1)} %collective-permute-done.2.refs_0_), channel_id=1, source_target_pairs={{0,144},{1,145},{2,146},{3,147},{4,148},{5,149},{6,150},{7,151},{8... | collective-permute-start | bytes 884744 | tf_op jit(solution)/shard_map/ppermute | solution.py:226
  121.8 6.8 %collective-permute-start.11 = (bf16[3,768,128]{2,1,0:T(8,128)(2,1)S(1)}, bf16[3,768,128]{2,1,0:T(8,128)(2,1)S(1)}, u32[]{:S(2)}, u32[]{:S(2)}) collective-permute-start(bf16[3,768,128]{2,1,0:T(8,128)(2,1)S(1)} %bitcast.82), channel_id=1, source_target_pairs={{0,1},{1,0},{2,3},{3,2},{4,5},{5,4},{6,7},{7,6},{8,9},{9,8},{10,11... | collective-permute-start | bytes 1769480 | tf_op jit(solution)/shard_map/ppermute | solution.py:293
  124.9 10.3 %collective-permute-start.10 = (bf16[384,384]{1,0:T(8,128)(2,1)S(1)}, bf16[384,384]{1,0:T(8,128)(2,1)S(1)}, u32[]{:S(2)}, u32[]{:S(2)}) collective-permute-start(bf16[384,384]{1,0:T(8,128)(2,1)S(1)} %pad_maximum_fusion.4.refs_0_), channel_id=1, source_target_pairs={{0,64},{32,96},{64,0},{96,32},{128,192},{160,224},{192,128},{224,1... | collective-permute-start | bytes 884744 | tf_op jit(solution)/shard_map/ppermute | solution.py:221
  125.0 10.2 %collective-permute-start.9 = (bf16[384,384]{1,0:T(8,128)(2,1)S(1)}, bf16[384,384]{1,0:T(8,128)(2,1)S(1)}, u32[]{:S(2)}, u32[]{:S(2)}) collective-permute-start(bf16[384,384]{1,0:T(8,128)(2,1)S(1)} %pad_maximum_fusion.4.refs_0_), channel_id=1, source_target_pairs={{0,144},{1,145},{2,146},{3,147},{4,148},{5,149},{6,150},{7,151},{8... | collective-permute-start | bytes 884744 | tf_op jit(solution)/shard_map/ppermute | solution.py:226
  126.0 15.8 %collective-permute-start.15 = (bf16[384,384]{1,0:T(8,128)(2,1)S(1)}, bf16[384,384]{1,0:T(8,128)(2,1)S(1)}, u32[]{:S(2)}, u32[]{:S(2)}) collective-permute-start(bf16[384,384]{1,0:T(8,128)(2,1)S(1)} %pad_maximum_fusion.4.refs_0_), channel_id=1, source_target_pairs={{0,32},{32,64},{64,96},{96,0},{128,160},{160,192},{192,224},{224,1... | collective-permute-start | bytes 884744 | tf_op jit(solution)/shard_map/ppermute | solution.py:221
  126.4 15.4 %collective-permute-start.16 = (bf16[384,384]{1,0:T(8,128)(2,1)S(1)}, bf16[384,384]{1,0:T(8,128)(2,1)S(1)}, u32[]{:S(2)}, u32[]{:S(2)}) collective-permute-start(bf16[384,384]{1,0:T(8,128)(2,1)S(1)} %pad_maximum_fusion.4.refs_0_), channel_id=1, source_target_pairs={{0,96},{32,0},{64,32},{96,64},{128,224},{160,128},{192,160},{224,1... | collective-permute-start | bytes 884744 | tf_op jit(solution)/shard_map/ppermute | solution.py:221
  135.2 14.8 %collective-permute-start.12 = (bf16[384,384]{1,0:T(8,128)(2,1)S(1)}, bf16[384,384]{1,0:T(8,128)(2,1)S(1)}, u32[]{:S(2)}, u32[]{:S(2)}) collective-permute-start(bf16[384,384]{1,0:T(8,128)(2,1)S(1)} %collective-permute-done.9.refs_3_), channel_id=1, source_target_pairs={{0,32},{32,64},{64,96},{96,0},{128,160},{160,192},{192,224},{224,1... | collective-permute-start | bytes 884744 | tf_op jit(solution)/shard_map/ppermute | solution.py:221
  135.2 14.7 %collective-permute-start.13 = (bf16[384,384]{1,0:T(8,128)(2,1)S(1)}, bf16[384,384]{1,0:T(8,128)(2,1)S(1)}, u32[]{:S(2)}, u32[]{:S(2)}) collective-permute-start(bf16[384,384]{1,0:T(8,128)(2,1)S(1)} %collective-permute-done.9.refs_3_), channel_id=1, source_target_pairs={{0,96},{32,0},{64,32},{96,64},{128,224},{160,128},{192,160},{224,1... | collective-permute-start | bytes 884744 | tf_op jit(solution)/shard_map/ppermute | solution.py:221
  137.9 12.1 %collective-permute-start.14 = (bf16[384,384]{1,0:T(8,128)(2,1)S(1)}, bf16[384,384]{1,0:T(8,128)(2,1)S(1)}, u32[]{:S(2)}, u32[]{:S(2)}) collective-permute-start(bf16[384,384]{1,0:T(8,128)(2,1)S(1)} %collective-permute-done.10.refs_0_), channel_id=1, source_target_pairs={{0,144},{1,145},{2,146},{3,147},{4,148},{5,149},{6,150},{7,151},{8... | collective-permute-start | bytes 884744 | tf_op jit(solution)/shard_map/ppermute | solution.py:226
  158.2 1.9 %collective-permute-start.17 = (bf16[3,384,128]{2,1,0:T(8,128)(2,1)S(1)}, bf16[3,384,128]{2,1,0:T(8,128)(2,1)S(1)}, u32[]{:S(2)}, u32[]{:S(2)}) collective-permute-start(bf16[3,384,128]{2,1,0:T(8,128)(2,1)S(1)} %slice.128), channel_id=1, source_target_pairs={{0,1},{1,0},{2,3},{3,2},{4,5},{5,4},{6,7},{7,6},{8,9},{9,8},{10,11... | collective-permute-start | bytes 884744 | tf_op jit(solution)/shard_map/ppermute | solution.py:305
  (2 other events, 6.7 us)

commit v6 on v5

--- a/solution.py
+++ b/solution.py
@@ -11,7 +11,7 @@
 WIDTH = 32
 CH = 128
 LOG2E = 1.4426950408889634
-CALLS = (4, 4)
+CALLS = (3, 5)
 NT = (((1,), (1,)), ((), ()))
 
 
@@ -161,7 +161,7 @@
     out = [jax.ShapeDtypeStruct(shape, jnp.bfloat16)]
     out_specs = [by_pair(out[0]) if whole_out else by_block(out[0])]
     if following:
-        out.append(jax.ShapeDtypeStruct((nrow, 8, xq.shape[1]), jnp.bfloat16))
+        out.append(jax.ShapeDtypeStruct((nrow, 16, xq.shape[1]), jnp.bfloat16))
         out_specs.append(by_pair(out[1]))
     small = [wo, ob[None]]
     return pl.pallas_call(
@@ -231,9 +231,9 @@
     def spread_on(bias, first, parts):
         near, far, over, two = first
         over, two, parts = lax.optimization_barrier((over, two, parts))
-        got = [bias, near, far, over, two, along_y(over, 1), along_y(over, 3), to_neighbour(two)]
+        got = [bias, over, two, near, far, along_y(over, 1), along_y(over, 3), to_neighbour(two)]
         x, y = lax.axis_index("row") // ny, lax.axis_index("row") % ny
-        turns = ((0, 0), (0, 1), (0, 3), (1, 0), (0, 2), (1, 1), (1, 3), (1, 2))
+        turns = ((0, 0), (1, 0), (0, 2), (0, 1), (0, 3), (1, 1), (1, 3), (1, 2))
         ids = [(x ^ dx) * ny + (y + ny - dy) % ny for dx, dy in turns]
         return got, jnp.stack(ids).astype(jnp.int32), parts
 
@@ -266,7 +266,7 @@
         first_biases = spread(bias)
         x = jnp.stack([x_own, x_other]).reshape(2, ng, nrow, ncol, CH)
         x = x.transpose(2, 0, 1, 3, 4).reshape(nrow, keys, CH)
-        following = [norm_gain[1][None], jnp.pad(w_bias[1].T, ((0, 8 - HEADS), (0, 0)))]
+        following = [norm_gain[1][None], jnp.pad(w_bias[1].T, ((0, 16 - HEADS), (0, 0)))]
         xq = x[:, :half]
         parts = prepare(x, xq, norm_gain[0], w_proj[0], gate_bias[0])
         biases, ids, parts = spread_on(bias, first_biases, parts)

time: 176 us -> 175 us (level)
  transfers between devices with their start and end apart: 19 -> 19, of which waited for: 7 -> 7; matrix products, arithmetic and copies ran while one was open for 1% -> 1% of each run, Pallas kernels for 13% -> 12%
where the time goes in v6:
time: 175 us
  blocking collectives  53.5 us (31%)
  Pallas kernels  42.8 us (24%)
  starting transfers between devices  34.7 us (20%)
  waiting for transfers between devices  31.9 us (18%)
  local copies, waits for them, and re-layouts  5.09 us (3%)
  other arithmetic  5.07 us (3%)
    all_to_all x1, blocking collectives, per_device(): lax.all_to_all(message, ('row', 'col'), 0, 0, tiled=True, axis_index_grou...  39.4 us
    pallas_call x4, Pallas kernels, attend(): pl.pallas_call(functools.partial(attention_kernel, nblk, len(done), stack...  35.7 us
    all_to_all x1, waiting for transfers between devices, all_to_all_16(): lax.all_to_all(message, 'col', 0, 0, tiled=True, axis_index_groups=same_c...  21.4 us
    all_to_all x1, blocking collectives, per_device(): got = lax.all_to_all(both.reshape(nr, -1, CH), 'row', 0, 0, tiled=True)  14.1 us
    ppermute x10, starting transfers between devices, along_y(): lax.ppermute(block, 'row', [(i, i // ny * ny + (i + dy) % ny) for i in ra...  13.8 us
    ppermute x10, waiting for transfers between devices, along_y(): lax.ppermute(block, 'row', [(i, i // ny * ny + (i + dy) % ny) for i in ra...  8.42 us
    all_to_all x1, starting transfers between devices, all_to_all_16(): lax.all_to_all(message, 'col', 0, 0, tiled=True, axis_index_groups=same_c...  7.63 us
    pallas_call x2, Pallas kernels, prepare(): pl.pallas_call(prepare_kernel, grid=(nrow,), in_specs=[by_row(x), by_row(...  7.13 us
  transfers between devices with their start and end apart: 19, of which 7 were waited for; matrix products, arithmetic and copies ran while one was open for 1% of the time, Pallas kernels for 12%

profile of v6, /device:TPU:1, one launch (start us, length us, event | category | flops | bytes accessed | tf_op | source)
XLA Modules:
  0.0 175.0 jit_solution(4091013863470881471)
XLA Ops:
  0.0 1.5 convert_reduce_fusion
  1.6 1.8 %fusion.2 = f32[96,24]{1,0:T(8,128)S(1)} fusion(bf16[96,24,128]{2,1,0:T(8,128)(2,1)} %param.7, f32[96,24]{1,0:T(8,128)S(1)} %broadcast_multiply_fusion), kind=kLoop, calls=%fused_computation.4 | loop fusion | flops 1177344 | bytes 608256 | tf_op jit(solution)/shard_map/reduce_sum | solution.py:21
  5.1 3.3 %collective-permute-start = (bf16[24,192]{1,0:T(8,128)(2,1)S(1)}, bf16[24,192]{1,0:T(8,128)(2,1)S(1)}, u32[]{:S(2)}, u32[]{:S(2)}) collective-permute-start(bf16[24,192]{1,0:T(8,128)(2,1)S(1)} %get-tuple-element.58), channel_id=1, source_target_pairs={{0,1},{1,0},{2,3},{3,2},{4,5},{5,4},{6,7},{7,6},{8,9},{9,8},{10,11... | collective-permute-start | bytes 27656 | tf_op jit(solution)/shard_map/ppermute | solution.py:257
  10.4 7.6 %all-to-all-start = ((bf16[16,216,128]{2,1,0:T(8,128)(2,1)}), bf16[16,216,128]{2,1,0:T(8,128)(2,1)S(1)}, u32[]{:S(2)}, u32[]{:S(2)}) async-start(bf16[16,216,128]{2,1,0:T(8,128)(2,1)} %pad_maximum_fusion.2), calls=%async_computation | async-start | bytes 1769472 | tf_op jit(solution)/shard_map/all_to_all | solution.py:241
  18.1 21.4 %all-to-all-done = bf16[16,216,128]{2,1,0:T(8,128)(2,1)S(1)} async-done(((bf16[16,216,128]{2,1,0:T(8,128)(2,1)}), bf16[16,216,128]{2,1,0:T(8,128)(2,1)S(1)}, u32[]{:S(2)}, u32[]{:S(2)}) %all-to-all-start) | async-done | bytes 884768 | tf_op jit(solution)/shard_map/all_to_all | solution.py:241
  39.6 3.3 %collective-permute-start.3 = (bf16[16,144,128]{2,1,0:T(8,128)(2,1)S(1)}, bf16[16,144,128]{2,1,0:T(8,128)(2,1)S(1)}, u32[]{:S(2)}, u32[]{:S(2)}) collective-permute-start(bf16[16,144,128]{2,1,0:T(8,128)(2,1)S(1)} %slice.120), channel_id=1, source_target_pairs={{0,1},{1,0},{2,3},{3,2},{4,5},{5,4},{6,7},{7,6},{8,9},{9,8},{10,11... | collective-permute-start | bytes 1769480 | tf_op jit(solution)/shard_map/ppermute | solution.py:264
  43.3 1.7 collective-permute-start.1
  45.0 2.9 %collective-permute-start.2 = (bf16[384,384]{1,0:T(8,128)(2,1)S(1)}, bf16[384,384]{1,0:T(8,128)(2,1)S(1)}, u32[]{:S(2)}, u32[]{:S(2)}) collective-permute-start(bf16[384,384]{1,0:T(8,128)(2,1)S(1)} %reshape.85.refs_0_), channel_id=1, source_target_pairs={{0,64},{32,96},{64,0},{96,32},{128,192},{160,224},{192,128},{224,1... | collective-permute-start | bytes 884744 | tf_op jit(solution)/shard_map/ppermute | solution.py:221
  48.3 2.3 %collective-permute-start.5 = (bf16[384,384]{1,0:T(8,128)(2,1)S(1)}, bf16[384,384]{1,0:T(8,128)(2,1)S(1)}, u32[]{:S(2)}, u32[]{:S(2)}) collective-permute-start(bf16[384,384]{1,0:T(8,128)(2,1)S(1)} %reshape.85.refs_0_), channel_id=1, source_target_pairs={{0,96},{32,0},{64,32},{96,64},{128,224},{160,128},{192,160},{224,1... | collective-permute-start | bytes 884744 | tf_op jit(solution)/shard_map/ppermute | solution.py:221
  51.1 3.6 %prepare.2 = (bf16[6,128,768]{2,1,0:T(8,128)(2,1)S(1)}, bf16[6,768,128]{2,1,0:T(8,128)(2,1)S(1)}, bf16[6,384,128]{2,1,0:T(8,128)(2,1)S(1)}, f32[6,384,128]{2,1,0:T(8,128)S(1)}) custom-call(bf16[6,768,128]{2,1,0:T(8,128)(2,1)S(1)} %bitcast.72, bf16[6,384,128]{2,1,0:T(8,128)(2,1)S(1)} %slice.121.xq_ref, f32[1,128]{1,0:T(1,128)S(1)} %get-tuple-element.66.gain_ref, ...), custom_call_target="tpu_custom_call" | custom-call | flops 4000000000 | bytes 6291456 | tf_op jit(solution)/shard_map/prepare/pallas_call | solution.py:65
  56.1 1.4 collective-permute-start.7
  58.6 6.8 %attend.4.refs_7_ = bf16[3,6,48,128]{3,2,1,0:T(8,128)(2,1)S(1)} custom-call(s32[3]{0:T(128)S(1)} %pad_add_fusion.blk_ref.done_blk_ref, s32[1]{0:T(128)} %bitcast.5.done_blk_ref, bf16[6,128,768]{2,1,0:T(8,128)(2,1)S(1)} %get-tuple-element.31.kt_ref, bf16[6,768,128]{2,1,0:T(8,128)(2,1)S(1)} %get-tuple-element.32.v_ref, ...), custom_call_target="tpu_custom_call" | custom-call | flops 8400000000 | bytes 6291456 | tf_op jit(solution)/shard_map/attend/pallas_call | solution.py:167
  65.5 2.6 %collective-permute-done.6.refs_2_ = bf16[384,384]{1,0:T(8,128)(2,1)S(1)} collective-permute-done((bf16[384,384]{1,0:T(8,128)(2,1)S(1)}, bf16[384,384]{1,0:T(8,128)(2,1)S(1)}, u32[]{:S(2)}, u32[]{:S(2)}) %collective-permute-start.6) | collective-permute-done | bytes 294944 | tf_op jit(solution)/shard_map/ppermute | solution.py:221
  68.1 11.9 %attend.5 = (bf16[6,384,128]{2,1,0:T(8,128)(2,1)S(1)}, bf16[6,16,384]{2,1,0:T(8,128)(2,1)S(1)}) custom-call(s32[5]{0:T(128)S(1)} %stack.61.blk_ref, s32[3]{0:T(128)S(1)} %pad_add_fusion.blk_ref.done_blk_ref, bf16[6,128,768]{2,1,0:T(8,128)(2,1)S(1)} %get-tuple-element.31.kt_ref, bf16[6,768,128]{2,1,0:T(8,128)(2,1)S(1)} %get-tuple-element.32.v_ref, ...), custom_call_target="tpu_custom_call" | custom-call | flops 14000000000 | bytes 6291456 | tf_op jit(solution)/shard_map/attend/pallas_call | solution.py:167
  81.8 39.4 %all_to_all.15 = bf16[128,32,128]{2,1,0:T(8,128)(2,1)S(1)} all-to-all(bf16[128,32,128]{2,1,0:T(8,128)(2,1)S(1)} %copy.35), channel_id=1, replica_groups={{0,2,4,6,8,10,12,14,16,18,20,22,24,26,28,30,32,34,36,38,40,42,44,46,48,..., dimensions={0} | all-to-all | bytes 2097152 | tf_op jit(solution)/shard_map/all_to_all | solution.py:289
  121.8 2.1 %collective-permute-start.11 = (bf16[3,768,128]{2,1,0:T(8,128)(2,1)S(1)}, bf16[3,768,128]{2,1,0:T(8,128)(2,1)S(1)}, u32[]{:S(2)}, u32[]{:S(2)}) collective-permute-start(bf16[3,768,128]{2,1,0:T(8,128)(2,1)S(1)} %bitcast.82), channel_id=1, source_target_pairs={{0,1},{1,0},{2,3},{3,2},{4,5},{5,4},{6,7},{7,6},{8,9},{9,8},{10,11... | collective-permute-start | bytes 1769480 | tf_op jit(solution)/shard_map/ppermute | solution.py:293
  126.1 2.3 %collective-permute-start.13 = (bf16[384,384]{1,0:T(8,128)(2,1)S(1)}, bf16[384,384]{1,0:T(8,128)(2,1)S(1)}, u32[]{:S(2)}, u32[]{:S(2)}) collective-permute-start(bf16[384,384]{1,0:T(8,128)(2,1)S(1)} %pad_maximum_fusion.4.refs_0_), channel_id=1, source_target_pairs={{0,96},{32,0},{64,32},{96,64},{128,224},{160,128},{192,160},{224,1... | collective-permute-start | bytes 884744 | tf_op jit(solution)/shard_map/ppermute | solution.py:221
  128.6 3.6 %prepare.3 = (bf16[6,128,768]{2,1,0:T(8,128)(2,1)S(1)}, bf16[6,768,128]{2,1,0:T(8,128)(2,1)S(1)}, bf16[6,384,128]{2,1,0:T(8,128)(2,1)S(1)}, f32[6,384,128]{2,1,0:T(8,128)S(1)}) custom-call(bf16[6,768,128]{2,1,0:T(8,128)(2,1)S(1)} %pad_maximum_fusion.1.x_ref, bf16[6,384,128]{2,1,0:T(8,128)(2,1)S(1)} %bitcast.73, ...), custom_call_target="tpu_custom_call" | custom-call | flops 4000000000 | bytes 6291456 | tf_op jit(solution)/shard_map/prepare/pallas_call | solution.py:65
  132.2 2.8 %collective-permute-done.10.refs_2_ = bf16[384,384]{1,0:T(8,128)(2,1)S(1)} collective-permute-done((bf16[384,384]{1,0:T(8,128)(2,1)S(1)}, bf16[384,384]{1,0:T(8,128)(2,1)S(1)}, u32[]{:S(2)}, u32[]{:S(2)}) %collective-permute-start.10) | collective-permute-done | bytes 294944 | tf_op jit(solution)/shard_map/ppermute | solution.py:221
  135.0 2.6 %collective-permute-start.15 = (bf16[384,384]{1,0:T(8,128)(2,1)S(1)}, bf16[384,384]{1,0:T(8,128)(2,1)S(1)}, u32[]{:S(2)}, u32[]{:S(2)}) collective-permute-start(bf16[384,384]{1,0:T(8,128)(2,1)S(1)} %collective-permute-done.9.refs_1_), channel_id=1, source_target_pairs={{0,96},{32,0},{64,32},{96,64},{128,224},{160,128},{192,160},{224,1... | collective-permute-start | bytes 884744 | tf_op jit(solution)/shard_map/ppermute | solution.py:221
  137.9 7.0 %attend.6.refs_7_ = bf16[3,6,48,128]{3,2,1,0:T(8,128)(2,1)S(1)} custom-call(s32[3]{0:T(128)S(1)} %pad_add_fusion.blk_ref.done_blk_ref, s32[1]{0:T(128)} %bitcast.5.done_blk_ref, bf16[6,128,768]{2,1,0:T(8,128)(2,1)S(1)} %get-tuple-element.43.kt_ref, bf16[6,768,128]{2,1,0:T(8,128)(2,1)S(1)} %get-tuple-element.44.v_ref, ...), custom_call_target="tpu_custom_call" | custom-call | flops 8400000000 | bytes 6291456 | tf_op jit(solution)/shard_map/attend/pallas_call | solution.py:167
  145.0 2.9 %collective-permute-done.14.refs_2_ = bf16[384,384]{1,0:T(8,128)(2,1)S(1)} collective-permute-done((bf16[384,384]{1,0:T(8,128)(2,1)S(1)}, bf16[384,384]{1,0:T(8,128)(2,1)S(1)}, u32[]{:S(2)}, u32[]{:S(2)}) %collective-permute-start.14) | collective-permute-done | bytes 294944 | tf_op jit(solution)/shard_map/ppermute | solution.py:221
  147.8 10.1 %attend.7 = bf16[6,384,128]{2,1,0:T(8,128)(2,1)S(1)} custom-call(s32[5]{0:T(128)S(1)} %stack.61.blk_ref, s32[3]{0:T(128)S(1)} %pad_add_fusion.blk_ref.done_blk_ref, bf16[6,128,768]{2,1,0:T(8,128)(2,1)S(1)} %get-tuple-element.43.kt_ref, bf16[6,768,128]{2,1,0:T(8,128)(2,1)S(1)} %get-tuple-element.44.v_ref, bf16[6,384,128]{2,1,0:T(8,128)(2,1)S(1)} %get-tuple-element.45.q_ref, ...), custom_call_target="tpu_custom_call" | custom-call | flops 14000000000 | bytes 6291456 | tf_op jit(solution)/shard_map/attend/pallas_call | solution.py:167
  159.9 14.1 %all_to_all.16 = bf16[8,288,128]{2,1,0:T(8,128)(2,1)S(1)} all-to-all(bf16[8,288,128]{2,1,0:T(8,128)(2,1)S(1)} %bitcast.78), channel_id=1, replica_groups=mesh['row'=8,'col'=32] {'row'}, dimensions={0} | all-to-all | bytes 1179648 | tf_op jit(solution)/shard_map/all_to_all | solution.py:308
  (89 shorter events, 15.8 us)
Async XLA Ops:
  0.0 3.4 %copy-start = (bf16[96,24,128]{2,1,0:T(8,128)(2,1)S(1)}, bf16[96,24,128]{2,1,0:T(8,128)(2,1)}, u32[]{:S(2)}) copy-start(bf16[96,24,128]{2,1,0:T(8,128)(2,1)} %param.7) | copy-start | bytes 1769476
  0.0 3.4 %copy-start.6 = (bf16[2,128,4]{1,2,0:T(4,128)(2,1)S(1)}, bf16[2,128,4]{1,2,0:T(4,128)(2,1)}, u32[]{:S(2)}) copy-start(bf16[2,128,4]{1,2,0:T(4,128)(2,1)} %param.10) | copy-start | bytes 6148
  5.1 4.1 %collective-permute-start = (bf16[24,192]{1,0:T(8,128)(2,1)S(1)}, bf16[24,192]{1,0:T(8,128)(2,1)S(1)}, u32[]{:S(2)}, u32[]{:S(2)}) collective-permute-start(bf16[24,192]{1,0:T(8,128)(2,1)S(1)} %get-tuple-element.58), channel_id=1, source_target_pairs={{0,1},{1,0},{2,3},{3,2},{4,5},{5,4},{6,7},{7,6},{8,9},{9,8},{10,11... | collective-permute-start | bytes 27656 | tf_op jit(solution)/shard_map/ppermute | solution.py:257
  10.4 32.4 %copy-start.3 = (f32[2,128]{1,0:T(2,128)S(1)}, f32[2,128]{1,0:T(2,128)}, u32[]{:S(2)}) copy-start(f32[2,128]{1,0:T(2,128)} %param.13) | copy-start | bytes 3076
  10.4 32.7 %copy-start.2 = (bf16[2,128,128]{2,1,0:T(8,128)(2,1)S(1)}, bf16[2,128,128]{2,1,0:T(8,128)(2,1)}, u32[]{:S(2)}) copy-start(bf16[2,128,128]{2,1,0:T(8,128)(2,1)} %param.12) | copy-start | bytes 196612
  10.4 29.1 %all-to-all-start = ((bf16[16,216,128]{2,1,0:T(8,128)(2,1)}), bf16[16,216,128]{2,1,0:T(8,128)(2,1)S(1)}, u32[]{:S(2)}, u32[]{:S(2)}) async-start(bf16[16,216,128]{2,1,0:T(8,128)(2,1)} %pad_maximum_fusion.2), calls=%async_computation | async-start | bytes 1769472 | tf_op jit(solution)/shard_map/all_to_all | solution.py:241
  18.0 25.1 %copy-start.1 = (bf16[2,128,512]{2,1,0:T(8,128)(2,1)S(1)}, bf16[2,128,512]{2,1,0:T(8,128)(2,1)}, u32[]{:S(2)}) copy-start(bf16[2,128,512]{2,1,0:T(8,128)(2,1)} %param.9) | copy-start | bytes 786436
  39.6 11.1 %collective-permute-start.3 = (bf16[16,144,128]{2,1,0:T(8,128)(2,1)S(1)}, bf16[16,144,128]{2,1,0:T(8,128)(2,1)S(1)}, u32[]{:S(2)}, u32[]{:S(2)}) collective-permute-start(bf16[16,144,128]{2,1,0:T(8,128)(2,1)S(1)} %slice.120), channel_id=1, source_target_pairs={{0,1},{1,0},{2,3},{3,2},{4,5},{5,4},{6,7},{7,6},{8,9},{9,8},{10,11... | collective-permute-start | bytes 1769480 | tf_op jit(solution)/shard_map/ppermute | solution.py:264
  43.3 11.3 %collective-permute-start.1 = (bf16[384,384]{1,0:T(8,128)(2,1)S(1)}, bf16[384,384]{1,0:T(8,128)(2,1)S(1)}, u32[]{:S(2)}, u32[]{:S(2)}) collective-permute-start(bf16[384,384]{1,0:T(8,128)(2,1)S(1)} %reshape.85.refs_0_), channel_id=1, source_target_pairs={{0,144},{1,145},{2,146},{3,147},{4,148},{5,149},{6,150},{7,151},{8... | collective-permute-start | bytes 884744 | tf_op jit(solution)/shard_map/ppermute | solution.py:226
  45.0 9.8 %collective-permute-start.2 = (bf16[384,384]{1,0:T(8,128)(2,1)S(1)}, bf16[384,384]{1,0:T(8,128)(2,1)S(1)}, u32[]{:S(2)}, u32[]{:S(2)}) collective-permute-start(bf16[384,384]{1,0:T(8,128)(2,1)S(1)} %reshape.85.refs_0_), channel_id=1, source_target_pairs={{0,64},{32,96},{64,0},{96,32},{128,192},{160,224},{192,128},{224,1... | collective-permute-start | bytes 884744 | tf_op jit(solution)/shard_map/ppermute | solution.py:221
  47.9 17.5 %collective-permute-start.4 = (bf16[384,384]{1,0:T(8,128)(2,1)S(1)}, bf16[384,384]{1,0:T(8,128)(2,1)S(1)}, u32[]{:S(2)}, u32[]{:S(2)}) collective-permute-start(bf16[384,384]{1,0:T(8,128)(2,1)S(1)} %reshape.85.refs_0_), channel_id=1, source_target_pairs={{0,32},{32,64},{64,96},{96,0},{128,160},{160,192},{192,224},{224,1... | collective-permute-start | bytes 884744 | tf_op jit(solution)/shard_map/ppermute | solution.py:221
  48.3 17.1 %collective-permute-start.5 = (bf16[384,384]{1,0:T(8,128)(2,1)S(1)}, bf16[384,384]{1,0:T(8,128)(2,1)S(1)}, u32[]{:S(2)}, u32[]{:S(2)}) collective-permute-start(bf16[384,384]{1,0:T(8,128)(2,1)S(1)} %reshape.85.refs_0_), channel_id=1, source_target_pairs={{0,96},{32,0},{64,32},{96,64},{128,224},{160,128},{192,160},{224,1... | collective-permute-start | bytes 884744 | tf_op jit(solution)/shard_map/ppermute | solution.py:221
  54.8 13.3 %collective-permute-start.6 = (bf16[384,384]{1,0:T(8,128)(2,1)S(1)}, bf16[384,384]{1,0:T(8,128)(2,1)S(1)}, u32[]{:S(2)}, u32[]{:S(2)}) collective-permute-start(bf16[384,384]{1,0:T(8,128)(2,1)S(1)} %collective-permute-done.1.refs_1_), channel_id=1, source_target_pairs={{0,32},{32,64},{64,96},{96,0},{128,160},{160,192},{192,224},{224,1... | collective-permute-start | bytes 884744 | tf_op jit(solution)/shard_map/ppermute | solution.py:221
  56.1 12.0 %collective-permute-start.7 = (bf16[384,384]{1,0:T(8,128)(2,1)S(1)}, bf16[384,384]{1,0:T(8,128)(2,1)S(1)}, u32[]{:S(2)}, u32[]{:S(2)}) collective-permute-start(bf16[384,384]{1,0:T(8,128)(2,1)S(1)} %collective-permute-done.1.refs_1_), channel_id=1, source_target_pairs={{0,96},{32,0},{64,32},{96,64},{128,224},{160,128},{192,160},{224,1... | collective-permute-start | bytes 884744 | tf_op jit(solution)/shard_map/ppermute | solution.py:221
  57.5 10.6 %collective-permute-start.8 = (bf16[384,384]{1,0:T(8,128)(2,1)S(1)}, bf16[384,384]{1,0:T(8,128)(2,1)S(1)}, u32[]{:S(2)}, u32[]{:S(2)}) collective-permute-start(bf16[384,384]{1,0:T(8,128)(2,1)S(1)} %collective-permute-done.2.refs_2_), channel_id=1, source_target_pairs={{0,144},{1,145},{2,146},{3,147},{4,148},{5,149},{6,150},{7,151},{8... | collective-permute-start | bytes 884744 | tf_op jit(solution)/shard_map/ppermute | solution.py:226
  121.8 6.6 %collective-permute-start.11 = (bf16[3,768,128]{2,1,0:T(8,128)(2,1)S(1)}, bf16[3,768,128]{2,1,0:T(8,128)(2,1)S(1)}, u32[]{:S(2)}, u32[]{:S(2)}) collective-permute-start(bf16[3,768,128]{2,1,0:T(8,128)(2,1)S(1)} %bitcast.82), channel_id=1, source_target_pairs={{0,1},{1,0},{2,3},{3,2},{4,5},{5,4},{6,7},{7,6},{8,9},{9,8},{10,11... | collective-permute-start | bytes 1769480 | tf_op jit(solution)/shard_map/ppermute | solution.py:293
  124.7 10.3 %collective-permute-start.10 = (bf16[384,384]{1,0:T(8,128)(2,1)S(1)}, bf16[384,384]{1,0:T(8,128)(2,1)S(1)}, u32[]{:S(2)}, u32[]{:S(2)}) collective-permute-start(bf16[384,384]{1,0:T(8,128)(2,1)S(1)} %pad_maximum_fusion.4.refs_0_), channel_id=1, source_target_pairs={{0,64},{32,96},{64,0},{96,32},{128,192},{160,224},{192,128},{224,1... | collective-permute-start | bytes 884744 | tf_op jit(solution)/shard_map/ppermute | solution.py:221
  124.8 10.2 %collective-permute-start.9 = (bf16[384,384]{1,0:T(8,128)(2,1)S(1)}, bf16[384,384]{1,0:T(8,128)(2,1)S(1)}, u32[]{:S(2)}, u32[]{:S(2)}) collective-permute-start(bf16[384,384]{1,0:T(8,128)(2,1)S(1)} %pad_maximum_fusion.4.refs_0_), channel_id=1, source_target_pairs={{0,144},{1,145},{2,146},{3,147},{4,148},{5,149},{6,150},{7,151},{8... | collective-permute-start | bytes 884744 | tf_op jit(solution)/shard_map/ppermute | solution.py:226
  125.7 19.2 %collective-permute-start.12 = (bf16[384,384]{1,0:T(8,128)(2,1)S(1)}, bf16[384,384]{1,0:T(8,128)(2,1)S(1)}, u32[]{:S(2)}, u32[]{:S(2)}) collective-permute-start(bf16[384,384]{1,0:T(8,128)(2,1)S(1)} %pad_maximum_fusion.4.refs_0_), channel_id=1, source_target_pairs={{0,32},{32,64},{64,96},{96,0},{128,160},{160,192},{192,224},{224,1... | collective-permute-start | bytes 884744 | tf_op jit(solution)/shard_map/ppermute | solution.py:221
  126.1 18.8 %collective-permute-start.13 = (bf16[384,384]{1,0:T(8,128)(2,1)S(1)}, bf16[384,384]{1,0:T(8,128)(2,1)S(1)}, u32[]{:S(2)}, u32[]{:S(2)}) collective-permute-start(bf16[384,384]{1,0:T(8,128)(2,1)S(1)} %pad_maximum_fusion.4.refs_0_), channel_id=1, source_target_pairs={{0,96},{32,0},{64,32},{96,64},{128,224},{160,128},{192,160},{224,1... | collective-permute-start | bytes 884744 | tf_op jit(solution)/shard_map/ppermute | solution.py:221
  134.9 12.9 %collective-permute-start.14 = (bf16[384,384]{1,0:T(8,128)(2,1)S(1)}, bf16[384,384]{1,0:T(8,128)(2,1)S(1)}, u32[]{:S(2)}, u32[]{:S(2)}) collective-permute-start(bf16[384,384]{1,0:T(8,128)(2,1)S(1)} %collective-permute-done.9.refs_1_), channel_id=1, source_target_pairs={{0,32},{32,64},{64,96},{96,0},{128,160},{160,192},{192,224},{224,1... | collective-permute-start | bytes 884744 | tf_op jit(solution)/shard_map/ppermute | solution.py:221
  135.0 12.8 %collective-permute-start.15 = (bf16[384,384]{1,0:T(8,128)(2,1)S(1)}, bf16[384,384]{1,0:T(8,128)(2,1)S(1)}, u32[]{:S(2)}, u32[]{:S(2)}) collective-permute-start(bf16[384,384]{1,0:T(8,128)(2,1)S(1)} %collective-permute-done.9.refs_1_), channel_id=1, source_target_pairs={{0,96},{32,0},{64,32},{96,64},{128,224},{160,128},{192,160},{224,1... | collective-permute-start | bytes 884744 | tf_op jit(solution)/shard_map/ppermute | solution.py:221
  137.6 10.2 %collective-permute-start.16 = (bf16[384,384]{1,0:T(8,128)(2,1)S(1)}, bf16[384,384]{1,0:T(8,128)(2,1)S(1)}, u32[]{:S(2)}, u32[]{:S(2)}) collective-permute-start(bf16[384,384]{1,0:T(8,128)(2,1)S(1)} %collective-permute-done.10.refs_2_), channel_id=1, source_target_pairs={{0,144},{1,145},{2,146},{3,147},{4,148},{5,149},{6,150},{7,151},{8... | collective-permute-start | bytes 884744 | tf_op jit(solution)/shard_map/ppermute | solution.py:226
  157.9 1.8 %collective-permute-start.17 = (bf16[3,384,128]{2,1,0:T(8,128)(2,1)S(1)}, bf16[3,384,128]{2,1,0:T(8,128)(2,1)S(1)}, u32[]{:S(2)}, u32[]{:S(2)}) collective-permute-start(bf16[3,384,128]{2,1,0:T(8,128)(2,1)S(1)} %slice.128), channel_id=1, source_target_pairs={{0,1},{1,0},{2,3},{3,2},{4,5},{5,4},{6,7},{7,6},{8,9},{9,8},{10,11... | collective-permute-start | bytes 884744 | tf_op jit(solution)/shard_map/ppermute | solution.py:305
  (2 other events, 6.7 us)

commit v7 on v6

--- a/solution.py
+++ b/solution.py
@@ -20,6 +20,14 @@
     center = jnp.mean(values, axis=-1, keepdims=True)
     spread = jnp.mean((values - center) ** 2, axis=-1, keepdims=True)
     return ((values - center) * lax.rsqrt(spread + 1e-05) * gain).astype(jnp.bfloat16)
+
+
+def normalize_once(values, gain):
+    values = values.astype(jnp.float32)
+    moved = values - values[..., :1]
+    center = jnp.mean(moved, axis=-1, keepdims=True)
+    spread = jnp.maximum(jnp.mean(moved * moved, axis=-1, keepdims=True) - center * center, 0.0)
+    return ((moved - center) * lax.rsqrt(spread + 1e-05) * gain).astype(jnp.bfloat16)
 
 
 def whole(a):
@@ -248,7 +256,7 @@
         ncol = pair.shape[1]
         keys = nc * ncol
         half = keys // 2
-        normed = normalize(pair, norm_gain[0])
+        normed = normalize_once(pair, norm_gain[0])
         local = jnp.einsum("qmc,ch->mhq", normed, w_bias[0], preferred_element_type=jnp.float32)
         local = local.astype(jnp.bfloat16).reshape(ncol, HEADS, 2, 2, ncol).transpose(0, 3, 1, 2, 4)
         local = local.reshape(ncol, 2, -1)
@@ -289,11 +297,12 @@
         got = lax.all_to_all(
             message, ("row", "col"), 0, 0, tiled=True, axis_index_groups=same_core_all
         )
+        bias = got[:, nrow * part : nrow * part + brow].reshape(2, half, half // 2)
+        bias = jnp.concatenate([bias[0], bias[1]], axis=1)
+        got, bias = lax.optimization_barrier((got, bias))
+        first_biases = spread(bias)
         x_own = got[:, : nrow * part].reshape(keys, part, CH).transpose(1, 0, 2)
         x_other = lax.ppermute(x_own, "col", swap_core)
-        bias = got[:, nrow * part : nrow * part + brow].reshape(2, half, half // 2)
-        bias = jnp.concatenate([bias[0], bias[1]], axis=1)
-        first_biases = spread(bias)
         x = jnp.concatenate([x_own, x_other])
         xq = x.reshape(2 * part, ng, 2, ncol, CH)
         xq = jnp.where(core == 0, xq[:, :, 0], xq[:, :, 1]).reshape(2 * part, half, CH)

time: 175 us -> 175 us (level)
  other arithmetic: 5.07 us -> 2.6 us
  local copies, waits for them, and re-layouts: 5.09 us -> 7.53 us
    reduce_sum x2 -> x1, other arithmetic: 3.26 us -> 0.37 us  [normalize_once(): center = jnp.mean(moved, axis=-1, keepdims=True)]
    unnamed x14 -> x15, local copies, waits for them, and re-layouts: 0.03 us -> 1.84 us
where the time goes in v7:
time: 175 us
  blocking collectives  53.4 us (31%)
  Pallas kernels  42.8 us (24%)
  starting transfers between devices  34.7 us (20%)
  waiting for transfers between devices  31.9 us (18%)
  local copies, waits for them, and re-layouts  7.53 us (4%)
  other arithmetic  2.6 us (1%)
    all_to_all x1, blocking collectives, per_device(): lax.all_to_all(message, ('row', 'col'), 0, 0, tiled=True, axis_index_grou...  39.4 us
    pallas_call x4, Pallas kernels, attend(): pl.pallas_call(functools.partial(attention_kernel, nblk, len(done), stack...  35.7 us
    all_to_all x1, waiting for transfers between devices, all_to_all_16(): lax.all_to_all(message, 'col', 0, 0, tiled=True, axis_index_groups=same_c...  21.5 us
    all_to_all x1, blocking collectives, per_device(): got = lax.all_to_all(both.reshape(nr, -1, CH), 'row', 0, 0, tiled=True)  14.1 us
    ppermute x10, starting transfers between devices, along_y(): lax.ppermute(block, 'row', [(i, i // ny * ny + (i + dy) % ny) for i in ra...  13.7 us
    ppermute x10, waiting for transfers between devices, along_y(): lax.ppermute(block, 'row', [(i, i // ny * ny + (i + dy) % ny) for i in ra...  8.42 us
    all_to_all x1, starting transfers between devices, all_to_all_16(): lax.all_to_all(message, 'col', 0, 0, tiled=True, axis_index_groups=same_c...  7.61 us
    pallas_call x2, Pallas kernels, prepare(): pl.pallas_call(prepare_kernel, grid=(nrow,), in_specs=[by_row(x), by_row(...  7.13 us
  transfers between devices with their start and end apart: 19, of which 7 were waited for; matrix products, arithmetic and copies ran while one was open for 1% of the time, Pallas kernels for 12%

profile of v7, /device:TPU:1, one launch (start us, length us, event | category | flops | bytes accessed | tf_op | source)
XLA Modules:
  0.0 174.6 jit_solution(12675096989532464189)
XLA Ops:
  0.0 1.7 copy.31
  4.8 3.3 %collective-permute-start = (bf16[24,192]{1,0:T(8,128)(2,1)S(1)}, bf16[24,192]{1,0:T(8,128)(2,1)S(1)}, u32[]{:S(2)}, u32[]{:S(2)}) collective-permute-start(bf16[24,192]{1,0:T(8,128)(2,1)S(1)} %get-tuple-element.64), channel_id=1, source_target_pairs={{0,1},{1,0},{2,3},{3,2},{4,5},{5,4},{6,7},{7,6},{8,9},{9,8},{10,11... | collective-permute-start | bytes 27656 | tf_op jit(solution)/shard_map/ppermute | solution.py:265
  10.1 7.6 %all-to-all-start = ((bf16[16,216,128]{2,1,0:T(8,128)(2,1)}), bf16[16,216,128]{2,1,0:T(8,128)(2,1)S(1)}, u32[]{:S(2)}, u32[]{:S(2)}) async-start(bf16[16,216,128]{2,1,0:T(8,128)(2,1)} %pad_maximum_fusion.2), calls=%async_computation | async-start | bytes 1769472 | tf_op jit(solution)/shard_map/all_to_all | solution.py:249
  17.7 21.5 %all-to-all-done = bf16[16,216,128]{2,1,0:T(8,128)(2,1)S(1)} async-done(((bf16[16,216,128]{2,1,0:T(8,128)(2,1)}), bf16[16,216,128]{2,1,0:T(8,128)(2,1)S(1)}, u32[]{:S(2)}, u32[]{:S(2)}) %all-to-all-start) | async-done | bytes 884768 | tf_op jit(solution)/shard_map/all_to_all | solution.py:249
  39.2 3.3 %collective-permute-start.3 = (bf16[16,144,128]{2,1,0:T(8,128)(2,1)S(1)}, bf16[16,144,128]{2,1,0:T(8,128)(2,1)S(1)}, u32[]{:S(2)}, u32[]{:S(2)}) collective-permute-start(bf16[16,144,128]{2,1,0:T(8,128)(2,1)S(1)} %slice.125), channel_id=1, source_target_pairs={{0,1},{1,0},{2,3},{3,2},{4,5},{5,4},{6,7},{7,6},{8,9},{9,8},{10,11... | collective-permute-start | bytes 1769480 | tf_op jit(solution)/shard_map/ppermute | solution.py:272
  43.0 1.7 collective-permute-start.1
  44.7 2.9 %collective-permute-start.2 = (bf16[384,384]{1,0:T(8,128)(2,1)S(1)}, bf16[384,384]{1,0:T(8,128)(2,1)S(1)}, u32[]{:S(2)}, u32[]{:S(2)}) collective-permute-start(bf16[384,384]{1,0:T(8,128)(2,1)S(1)} %reshape.93.refs_0_), channel_id=1, source_target_pairs={{0,64},{32,96},{64,0},{96,32},{128,192},{160,224},{192,128},{224,1... | collective-permute-start | bytes 884744 | tf_op jit(solution)/shard_map/ppermute | solution.py:229
  48.0 2.3 %collective-permute-start.5 = (bf16[384,384]{1,0:T(8,128)(2,1)S(1)}, bf16[384,384]{1,0:T(8,128)(2,1)S(1)}, u32[]{:S(2)}, u32[]{:S(2)}) collective-permute-start(bf16[384,384]{1,0:T(8,128)(2,1)S(1)} %reshape.93.refs_0_), channel_id=1, source_target_pairs={{0,96},{32,0},{64,32},{96,64},{128,224},{160,128},{192,160},{224,1... | collective-permute-start | bytes 884744 | tf_op jit(solution)/shard_map/ppermute | solution.py:229
  50.7 3.6 %prepare.2 = (bf16[6,128,768]{2,1,0:T(8,128)(2,1)S(1)}, bf16[6,768,128]{2,1,0:T(8,128)(2,1)S(1)}, bf16[6,384,128]{2,1,0:T(8,128)(2,1)S(1)}, f32[6,384,128]{2,1,0:T(8,128)S(1)}) custom-call(bf16[6,768,128]{2,1,0:T(8,128)(2,1)S(1)} %bitcast.75, bf16[6,384,128]{2,1,0:T(8,128)(2,1)S(1)} %slice.126.xq_ref, f32[1,128]{1,0:T(1,128)S(1)} %get-tuple-element.74.gain_ref, ...), custom_call_target="tpu_custom_call" | custom-call | flops 4000000000 | bytes 6291456 | tf_op jit(solution)/shard_map/prepare/pallas_call | solution.py:73
  54.5 1.3 collective-permute-start.6
  55.8 1.4 collective-permute-start.7
  58.3 6.8 %attend.4.refs_7_ = bf16[3,6,48,128]{3,2,1,0:T(8,128)(2,1)S(1)} custom-call(s32[3]{0:T(128)S(1)} %pad_add_fusion.blk_ref.done_blk_ref, s32[1]{0:T(128)} %bitcast.5.done_blk_ref, bf16[6,128,768]{2,1,0:T(8,128)(2,1)S(1)} %get-tuple-element.33.kt_ref, bf16[6,768,128]{2,1,0:T(8,128)(2,1)S(1)} %get-tuple-element.34.v_ref, ...), custom_call_target="tpu_custom_call" | custom-call | flops 8400000000 | bytes 6291456 | tf_op jit(solution)/shard_map/attend/pallas_call | solution.py:175
  65.1 2.6 %collective-permute-done.6.refs_2_ = bf16[384,384]{1,0:T(8,128)(2,1)S(1)} collective-permute-done((bf16[384,384]{1,0:T(8,128)(2,1)S(1)}, bf16[384,384]{1,0:T(8,128)(2,1)S(1)}, u32[]{:S(2)}, u32[]{:S(2)}) %collective-permute-start.6) | collective-permute-done | bytes 294944 | tf_op jit(solution)/shard_map/ppermute | solution.py:229
  67.8 11.9 %attend.5 = (bf16[6,384,128]{2,1,0:T(8,128)(2,1)S(1)}, bf16[6,16,384]{2,1,0:T(8,128)(2,1)S(1)}) custom-call(s32[5]{0:T(128)S(1)} %stack.61.blk_ref, s32[3]{0:T(128)S(1)} %pad_add_fusion.blk_ref.done_blk_ref, bf16[6,128,768]{2,1,0:T(8,128)(2,1)S(1)} %get-tuple-element.33.kt_ref, bf16[6,768,128]{2,1,0:T(8,128)(2,1)S(1)} %get-tuple-element.34.v_ref, ...), custom_call_target="tpu_custom_call" | custom-call | flops 14000000000 | bytes 6291456 | tf_op jit(solution)/shard_map/attend/pallas_call | solution.py:175
  81.4 39.4 %all_to_all.15 = bf16[128,32,128]{2,1,0:T(8,128)(2,1)S(1)} all-to-all(bf16[128,32,128]{2,1,0:T(8,128)(2,1)S(1)} %copy.39), channel_id=1, replica_groups={{0,2,4,6,8,10,12,14,16,18,20,22,24,26,28,30,32,34,36,38,40,42,44,46,48,..., dimensions={0} | all-to-all | bytes 2097152 | tf_op jit(solution)/shard_map/all_to_all | solution.py:297
  122.2 2.1 %collective-permute-start.11 = (bf16[3,768,128]{2,1,0:T(8,128)(2,1)S(1)}, bf16[3,768,128]{2,1,0:T(8,128)(2,1)S(1)}, u32[]{:S(2)}, u32[]{:S(2)}) collective-permute-start(bf16[3,768,128]{2,1,0:T(8,128)(2,1)S(1)} %bitcast.85), channel_id=1, source_target_pairs={{0,1},{1,0},{2,3},{3,2},{4,5},{5,4},{6,7},{7,6},{8,9},{9,8},{10,11... | collective-permute-start | bytes 1769480 | tf_op jit(solution)/shard_map/ppermute | solution.py:305
  125.7 2.3 %collective-permute-start.13 = (bf16[384,384]{1,0:T(8,128)(2,1)S(1)}, bf16[384,384]{1,0:T(8,128)(2,1)S(1)}, u32[]{:S(2)}, u32[]{:S(2)}) collective-permute-start(bf16[384,384]{1,0:T(8,128)(2,1)S(1)} %pad_maximum_fusion.4.refs_0_), channel_id=1, source_target_pairs={{0,96},{32,0},{64,32},{96,64},{128,224},{160,128},{192,160},{224,1... | collective-permute-start | bytes 884744 | tf_op jit(solution)/shard_map/ppermute | solution.py:229
  128.2 3.6 %prepare.3 = (bf16[6,128,768]{2,1,0:T(8,128)(2,1)S(1)}, bf16[6,768,128]{2,1,0:T(8,128)(2,1)S(1)}, bf16[6,384,128]{2,1,0:T(8,128)(2,1)S(1)}, f32[6,384,128]{2,1,0:T(8,128)S(1)}) custom-call(bf16[6,768,128]{2,1,0:T(8,128)(2,1)S(1)} %pad_maximum_fusion.1.x_ref, bf16[6,384,128]{2,1,0:T(8,128)(2,1)S(1)} %bitcast.76, ...), custom_call_target="tpu_custom_call" | custom-call | flops 4000000000 | bytes 6291456 | tf_op jit(solution)/shard_map/prepare/pallas_call | solution.py:73
  131.7 2.7 %collective-permute-done.10.refs_2_ = bf16[384,384]{1,0:T(8,128)(2,1)S(1)} collective-permute-done((bf16[384,384]{1,0:T(8,128)(2,1)S(1)}, bf16[384,384]{1,0:T(8,128)(2,1)S(1)}, u32[]{:S(2)}, u32[]{:S(2)}) %collective-permute-start.10) | collective-permute-done | bytes 294944 | tf_op jit(solution)/shard_map/ppermute | solution.py:229
  134.5 2.6 %collective-permute-start.15 = (bf16[384,384]{1,0:T(8,128)(2,1)S(1)}, bf16[384,384]{1,0:T(8,128)(2,1)S(1)}, u32[]{:S(2)}, u32[]{:S(2)}) collective-permute-start(bf16[384,384]{1,0:T(8,128)(2,1)S(1)} %collective-permute-done.9.refs_1_), channel_id=1, source_target_pairs={{0,96},{32,0},{64,32},{96,64},{128,224},{160,128},{192,160},{224,1... | collective-permute-start | bytes 884744 | tf_op jit(solution)/shard_map/ppermute | solution.py:229
  137.4 7.0 %attend.6.refs_7_ = bf16[3,6,48,128]{3,2,1,0:T(8,128)(2,1)S(1)} custom-call(s32[3]{0:T(128)S(1)} %pad_add_fusion.blk_ref.done_blk_ref, s32[1]{0:T(128)} %bitcast.5.done_blk_ref, bf16[6,128,768]{2,1,0:T(8,128)(2,1)S(1)} %get-tuple-element.47.kt_ref, bf16[6,768,128]{2,1,0:T(8,128)(2,1)S(1)} %get-tuple-element.48.v_ref, ...), custom_call_target="tpu_custom_call" | custom-call | flops 8400000000 | bytes 6291456 | tf_op jit(solution)/shard_map/attend/pallas_call | solution.py:175
  144.5 2.9 %collective-permute-done.14.refs_2_ = bf16[384,384]{1,0:T(8,128)(2,1)S(1)} collective-permute-done((bf16[384,384]{1,0:T(8,128)(2,1)S(1)}, bf16[384,384]{1,0:T(8,128)(2,1)S(1)}, u32[]{:S(2)}, u32[]{:S(2)}) %collective-permute-start.14) | collective-permute-done | bytes 294944 | tf_op jit(solution)/shard_map/ppermute | solution.py:229
  147.4 10.0 %attend.7 = bf16[6,384,128]{2,1,0:T(8,128)(2,1)S(1)} custom-call(s32[5]{0:T(128)S(1)} %stack.61.blk_ref, s32[3]{0:T(128)S(1)} %pad_add_fusion.blk_ref.done_blk_ref, bf16[6,128,768]{2,1,0:T(8,128)(2,1)S(1)} %get-tuple-element.47.kt_ref, bf16[6,768,128]{2,1,0:T(8,128)(2,1)S(1)} %get-tuple-element.48.v_ref, bf16[6,384,128]{2,1,0:T(8,128)(2,1)S(1)} %get-tuple-element.49.q_ref, ...), custom_call_target="tpu_custom_call" | custom-call | flops 14000000000 | bytes 6291456 | tf_op jit(solution)/shard_map/attend/pallas_call | solution.py:175
  159.4 14.1 %all_to_all.16 = bf16[8,288,128]{2,1,0:T(8,128)(2,1)S(1)} all-to-all(bf16[8,288,128]{2,1,0:T(8,128)(2,1)S(1)} %bitcast.81), channel_id=1, replica_groups=mesh['row'=8,'col'=32] {'row'}, dimensions={0} | all-to-all | bytes 1179648 | tf_op jit(solution)/shard_map/all_to_all | solution.py:317
  (92 shorter events, 15.7 us)
Async XLA Ops:
  2.2 1.2 copy-start.3
  2.7 6.4 %copy-start = (bf16[96,24,128]{2,1,0:T(8,128)(2,1)S(1)}, bf16[96,24,128]{2,1,0:T(8,128)(2,1)}, u32[]{:S(2)}) copy-start(bf16[96,24,128]{2,1,0:T(8,128)(2,1)} %param.7) | copy-start | bytes 1769476
  4.8 4.2 %collective-permute-start = (bf16[24,192]{1,0:T(8,128)(2,1)S(1)}, bf16[24,192]{1,0:T(8,128)(2,1)S(1)}, u32[]{:S(2)}, u32[]{:S(2)}) collective-permute-start(bf16[24,192]{1,0:T(8,128)(2,1)S(1)} %get-tuple-element.64), channel_id=1, source_target_pairs={{0,1},{1,0},{2,3},{3,2},{4,5},{5,4},{6,7},{7,6},{8,9},{9,8},{10,11... | collective-permute-start | bytes 27656 | tf_op jit(solution)/shard_map/ppermute | solution.py:265
  10.1 32.4 %copy-start.4 = (f32[2,128]{1,0:T(2,128)S(1)}, f32[2,128]{1,0:T(2,128)}, u32[]{:S(2)}) copy-start(f32[2,128]{1,0:T(2,128)} %param.13) | copy-start | bytes 3076
  10.1 32.7 %copy-start.2 = (bf16[2,128,128]{2,1,0:T(8,128)(2,1)S(1)}, bf16[2,128,128]{2,1,0:T(8,128)(2,1)}, u32[]{:S(2)}) copy-start(bf16[2,128,128]{2,1,0:T(8,128)(2,1)} %param.12) | copy-start | bytes 196612
  10.1 32.7 %copy-start.1 = (bf16[2,128,512]{2,1,0:T(8,128)(2,1)S(1)}, bf16[2,128,512]{2,1,0:T(8,128)(2,1)}, u32[]{:S(2)}) copy-start(bf16[2,128,512]{2,1,0:T(8,128)(2,1)} %param.9) | copy-start | bytes 786436
  10.1 29.1 %all-to-all-start = ((bf16[16,216,128]{2,1,0:T(8,128)(2,1)}), bf16[16,216,128]{2,1,0:T(8,128)(2,1)S(1)}, u32[]{:S(2)}, u32[]{:S(2)}) async-start(bf16[16,216,128]{2,1,0:T(8,128)(2,1)} %pad_maximum_fusion.2), calls=%async_computation | async-start | bytes 1769472 | tf_op jit(solution)/shard_map/all_to_all | solution.py:249
  39.2 11.1 %collective-permute-start.3 = (bf16[16,144,128]{2,1,0:T(8,128)(2,1)S(1)}, bf16[16,144,128]{2,1,0:T(8,128)(2,1)S(1)}, u32[]{:S(2)}, u32[]{:S(2)}) collective-permute-start(bf16[16,144,128]{2,1,0:T(8,128)(2,1)S(1)} %slice.125), channel_id=1, source_target_pairs={{0,1},{1,0},{2,3},{3,2},{4,5},{5,4},{6,7},{7,6},{8,9},{9,8},{10,11... | collective-permute-start | bytes 1769480 | tf_op jit(solution)/shard_map/ppermute | solution.py:272
  43.0 11.3 %collective-permute-start.1 = (bf16[384,384]{1,0:T(8,128)(2,1)S(1)}, bf16[384,384]{1,0:T(8,128)(2,1)S(1)}, u32[]{:S(2)}, u32[]{:S(2)}) collective-permute-start(bf16[384,384]{1,0:T(8,128)(2,1)S(1)} %reshape.93.refs_0_), channel_id=1, source_target_pairs={{0,144},{1,145},{2,146},{3,147},{4,148},{5,149},{6,150},{7,151},{8... | collective-permute-start | bytes 884744 | tf_op jit(solution)/shard_map/ppermute | solution.py:234
  44.7 9.8 %collective-permute-start.2 = (bf16[384,384]{1,0:T(8,128)(2,1)S(1)}, bf16[384,384]{1,0:T(8,128)(2,1)S(1)}, u32[]{:S(2)}, u32[]{:S(2)}) collective-permute-start(bf16[384,384]{1,0:T(8,128)(2,1)S(1)} %reshape.93.refs_0_), channel_id=1, source_target_pairs={{0,64},{32,96},{64,0},{96,32},{128,192},{160,224},{192,128},{224,1... | collective-permute-start | bytes 884744 | tf_op jit(solution)/shard_map/ppermute | solution.py:229
  47.6 17.5 %collective-permute-start.4 = (bf16[384,384]{1,0:T(8,128)(2,1)S(1)}, bf16[384,384]{1,0:T(8,128)(2,1)S(1)}, u32[]{:S(2)}, u32[]{:S(2)}) collective-permute-start(bf16[384,384]{1,0:T(8,128)(2,1)S(1)} %reshape.93.refs_0_), channel_id=1, source_target_pairs={{0,32},{32,64},{64,96},{96,0},{128,160},{160,192},{192,224},{224,1... | collective-permute-start | bytes 884744 | tf_op jit(solution)/shard_map/ppermute | solution.py:229
  48.0 17.1 %collective-permute-start.5 = (bf16[384,384]{1,0:T(8,128)(2,1)S(1)}, bf16[384,384]{1,0:T(8,128)(2,1)S(1)}, u32[]{:S(2)}, u32[]{:S(2)}) collective-permute-start(bf16[384,384]{1,0:T(8,128)(2,1)S(1)} %reshape.93.refs_0_), channel_id=1, source_target_pairs={{0,96},{32,0},{64,32},{96,64},{128,224},{160,128},{192,160},{224,1... | collective-permute-start | bytes 884744 | tf_op jit(solution)/shard_map/ppermute | solution.py:229
  54.5 13.3 %collective-permute-start.6 = (bf16[384,384]{1,0:T(8,128)(2,1)S(1)}, bf16[384,384]{1,0:T(8,128)(2,1)S(1)}, u32[]{:S(2)}, u32[]{:S(2)}) collective-permute-start(bf16[384,384]{1,0:T(8,128)(2,1)S(1)} %collective-permute-done.1.refs_1_), channel_id=1, source_target_pairs={{0,32},{32,64},{64,96},{96,0},{128,160},{160,192},{192,224},{224,1... | collective-permute-start | bytes 884744 | tf_op jit(solution)/shard_map/ppermute | solution.py:229
  55.8 12.0 %collective-permute-start.7 = (bf16[384,384]{1,0:T(8,128)(2,1)S(1)}, bf16[384,384]{1,0:T(8,128)(2,1)S(1)}, u32[]{:S(2)}, u32[]{:S(2)}) collective-permute-start(bf16[384,384]{1,0:T(8,128)(2,1)S(1)} %collective-permute-done.1.refs_1_), channel_id=1, source_target_pairs={{0,96},{32,0},{64,32},{96,64},{128,224},{160,128},{192,160},{224,1... | collective-permute-start | bytes 884744 | tf_op jit(solution)/shard_map/ppermute | solution.py:229
  57.2 10.6 %collective-permute-start.8 = (bf16[384,384]{1,0:T(8,128)(2,1)S(1)}, bf16[384,384]{1,0:T(8,128)(2,1)S(1)}, u32[]{:S(2)}, u32[]{:S(2)}) collective-permute-start(bf16[384,384]{1,0:T(8,128)(2,1)S(1)} %collective-permute-done.2.refs_2_), channel_id=1, source_target_pairs={{0,144},{1,145},{2,146},{3,147},{4,148},{5,149},{6,150},{7,151},{8... | collective-permute-start | bytes 884744 | tf_op jit(solution)/shard_map/ppermute | solution.py:234
  122.2 5.8 %collective-permute-start.11 = (bf16[3,768,128]{2,1,0:T(8,128)(2,1)S(1)}, bf16[3,768,128]{2,1,0:T(8,128)(2,1)S(1)}, u32[]{:S(2)}, u32[]{:S(2)}) collective-permute-start(bf16[3,768,128]{2,1,0:T(8,128)(2,1)S(1)} %bitcast.85), channel_id=1, source_target_pairs={{0,1},{1,0},{2,3},{3,2},{4,5},{5,4},{6,7},{7,6},{8,9},{9,8},{10,11... | collective-permute-start | bytes 1769480 | tf_op jit(solution)/shard_map/ppermute | solution.py:305
  124.3 10.1 %collective-permute-start.10 = (bf16[384,384]{1,0:T(8,128)(2,1)S(1)}, bf16[384,384]{1,0:T(8,128)(2,1)S(1)}, u32[]{:S(2)}, u32[]{:S(2)}) collective-permute-start(bf16[384,384]{1,0:T(8,128)(2,1)S(1)} %pad_maximum_fusion.4.refs_0_), channel_id=1, source_target_pairs={{0,64},{32,96},{64,0},{96,32},{128,192},{160,224},{192,128},{224,1... | collective-permute-start | bytes 884744 | tf_op jit(solution)/shard_map/ppermute | solution.py:229
  124.3 10.1 %collective-permute-start.9 = (bf16[384,384]{1,0:T(8,128)(2,1)S(1)}, bf16[384,384]{1,0:T(8,128)(2,1)S(1)}, u32[]{:S(2)}, u32[]{:S(2)}) collective-permute-start(bf16[384,384]{1,0:T(8,128)(2,1)S(1)} %pad_maximum_fusion.4.refs_0_), channel_id=1, source_target_pairs={{0,144},{1,145},{2,146},{3,147},{4,148},{5,149},{6,150},{7,151},{8... | collective-permute-start | bytes 884744 | tf_op jit(solution)/shard_map/ppermute | solution.py:234
  125.3 19.1 %collective-permute-start.12 = (bf16[384,384]{1,0:T(8,128)(2,1)S(1)}, bf16[384,384]{1,0:T(8,128)(2,1)S(1)}, u32[]{:S(2)}, u32[]{:S(2)}) collective-permute-start(bf16[384,384]{1,0:T(8,128)(2,1)S(1)} %pad_maximum_fusion.4.refs_0_), channel_id=1, source_target_pairs={{0,32},{32,64},{64,96},{96,0},{128,160},{160,192},{192,224},{224,1... | collective-permute-start | bytes 884744 | tf_op jit(solution)/shard_map/ppermute | solution.py:229
  125.7 18.8 %collective-permute-start.13 = (bf16[384,384]{1,0:T(8,128)(2,1)S(1)}, bf16[384,384]{1,0:T(8,128)(2,1)S(1)}, u32[]{:S(2)}, u32[]{:S(2)}) collective-permute-start(bf16[384,384]{1,0:T(8,128)(2,1)S(1)} %pad_maximum_fusion.4.refs_0_), channel_id=1, source_target_pairs={{0,96},{32,0},{64,32},{96,64},{128,224},{160,128},{192,160},{224,1... | collective-permute-start | bytes 884744 | tf_op jit(solution)/shard_map/ppermute | solution.py:229
  134.4 13.0 %collective-permute-start.14 = (bf16[384,384]{1,0:T(8,128)(2,1)S(1)}, bf16[384,384]{1,0:T(8,128)(2,1)S(1)}, u32[]{:S(2)}, u32[]{:S(2)}) collective-permute-start(bf16[384,384]{1,0:T(8,128)(2,1)S(1)} %collective-permute-done.9.refs_1_), channel_id=1, source_target_pairs={{0,32},{32,64},{64,96},{96,0},{128,160},{160,192},{192,224},{224,1... | collective-permute-start | bytes 884744 | tf_op jit(solution)/shard_map/ppermute | solution.py:229
  134.5 12.9 %collective-permute-start.15 = (bf16[384,384]{1,0:T(8,128)(2,1)S(1)}, bf16[384,384]{1,0:T(8,128)(2,1)S(1)}, u32[]{:S(2)}, u32[]{:S(2)}) collective-permute-start(bf16[384,384]{1,0:T(8,128)(2,1)S(1)} %collective-permute-done.9.refs_1_), channel_id=1, source_target_pairs={{0,96},{32,0},{64,32},{96,64},{128,224},{160,128},{192,160},{224,1... | collective-permute-start | bytes 884744 | tf_op jit(solution)/shard_map/ppermute | solution.py:229
  137.1 10.3 %collective-permute-start.16 = (bf16[384,384]{1,0:T(8,128)(2,1)S(1)}, bf16[384,384]{1,0:T(8,128)(2,1)S(1)}, u32[]{:S(2)}, u32[]{:S(2)}) collective-permute-start(bf16[384,384]{1,0:T(8,128)(2,1)S(1)} %collective-permute-done.10.refs_2_), channel_id=1, source_target_pairs={{0,144},{1,145},{2,146},{3,147},{4,148},{5,149},{6,150},{7,151},{8... | collective-permute-start | bytes 884744 | tf_op jit(solution)/shard_map/ppermute | solution.py:234
  157.5 1.8 %collective-permute-start.17 = (bf16[3,384,128]{2,1,0:T(8,128)(2,1)S(1)}, bf16[3,384,128]{2,1,0:T(8,128)(2,1)S(1)}, u32[]{:S(2)}, u32[]{:S(2)}) collective-permute-start(bf16[3,384,128]{2,1,0:T(8,128)(2,1)S(1)} %slice.132), channel_id=1, source_target_pairs={{0,1},{1,0},{2,3},{3,2},{4,5},{5,4},{6,7},{7,6},{8,9},{9,8},{10,11... | collective-permute-start | bytes 884744 | tf_op jit(solution)/shard_map/ppermute | solution.py:314
  (2 other events, 1.4 us)
